TPU v7x, 32 devices: a whole 2x2x4 slice. The times are simulated.
32 devices in a mesh: img: 4 (over x, core), txt: 8 (over z, y).
Axes of the slice: x: 2, y: 2, z: 4, core: 2. Of those that a mesh axis runs over, the one named last changes fastest.
Arguments:
- images: bfloat16 [1536, 1152], P(('img', 'txt')), may hold values from -36 to 36
- texts: bfloat16 [1536, 640], P(('txt', 'img')), may hold values from -36 to 36
- head_weight: bfloat16 [1152, 640], replicated, may hold values from -0.088388348 to 0.088388348
- log_scale: float32 [1], replicated, may hold values from 1.5 to 2.5
- logit_bias: float32 [1], replicated, may hold values from -4 to -1
Outputs:
- image_grads: bfloat16 [1536, 1152], P(('img', 'txt'))
- text_grads: bfloat16 [1536, 640], P(('txt', 'img'))
- head_grad: float32 [1152, 640], replicated
All inputs are finite; a program needn't handle non-finite values.
Results may differ from a plain program's by a relative error of at most 0.02.
Values may be sent and summed in bfloat16 or wider, within the bound.
No kernel may reach another device: no remote copies, remote signals or barrier semaphores. Data moves between devices by JAX's collectives and lax.ppermute only.
A program may use at most 64 MiB of HBM per device.

v0:
```python
import jax
import jax.numpy as jnp
from jax import lax
from jax.sharding import PartitionSpec as P

eps = 1e-06


def shards(images, texts, head_weight, log_scale, logit_bias):
    scale = jnp.exp(log_scale[0])
    bias = logit_bias[0]
    hidden = jnp.dot(images, head_weight, preferred_element_type=jnp.float32)
    img_inv = lax.rsqrt(jnp.sum(hidden * hidden, axis=1, keepdims=True) + eps)
    img_unit = (hidden * img_inv).astype(jnp.bfloat16)
    txt_full = texts.astype(jnp.float32)
    txt_inv = lax.rsqrt(jnp.sum(txt_full * txt_full, axis=1, keepdims=True) + eps)
    txt_unit = (txt_full * txt_inv).astype(jnp.bfloat16)
    img_block = lax.all_gather(img_unit, "txt", axis=0, tiled=True)
    txt_block = lax.all_gather(txt_unit, "img", axis=0, tiled=True)
    total_rows = img_block.shape[0]
    total_cols = txt_block.shape[0]
    features = img_block.shape[1]
    row_first = lax.axis_index("img") * total_rows
    col_first = lax.axis_index("txt") * total_cols
    columns = col_first + jnp.arange(total_cols, dtype=jnp.int32)
    width = 512 if total_rows % 512 == 0 else total_rows
    count = total_rows // width
    blocks = img_block.reshape(count, width, features)

    def step(carry, inputs):
        block, index = inputs
        logits = scale * jnp.dot(block, txt_block.T, preferred_element_type=jnp.float32) + bias
        row_ids = row_first + index * width + jnp.arange(width, dtype=jnp.int32)
        label = jnp.where(row_ids[:, None] == columns[None, :], 1.0, -1.0).astype(jnp.float32)
        grad = (-label * jax.nn.sigmoid(-label * logits)).astype(jnp.bfloat16)
        d_rows = scale * jnp.dot(grad, txt_block, preferred_element_type=jnp.float32)
        carry = carry + scale * lax.dot_general(
            grad, block, (((0,), (0,)), ((), ())), preferred_element_type=jnp.float32
        )
        return (carry, d_rows)

    txt_terms, row_terms = lax.scan(
        step,
        jnp.zeros((total_cols, features), jnp.float32),
        (blocks, jnp.arange(count, dtype=jnp.int32)),
    )
    img_terms = row_terms.reshape(total_rows, features)
    d_img = lax.psum_scatter(
        img_terms.astype(jnp.bfloat16), "txt", scatter_dimension=0, tiled=True
    ).astype(jnp.float32)
    inner = jnp.sum(hidden * d_img, axis=1, keepdims=True)
    d_hidden = (img_inv * (d_img - hidden * img_inv * img_inv * inner)).astype(jnp.bfloat16)
    image_grads = jnp.dot(d_hidden, head_weight.T, preferred_element_type=jnp.float32).astype(
        jnp.bfloat16
    )
    head_term = lax.dot_general(
        images, d_hidden, (((0,), (0,)), ((), ())), preferred_element_type=jnp.float32
    )
    head_grad = lax.psum(head_term, ("img", "txt"))
    image_grads, head_grad = (image_grads, head_grad)
    d_txt = lax.psum_scatter(
        txt_terms.astype(jnp.bfloat16), "img", scatter_dimension=0, tiled=True
    ).astype(jnp.float32)
    inner_txt = jnp.sum(txt_full * d_txt, axis=1, keepdims=True)
    text_grads = (txt_inv * (d_txt - txt_full * txt_inv * txt_inv * inner_txt)).astype(jnp.bfloat16)
    return (image_grads, text_grads, head_grad)


def solution(mesh):
    return jax.shard_map(
        shards,
        mesh=mesh,
        in_specs=(P(("img", "txt"), None), P(("txt", "img"), None), P(), P(), P()),
        out_specs=(P(("img", "txt"), None), P(("txt", "img"), None), P()),
        check_vma=False,
    )
```

profile of v0, /device:TPU:0, one launch (start us, length us, event | category | flops | bytes accessed | tf_op | source)
XLA Modules:
  0.0 289.3 jit_solution(2210695961409550593)
XLA Ops:
  7.2 0.0 copy-start
  7.2 0.0 reduce-scatter.3.cloned.1.call-start
  8.7 0.9 fusion.18
  9.7 0.9 fusion.11
  10.6 0.0 copy-done
  10.6 1.4 multiply_reduce_fusion
  12.0 7.1 %all_gather.7 = bf16[192,640]{1,0:T(8,128)(2,1)S(1)} all-gather(bf16[48,640]{1,0:T(8,128)(2,1)S(1)} %fusion.11), channel_id=1, replica_groups=mesh['img'=4,'txt'=8] {'img'}, dimensions={0}, use_global_device_ids=true | all-gather | bytes 307200 | tf_op jit(solution)/shard_map/all_gather | solution.py:19
  19.1 0.1 multiply_convert_fusion
  19.2 31.9 %all_gather.6 = bf16[384,640]{1,0:T(8,128)(2,1)S(1)} all-gather(bf16[48,640]{1,0:T(8,128)(2,1)S(1)} %multiply_convert_fusion), channel_id=1, replica_groups=mesh['img'=4,'txt'=8] {'txt'}, dimensions={0}, use_global_device_ids=true | all-gather | bytes 552960 | tf_op jit(solution)/shard_map/all_gather | solution.py:18
  51.1 0.4 fusion.9
  51.5 0.0 copy-start.3
  51.5 1.2 fusion
  52.7 0.0 reduce-scatter.3.cloned.1.call-update
  52.7 0.0 reduce-scatter.5.cloned.1.call-start
  52.7 1.0 fusion.1
  53.7 0.0 reduce-scatter.5.cloned.1.call-update
  53.8 0.0 all-reduce.2.cloned.1.call-start
  53.8 59.1 %reduce-scatter.3.cloned.1.call-done = bf16[48,640]{1,0:T(8,128)(2,1)} async-done(((bf16[384,640]{1,0:T(8,128)(2,1)}), bf16[48,640]{1,0:T(8,128)(2,1)}) %reduce-scatter.3.cloned.1.call-update) | async-done | bytes 61456 | tf_op jit(solution)/shard_map/reduce_scatter | solution.py:48
  112.9 0.9 fusion.13
  113.8 0.0 copy-done.3
  113.8 3.1 %convolution_bitcast_fusion = f32[1152,640]{0,1:T(8,128)} fusion(bf16[48,1152]{1,0:T(8,128)(2,1)S(1)} %copy-done.3, bf16[48,640]{1,0:T(8,128)(2,1)} %reduce-scatter.3.cloned.1.call-done, f32[48,640]{1,0:T(8,128)S(1)} %get-tuple-element.25, f32[48]{0:T(128)S(1)} %fusion.13, f32[48]{0:T(128)S(1)} %add_rsqrt_fusion.1), kind=kOutput, calls=%fused_computation | convolution fusion | flops 70993920 | bytes 3244416 | tf_op jit(solution)/shard_map/dot_general | solution.py:56
  116.9 0.0 copy-start.1
  116.9 0.0 copy-start.2
  116.9 0.0 all-reduce.2.cloned.1.call-update
  117.0 17.3 %reduce-scatter.5.cloned.1.call-done = bf16[48,640]{1,0:T(8,128)(2,1)} async-done(((bf16[192,640]{1,0:T(8,128)(2,1)}), bf16[48,640]{1,0:T(8,128)(2,1)}) %reduce-scatter.5.cloned.1.call-update) | async-done | bytes 61456 | tf_op jit(solution)/shard_map/reduce_scatter | solution.py:61
  134.3 0.0 copy-done.1
  134.3 1.0 fusion.19
  135.3 1.6 fusion.17
  136.8 0.0 copy-done.2
  136.8 1.2 convolution_convert_fusion
  138.0 140.0 %all-reduce.2.cloned.1.call-done = f32[1152,640]{0,1:T(8,128)} async-done(((f32[1152,640]{0,1:T(8,128)}), f32[1152,640]{0,1:T(8,128)}) %all-reduce.2.cloned.1.call-update) | async-done | bytes 2949136 | tf_op jit(solution)/shard_map/psum | solution.py:59
  278.1 4.7 %copy.8 = f32[1152,640]{1,0:T(8,128)} copy(f32[1152,640]{0,1:T(8,128)} %all-reduce.2.cloned.1.call-done) | data formatting | bytes 5898240
  (4 shorter events, 0.0 us)
Async XLA Ops:
  7.2 3.4 %copy-start = (bf16[1152,640]{1,0:T(8,128)(2,1)S(1)}, bf16[1152,640]{1,0:T(8,128)(2,1)}, u32[]{:S(2)}) copy-start(bf16[1152,640]{1,0:T(8,128)(2,1)} %param.7) | copy-start | bytes 4423684
  7.2 105.7 %reduce-scatter.3.cloned.1.call-start = ((), (), s32[]{:S(2)}) async-start(), calls=%async_computation.2 | async-start | bytes 552960 | tf_op jit(solution)/shard_map/reduce_scatter | solution.py:48
  51.5 62.3 %copy-start.3 = (bf16[48,1152]{1,0:T(8,128)(2,1)S(1)}, bf16[48,1152]{1,0:T(8,128)(2,1)}, u32[]{:S(2)}) copy-start(bf16[48,1152]{1,0:T(8,128)(2,1)} %param.5) | copy-start | bytes 331780
  52.7 81.6 %reduce-scatter.5.cloned.1.call-start = ((), (), s32[]{:S(2)}) async-start(), calls=%async_computation.3 | async-start | bytes 307200 | tf_op jit(solution)/shard_map/reduce_scatter | solution.py:61
  53.8 224.3 %all-reduce.2.cloned.1.call-start = ((), (), s32[]{:S(2)}) async-start(), calls=%async_computation.4 | async-start | bytes 5898240 | tf_op jit(solution)/shard_map/psum | solution.py:59
  116.9 17.4 %copy-start.1 = (bf16[48,640]{1,0:T(8,128)(2,1)S(1)}, bf16[48,640]{1,0:T(8,128)(2,1)}, u32[]{:S(2)}) copy-start(bf16[48,640]{1,0:T(8,128)(2,1)} %param.6) | copy-start | bytes 184324
  116.9 19.9 %copy-start.2 = (bf16[48,640]{1,0:T(8,128)(2,1)S(1)}, bf16[48,640]{1,0:T(8,128)(2,1)}, u32[]{:S(2)}) copy-start(bf16[48,640]{1,0:T(8,128)(2,1)} %reduce-scatter.3.cloned.1.call-done) | copy-start | bytes 184324
Sparse Core Ops, SparseCore 0:
  52.8 60.0 reduce-scatter.2
  115.3 18.9 reduce-scatter.4
  141.3 136.7 all-reduce.1
where the time goes:
time: 290 us; the launch traced here: 289 us
  waiting for transfers between devices  216 us (74%)
  blocking collectives  39 us (13%)
  between operations  15.3 us (5%)
  matrix products  8.24 us (3%)
  other arithmetic  5.41 us (2%)
  local copies, waits for them, and re-layouts  4.75 us (2%)
    psum x1, waiting for transfers between devices, shards(): head_grad = lax.psum(head_term, ('img', 'txt'))  140 us
    reduce_scatter x1, waiting for transfers between devices, shards(): lax.psum_scatter(img_terms.astype(jnp.bfloat16), 'txt', scatter_dimension...  59.1 us
    all_gather x1, blocking collectives, shards(): img_block = lax.all_gather(img_unit, 'txt', axis=0, tiled=True)  31.9 us
    reduce_scatter x1, waiting for transfers between devices, shards(): lax.psum_scatter(txt_terms.astype(jnp.bfloat16), 'img', scatter_dimension...  17.3 us
    all_gather x1, blocking collectives, shards(): txt_block = lax.all_gather(txt_unit, 'img', axis=0, tiled=True)  7.11 us
  transfers between devices with their start and end apart: 3, of which 3 were waited for; matrix products, arithmetic and copies ran while one was open for 3% of the time, Pallas kernels for 0%

commit v1 on v0

v1 whole, which is shorter than its diff:
```python
import functools

import jax
import jax.numpy as jnp
import numpy as np
from jax import lax
from jax.experimental import pallas as pl
from jax.experimental.pallas import tpu as pltpu
from jax.sharding import PartitionSpec as P

eps = 1e-06
f32, bf16 = jnp.float32, jnp.bfloat16
NT = (((1,), (1,)), ((), ()))
TN = (((0,), (0,)), ((), ()))
VMEM = pl.BlockSpec(memory_space=pltpu.VMEM)
SMEM = pl.BlockSpec(memory_space=pltpu.SMEM)
LIMIT = 32 * 1024 * 1024
GATHER_BYTES = 8 * 1024 * 1024


def dot(a, b, dims=(((1,), (0,)), ((), ()))):
    return lax.dot_general(a, b, dims, preferred_element_type=f32)


def call(body, out_shape, in_specs, flops, scratch=()):
    return pl.pallas_call(
        body,
        out_shape=out_shape,
        in_specs=in_specs,
        out_specs=jax.tree.map(lambda _: VMEM, out_shape),
        scratch_shapes=scratch,
        compiler_params=pltpu.CompilerParams(vmem_limit_bytes=LIMIT),
        cost_estimate=pl.CostEstimate(flops=flops, bytes_accessed=4_000_000, transcendentals=0),
    )


def unit_body(*refs):
    out = refs[-1]
    first = 0
    for ref in refs[:-1]:
        rows = ref.shape[0]
        full = ref[...].astype(f32)
        inv = lax.rsqrt(jnp.sum(full * full, axis=1, keepdims=True) + eps)
        out[pl.ds(first, rows), :] = (full * inv).astype(bf16)
        first += rows


def chunks(total):
    width = 256
    return [(c, min(width, total - c)) for c in range(0, total, width)]


def batch_body(first, scalars, img_a, img_b, weight, txt_own, txt_sib, row_ids, col_ids, *refs):
    if first:
        d_hidden_ref, own_ref, sib_ref, grads_ref, hidden_ref, unit_ref, d_img_ref = refs
    else:
        own_in, sib_in, d_hidden_ref, own_ref, sib_ref, hidden_ref, unit_ref, d_img_ref = refs
    scale, bias = scalars[0], scalars[1]
    half = img_a.shape[0]
    rows = 2 * half
    block = own_ref.shape[0]
    for at, ref in ((0, img_a), (half, img_b)):
        hidden_ref[pl.ds(at, half), :] = dot(ref[...], weight[...])
    hidden = hidden_ref[...]
    inv = lax.rsqrt(jnp.sum(hidden * hidden, axis=1, keepdims=True) + eps)
    unit_ref[...] = (hidden * inv).astype(bf16)
    ids = row_ids[...]
    begun = False
    for side, txt in enumerate((txt_own, txt_sib)):
        total = txt.shape[0]
        for at, width in chunks(total):
            text = txt[pl.ds(at, width), :]
            logits = scale * dot(unit_ref[...], text, NT) + bias
            same = ids == col_ids[:, pl.ds(side * total + at, width)]
            flip = jnp.where(same, -1.0, 1.0)
            grad = (flip * jax.nn.sigmoid(flip * logits)).astype(bf16)
            part = dot(grad, text)
            d_img_ref[...] = d_img_ref[...] + part if begun else part
            begun = True
            if at == 0:
                edge = min(128, width)
                term = dot(grad[:, :edge], unit_ref[...], TN)[:block, :]
                ref = (own_ref, sib_ref)[side]
                ref[...] = term if first else term + (own_in, sib_in)[side][...]
    d_img = scale * d_img_ref[...]
    hidden = hidden_ref[...]
    inner = jnp.sum(hidden * d_img, axis=1, keepdims=True)
    d_hidden = (inv * (d_img - hidden * (inv * inv * inner))).astype(bf16)
    d_hidden_ref[...] = d_hidden
    if first:
        grads_ref[...] = dot(d_hidden[:block, :], weight[...], NT).astype(bf16)


def head_body(count, *refs):
    images, d_hidden, out = refs[:count], refs[count:-1], refs[-1]
    left = jnp.concatenate([ref[...] for ref in images], axis=0)
    right = jnp.concatenate([ref[...] for ref in d_hidden], axis=0)
    out[...] = dot(left, right, TN)


def text_body(scalars, texts, own, received, out):
    full = texts[...].astype(f32)
    inv = lax.rsqrt(jnp.sum(full * full, axis=1, keepdims=True) + eps)
    d_txt = scalars[0] * (own[...] + received[...])
    inner = jnp.sum(full * d_txt, axis=1, keepdims=True)
    out[...] = (inv * (d_txt - full * (inv * inv * inner))).astype(bf16)


def gathered(n_img, n_txt, images, texts, head_weight, log_scale, logit_bias):
    rows, emb = images.shape
    features = texts.shape[1]

    def move(array, axis, mask):
        size = n_img if axis == "img" else n_txt
        return lax.ppermute(array, axis, [(i, i ^ mask) for i in range(size)])

    core = functools.partial(move, axis="img", mask=1)
    over_x = functools.partial(move, axis="img", mask=2)
    over_y = functools.partial(move, axis="txt", mask=1)

    def over_z(block):
        return [block] + [move(block, "txt", mask) for mask in range(2, n_txt, 2)]

    def stack(*blocks):
        return jnp.concatenate(blocks, axis=0)

    def spread(blocks):
        middle = len(blocks) // 2
        a, b = stack(*blocks[:middle]), stack(*blocks[middle:])
        a, b = stack(a, over_y(a)), stack(b, over_x(b))
        return a, b, over_x(a), over_y(b)

    z = list(range(0, n_txt, 2))
    middle = len(z) // 2
    a = [(m, 0) for m in z[:middle]] + [(m ^ 1, 0) for m in z[:middle]]
    b = [(m, 0) for m in z[middle:]] + [(m, 2) for m in z[middle:]]
    order = a + b + [(t, i ^ 2) for t, i in a] + [(t ^ 1, i) for t, i in b]
    txt_at, img_at = lax.axis_index("txt"), lax.axis_index("img")
    within = np.tile(np.arange(rows, dtype=np.int32), len(order))
    txt_mask = np.repeat(np.array([t for t, _ in order], np.int32), rows)
    img_mask = np.repeat(np.array([i for _, i in order], np.int32), rows)
    row_ids = ((img_at ^ img_mask) * n_txt + (txt_at ^ txt_mask)) * rows + within
    own_ids = ((txt_at ^ txt_mask) * n_img + (img_at ^ img_mask)) * rows + within
    sib_ids = ((txt_at ^ txt_mask) * n_img + (img_at ^ 1 ^ img_mask)) * rows + within
    col_ids = stack(own_ids, sib_ids)[None, :]
    row_ids = row_ids[:, None]

    scalars = jnp.concatenate([jnp.exp(log_scale), logit_bias])
    txt_z = over_z(texts)
    images_later, _ = lax.optimization_barrier((images, txt_z[1]))
    img_z = over_z(images_later)
    txt_parts = spread(txt_z)
    total = len(order) * rows
    txt_own = call(unit_body, jax.ShapeDtypeStruct((total, features), bf16), [VMEM] * 4, 0)(*txt_parts)
    txt_sib = core(txt_own)
    img_parts = spread(img_z)
    sib_parts = [core(part) for part in img_parts]

    batch = total // 2
    term = jax.ShapeDtypeStruct((rows, features), f32)
    d_shape = jax.ShapeDtypeStruct((batch, features), bf16)
    scratch = [
        pltpu.VMEM((batch, features), f32),
        pltpu.VMEM((batch, features), bf16),
        pltpu.VMEM((batch, features), f32),
    ]
    flops = 2 * batch * features * (emb + 4 * total)
    d_first, own, sib, image_grads = call(
        functools.partial(batch_body, True),
        (d_shape, term, term, jax.ShapeDtypeStruct((rows, emb), bf16)),
        [SMEM] + [VMEM] * 7,
        flops,
        scratch,
    )(scalars, *img_parts[:2], head_weight, txt_own, txt_sib, row_ids[:batch], col_ids)
    d_first_sib = core(d_first)
    d_second, own, sib = call(
        functools.partial(batch_body, False),
        (d_shape, term, term),
        [SMEM] + [VMEM] * 9,
        flops,
        scratch,
    )(scalars, *img_parts[2:], head_weight, txt_own, txt_sib, row_ids[batch:], col_ids, own, sib)
    d_second_sib = core(d_second)
    received = core(sib)
    text_grads = call(
        text_body, jax.ShapeDtypeStruct((rows, features), bf16), [SMEM] + [VMEM] * 3, 0
    )(scalars, texts, own, received)

    pieces = list(img_parts) + sib_parts
    d_all = [d_first, d_second, d_first_sib, d_second_sib]
    wide = 3 if emb % 384 == 0 else 1
    head_grad = pl.pallas_call(
        functools.partial(head_body, len(pieces)),
        grid=(wide,),
        out_shape=jax.ShapeDtypeStruct((emb, features), f32),
        in_specs=[pl.BlockSpec((p.shape[0], emb // wide), lambda i: (0, i)) for p in pieces]
        + [pl.BlockSpec(d.shape, lambda i: (0, 0)) for d in d_all],
        out_specs=pl.BlockSpec((emb // wide, features), lambda i: (i, 0)),
        compiler_params=pltpu.CompilerParams(vmem_limit_bytes=LIMIT),
        cost_estimate=pl.CostEstimate(
            flops=4 * total * emb * features, bytes_accessed=8_000_000, transcendentals=0
        ),
    )(*pieces, *d_all)
    return image_grads, text_grads, head_grad


def blocked(images, texts, head_weight, log_scale, logit_bias):
    scale = jnp.exp(log_scale[0])
    bias = logit_bias[0]
    hidden = jnp.dot(images, head_weight, preferred_element_type=f32)
    img_inv = lax.rsqrt(jnp.sum(hidden * hidden, axis=1, keepdims=True) + eps)
    img_unit = (hidden * img_inv).astype(bf16)
    txt_full = texts.astype(f32)
    txt_inv = lax.rsqrt(jnp.sum(txt_full * txt_full, axis=1, keepdims=True) + eps)
    txt_unit = (txt_full * txt_inv).astype(bf16)
    img_block = lax.all_gather(img_unit, "txt", axis=0, tiled=True)
    txt_block = lax.all_gather(txt_unit, "img", axis=0, tiled=True)
    total_rows = img_block.shape[0]
    total_cols = txt_block.shape[0]
    features = img_block.shape[1]
    row_first = lax.axis_index("img") * total_rows
    col_first = lax.axis_index("txt") * total_cols
    columns = col_first + jnp.arange(total_cols, dtype=jnp.int32)
    width = 512 if total_rows % 512 == 0 else total_rows
    count = total_rows // width
    blocks = img_block.reshape(count, width, features)

    def step(carry, inputs):
        block, index = inputs
        logits = scale * dot(block, txt_block, NT) + bias
        row_ids = row_first + index * width + jnp.arange(width, dtype=jnp.int32)
        label = jnp.where(row_ids[:, None] == columns[None, :], 1.0, -1.0).astype(f32)
        grad = (-label * jax.nn.sigmoid(-label * logits)).astype(bf16)
        d_rows = scale * dot(grad, txt_block)
        carry = carry + scale * dot(grad, block, TN)
        return (carry, d_rows)

    txt_terms, row_terms = lax.scan(
        step,
        jnp.zeros((total_cols, features), f32),
        (blocks, jnp.arange(count, dtype=jnp.int32)),
    )
    img_terms = row_terms.reshape(total_rows, features)
    d_img = lax.psum_scatter(
        img_terms.astype(bf16), "txt", scatter_dimension=0, tiled=True
    ).astype(f32)
    inner = jnp.sum(hidden * d_img, axis=1, keepdims=True)
    d_hidden = (img_inv * (d_img - hidden * img_inv * img_inv * inner)).astype(bf16)
    image_grads = dot(d_hidden, head_weight, NT).astype(bf16)
    head_grad = lax.psum(dot(images, d_hidden, TN), ("img", "txt"))
    d_txt = lax.psum_scatter(
        txt_terms.astype(bf16), "img", scatter_dimension=0, tiled=True
    ).astype(f32)
    inner_txt = jnp.sum(txt_full * d_txt, axis=1, keepdims=True)
    text_grads = (txt_inv * (d_txt - txt_full * txt_inv * txt_inv * inner_txt)).astype(bf16)
    return (image_grads, text_grads, head_grad)


def solution(mesh):
    n_img, n_txt = mesh.shape["img"], mesh.shape["txt"]

    def shards(images, texts, head_weight, log_scale, logit_bias):
        width = images.shape[1] + texts.shape[1]
        held = 2 * n_img * n_txt * images.shape[0] * width
        same = images.shape[0] == texts.shape[0]
        if n_img == 4 and n_txt % 4 == 0 and same and held <= GATHER_BYTES:
            return gathered(n_img, n_txt, images, texts, head_weight, log_scale, logit_bias)
        return blocked(images, texts, head_weight, log_scale, logit_bias)

    return jax.shard_map(
        shards,
        mesh=mesh,
        in_specs=(P(("img", "txt"), None), P(("txt", "img"), None), P(), P(), P()),
        out_specs=(P(("img", "txt"), None), P(("txt", "img"), None), P()),
        check_vma=False,
    )
```

time: 290 us -> 63.9 us (0.22)
  waiting for transfers between devices: 216 us -> 18.7 us
  blocking collectives: 39 us -> 0 us
  starting transfers between devices: 0.12 us -> 21.4 us
  Pallas kernels: 0 us -> 16.5 us
  between operations: 15.3 us -> 2.14 us
  matrix products: 8.24 us -> 0 us
    psum x1 -> x0, waiting for transfers between devices: 140 us -> none  [shards(): head_grad = lax.psum(head_term, ('img', 'txt'))]
    reduce_scatter x2 -> x0, waiting for transfers between devices: 76.4 us -> none  [the longest x1 59.1 us: shards(): lax.psum_scatter(img_terms.astype(jnp.bfloat16), 'txt', scatter_dimension...]
    all_gather x2 -> x0, blocking collectives: 39 us -> none  [the longest x1 31.9 us: shards(): img_block = lax.all_gather(img_unit, 'txt', axis=0, tiled=True)]
    ppermute x0 -> x22, starting transfers between devices: none -> 21.4 us  [move(): return lax.ppermute(array, axis, [(i, i ^ mask) for i in range(size)])]
    ppermute x0 -> x22, waiting for transfers between devices: none -> 18.7 us  [move(): return lax.ppermute(array, axis, [(i, i ^ mask) for i in range(size)])]
    pallas_call x0 -> x5, Pallas kernels: none -> 16.5 us  [the longest x1 5.72 us: gathered(): call(functools.partial(batch_body, True), (d_shape, term, term, jax.Shape...]
    dot_general x6 -> x0, matrix products: 8.24 us -> none  [the longest x1 3.08 us: shards(): lax.dot_general(images, d_hidden, (((0,), (0,)), ((), ())), preferred_ele...]
  transfers between devices with their start and end apart: 3 -> 22, of which waited for: 3 -> 9; matrix products, arithmetic and copies ran while one was open for 3% -> 8% of each run, Pallas kernels for 0% -> 18%
where the time goes in v1:
time: 63.9 us; the launch traced here: 63.6 us
  starting transfers between devices  21.4 us (33%)
  waiting for transfers between devices  18.7 us (29%)
  Pallas kernels  16.5 us (26%)
  other arithmetic  2.61 us (4%)
  local copies, waits for them, and re-layouts  2.18 us (3%)
  between operations  2.14 us (3%)
    ppermute x22, starting transfers between devices, move(): return lax.ppermute(array, axis, [(i, i ^ mask) for i in range(size)])  21.4 us
    ppermute x22, waiting for transfers between devices, move(): return lax.ppermute(array, axis, [(i, i ^ mask) for i in range(size)])  18.7 us
    pallas_call x1, Pallas kernels, gathered(): call(functools.partial(batch_body, True), (d_shape, term, term, jax.Shape...  5.72 us
    pallas_call x1, Pallas kernels, gathered(): pl.pallas_call(functools.partial(head_body, len(pieces)), grid=(wide,), o...  4.84 us
    pallas_call x1, Pallas kernels, gathered(): call(functools.partial(batch_body, False), (d_shape, term, term), [SMEM]...  4.37 us
    unnamed x12, local copies, waits for them, and re-layouts  1.86 us
    concatenate x5, other arithmetic, stack(): return jnp.concatenate(blocks, axis=0)  1.8 us
    pallas_call x1, Pallas kernels, gathered(): call(text_body, jax.ShapeDtypeStruct((rows, features), bf16), [SMEM] + [V...  1.28 us
  transfers between devices with their start and end apart: 22, of which 9 were waited for; matrix products, arithmetic and copies ran while one was open for 8% of the time, Pallas kernels for 18%

profile of v1, /device:TPU:0, one launch (start us, length us, event | category | flops | bytes accessed | tf_op | source)
XLA Modules:
  0.0 63.6 jit_solution(6741478419627286246)
XLA Ops:
  0.6 4.1 %collective-permute-start.7 = (bf16[48,640]{1,0:T(8,128)(2,1)}, bf16[48,640]{1,0:T(8,128)(2,1)S(1)}, u32[]{:S(2)}, u32[]{:S(2)}) collective-permute-start(bf16[48,640]{1,0:T(8,128)(2,1)} %texts.1), channel_id=1, source_target_pairs={{0,4},{1,5},{2,6},{3,7},{4,0},{5,1},{6,2},{7,3},{8,12},{9,13},{10,... | collective-permute-start | bytes 184328 | tf_op jit(solution)/shard_map/ppermute | solution.py:115
  4.7 1.6 %collective-permute-start = (bf16[48,640]{1,0:T(8,128)(2,1)}, bf16[48,640]{1,0:T(8,128)(2,1)S(1)}, u32[]{:S(2)}, u32[]{:S(2)}) collective-permute-start(bf16[48,640]{1,0:T(8,128)(2,1)} %texts.1), channel_id=1, source_target_pairs={{0,2},{1,3},{2,0},{3,1},{4,6},{5,7},{6,4},{7,5},{8,10},{9,11},{10,... | collective-permute-start | bytes 184328 | tf_op jit(solution)/shard_map/ppermute | solution.py:115
  7.7 0.7 %fusion.4 = (s32[768]{0:T(1024)S(1)}, s32[768]{0:T(1024)S(1)}, s32[768]{0:T(1024)S(1)}) fusion(s32[768]{0:T(1024)} %constant.24.clone, s32[768]{0:T(1024)} %constant.22.clone, s32[768]{0:T(1024)} %constant.23.clone, s32[]{:T(128)S(6)} %axis_index.25, s32[]{:T(128)S(6)} %axis_index.23, s32[]{:T(128)S(6)} %xor.31), kind=kLoop, calls=%fused_computation.25 | loop fusion | flops 10752 | bytes 18444 | tf_op jit(solution)/shard_map/add | solution.py:143
  8.4 0.8 %constant_dynamic-update-slice_fusion.8 = bf16[192,640]{1,0:T(8,128)(2,1)S(1)} fusion(bf16[48,640]{1,0:T(8,128)(2,1)} %texts.1), kind=kLoop, calls=%fused_computation.12 | loop fusion | bytes 122880
  9.2 0.0 collective-permute-done
  9.3 3.9 %collective-permute-start.4 = (bf16[48,1152]{1,0:T(8,128)(2,1)}, bf16[48,1152]{1,0:T(8,128)(2,1)S(1)}, u32[]{:S(2)}, u32[]{:S(2)}) collective-permute-start(bf16[48,1152]{1,0:T(8,128)(2,1)} %param.8), channel_id=1, source_target_pairs={{0,6},{1,7},{2,4},{3,5},{4,2},{5,3},{6,0},{7,1},{8,14},{9,15},{10,... | collective-permute-start | bytes 331784 | tf_op jit(solution)/shard_map/ppermute | solution.py:115
  13.1 0.0 collective-permute-start.3
  13.1 0.6 %collective-permute-start.1 = (bf16[48,1152]{1,0:T(8,128)(2,1)}, bf16[48,1152]{1,0:T(8,128)(2,1)S(1)}, u32[]{:S(2)}, u32[]{:S(2)}) collective-permute-start(bf16[48,1152]{1,0:T(8,128)(2,1)} %param.8), channel_id=1, source_target_pairs={{0,2},{1,3},{2,0},{3,1},{4,6},{5,7},{6,4},{7,5},{8,10},{9,11},{10,... | collective-permute-start | bytes 331784 | tf_op jit(solution)/shard_map/ppermute | solution.py:115
  13.8 0.9 %constant_dynamic-update-slice_fusion.2 = bf16[192,1152]{1,0:T(8,128)(2,1)S(1)} fusion(bf16[48,1152]{1,0:T(8,128)(2,1)} %param.8), kind=kLoop, calls=%fused_computation.6 | loop fusion | bytes 221184
  14.7 0.8 %pad_maximum_fusion.2 = bf16[96,640]{1,0:T(8,128)(2,1)S(1)} fusion(bf16[48,640]{1,0:T(8,128)(2,1)S(1)} %collective-permute-done, bf16[48,640]{1,0:T(8,128)(2,1)} %texts.1), kind=kLoop, calls=%fused_computation.2 | loop fusion | flops 245760 | bytes 245760 | tf_op jit(solution)/shard_map/concatenate | solution.py:125
  15.6 0.0 copy-start.1
  15.6 0.0 collective-permute-done.7
  15.6 1.7 %collective-permute-start.6 = (bf16[96,640]{1,0:T(8,128)(2,1)S(1)}, bf16[96,640]{1,0:T(8,128)(2,1)S(1)}, u32[]{:S(2)}, u32[]{:S(2)}) collective-permute-start(bf16[96,640]{1,0:T(8,128)(2,1)S(1)} %pad_maximum_fusion.2), channel_id=1, source_target_pairs={{0,1},{1,0},{2,3},{3,2},{4,5},{5,4},{6,7},{7,6},{8,9},{9,8},{10,11... | collective-permute-start | bytes 368648 | tf_op jit(solution)/shard_map/ppermute | solution.py:115
  17.3 0.0 collective-permute-done.8
  17.3 1.6 %collective-permute-start.9 = (bf16[96,640]{1,0:T(8,128)(2,1)S(1)}, bf16[96,640]{1,0:T(8,128)(2,1)S(1)}, u32[]{:S(2)}, u32[]{:S(2)}) collective-permute-start(bf16[96,640]{1,0:T(8,128)(2,1)S(1)} %pad_maximum_fusion.3), channel_id=1, source_target_pairs={{0,16},{8,24},{16,0},{24,8},{1,17},{9,25},{17,1},{25,9},{2,18},{10... | collective-permute-start | bytes 368648 | tf_op jit(solution)/shard_map/ppermute | solution.py:115
  18.9 0.0 collective-permute-done.4
  18.9 3.1 %collective-permute-done.3 = bf16[48,1152]{1,0:T(8,128)(2,1)S(1)} collective-permute-done((bf16[48,1152]{1,0:T(8,128)(2,1)}, bf16[48,1152]{1,0:T(8,128)(2,1)S(1)}, u32[]{:S(2)}, u32[]{:S(2)}) %collective-permute-start.3) | collective-permute-done | bytes 110624 | tf_op jit(solution)/shard_map/ppermute | solution.py:115
  22.0 1.6 %collective-permute-start.5 = (bf16[96,1152]{1,0:T(8,128)(2,1)S(1)}, bf16[96,1152]{1,0:T(8,128)(2,1)S(1)}, u32[]{:S(2)}, u32[]{:S(2)}) collective-permute-start(bf16[96,1152]{1,0:T(8,128)(2,1)S(1)} %pad_maximum_fusion.1), channel_id=1, source_target_pairs={{0,16},{8,24},{16,0},{24,8},{1,17},{9,25},{17,1},{25,9},{2,18},{10... | collective-permute-start | bytes 663560 | tf_op jit(solution)/shard_map/ppermute | solution.py:115
  23.6 0.9 %pad_maximum_fusion = bf16[96,1152]{1,0:T(8,128)(2,1)S(1)} fusion(bf16[48,1152]{1,0:T(8,128)(2,1)S(1)} %collective-permute-done.1, bf16[48,1152]{1,0:T(8,128)(2,1)} %param.8), kind=kLoop, calls=%fused_computation | loop fusion | flops 442368 | bytes 442368 | tf_op jit(solution)/shard_map/concatenate | solution.py:125
  24.5 1.6 %collective-permute-start.2 = (bf16[96,1152]{1,0:T(8,128)(2,1)S(1)}, bf16[96,1152]{1,0:T(8,128)(2,1)S(1)}, u32[]{:S(2)}, u32[]{:S(2)}) collective-permute-start(bf16[96,1152]{1,0:T(8,128)(2,1)S(1)} %pad_maximum_fusion), channel_id=1, source_target_pairs={{0,1},{1,0},{2,3},{3,2},{4,5},{5,4},{6,7},{7,6},{8,9},{9,8},{10,11... | collective-permute-start | bytes 663560 | tf_op jit(solution)/shard_map/ppermute | solution.py:115
  26.1 0.6 collective-permute-start.10
  26.8 0.6 collective-permute-start.11
  27.4 6.6 %collective-permute-done.10.refs_2_ = bf16[192,640]{1,0:T(8,128)(2,1)S(1)} collective-permute-done((bf16[192,640]{1,0:T(8,128)(2,1)S(1)}, bf16[192,640]{1,0:T(8,128)(2,1)S(1)}, u32[]{:S(2)}, u32[]{:S(2)}) %collective-permute-start.10) | collective-permute-done | bytes 245792 | tf_op jit(solution)/shard_map/ppermute | solution.py:115
  34.0 2.2 %collective-permute-done.11.refs_3_ = bf16[192,640]{1,0:T(8,128)(2,1)S(1)} collective-permute-done((bf16[192,640]{1,0:T(8,128)(2,1)S(1)}, bf16[192,640]{1,0:T(8,128)(2,1)S(1)}, u32[]{:S(2)}, u32[]{:S(2)}) %collective-permute-start.11) | collective-permute-done | bytes 245792 | tf_op jit(solution)/shard_map/ppermute | solution.py:115
  36.2 0.3 shard_map.103.txt_own
  36.5 0.1 collective-permute-start.12
  36.7 0.6 collective-permute-start.13
  37.3 1.6 %collective-permute-start.14 = (bf16[192,1152]{1,0:T(8,128)(2,1)S(1)}, bf16[192,1152]{1,0:T(8,128)(2,1)S(1)}, u32[]{:S(2)}, u32[]{:S(2)}) collective-permute-start(bf16[192,1152]{1,0:T(8,128)(2,1)S(1)} %constant_dynamic-update-slice_fusion.3.img_b.refs_1_), channel_id=1, source_target_pairs={{0,1},{1,0},{2,3},{3,2},{4,5},{5,4},{6,7},{7,6},{8,9},{9,8},{10,11... | collective-permute-start | bytes 1327112 | tf_op jit(solution)/shard_map/ppermute | solution.py:115
  38.9 0.1 slice.17.row_ids
  39.0 0.1 slice.16.row_ids
  39.1 0.1 pad_maximum_fusion.4.scalars
  39.2 0.0 collective-permute-start.16
  39.2 5.7 %shard_map.104 = (bf16[384,640]{1,0:T(8,128)(2,1)S(1)}, f32[48,640]{1,0:T(8,128)S(1)}, f32[48,640]{1,0:T(8,128)S(1)}, bf16[48,1152]{1,0:T(8,128)(2,1)}) custom-call(f32[2]{0:T(128)S(1)} %pad_maximum_fusion.4.scalars, bf16[192,1152]{1,0:T(8,128)(2,1)S(1)} %constant_dynamic-update-slice_fusion.img_a.refs_0_, ...), custom_call_target="tpu_custom_call" | custom-call | flops 2076180480 | bytes 4000000 | tf_op jit(solution)/shard_map/pallas_call | solution.py:168
  44.9 4.3 %collective-permute-done.13.img_a.refs_2_ = bf16[192,1152]{1,0:T(8,128)(2,1)S(1)} collective-permute-done((bf16[192,1152]{1,0:T(8,128)(2,1)S(1)}, bf16[192,1152]{1,0:T(8,128)(2,1)S(1)}, u32[]{:S(2)}, u32[]{:S(2)}) %collective-permute-start.13) | collective-permute-done | bytes 442400 | tf_op jit(solution)/shard_map/ppermute | solution.py:115
  49.3 0.3 collective-permute-done.14.img_b.refs_3_
  49.6 4.4 %shard_map.105 = (bf16[384,640]{1,0:T(8,128)(2,1)S(1)}, f32[48,640]{1,0:T(8,128)S(1)}, f32[48,640]{1,0:T(8,128)S(1)}) custom-call(f32[2]{0:T(128)S(1)} %pad_maximum_fusion.4.scalars, bf16[192,1152]{1,0:T(8,128)(2,1)S(1)} %collective-permute-done.13.img_a.refs_2_, bf16[192,1152]{1,0:T(8,128)(2,1)S(1)} %collective-permute-done.14.img_b.refs_3_, ...), custom_call_target="tpu_custom_call" | custom-call | flops 2076180480 | bytes 4000000 | tf_op jit(solution)/shard_map/pallas_call | solution.py:176
  54.0 0.1 collective-permute-start.15
  54.1 0.5 collective-permute-start.21
  54.6 0.1 collective-permute-start.20
  54.7 0.4 collective-permute-start.17
  55.1 0.1 collective-permute-start.18
  55.2 0.2 collective-permute-done.15.received
  55.4 0.2 collective-permute-start.19
  55.6 1.3 %shard_map.106 = bf16[48,640]{1,0:T(8,128)(2,1)} custom-call(f32[2]{0:T(128)S(1)} %pad_maximum_fusion.4.scalars, bf16[48,640]{1,0:T(8,128)(2,1)S(1)} %copy-done, f32[48,640]{1,0:T(8,128)S(1)} %get-tuple-element.15.own, f32[48,640]{1,0:T(8,128)S(1)} %collective-permute-done.15.received), custom_call_target="tpu_custom_call" | custom-call | bytes 4000000 | tf_op jit(solution)/shard_map/pallas_call | solution.py:185
  56.9 0.6 collective-permute-done.17.refs_5_
  57.5 0.6 collective-permute-done.18.refs_6_
  58.1 0.6 collective-permute-done.19.refs_7_
  58.7 4.8 %shard_map.107 = f32[1152,640]{1,0:T(8,128)} custom-call(bf16[192,1152]{1,0:T(8,128)(2,1)S(1)} %constant_dynamic-update-slice_fusion.img_a.refs_0_, bf16[192,1152]{1,0:T(8,128)(2,1)S(1)} %constant_dynamic-update-slice_fusion.3.img_b.refs_1_, bf16[192,1152]{1,0:T(8,128)(2,1)S(1)} %collective-permute-done.13.img_a.refs_2_, ...), custom_call_target="tpu_custom_call" | custom-call | flops 2264924160 | bytes 8000000 | tf_op jit(solution)/shard_map/pallas_call | solution.py:192
  (28 shorter events, 0.2 us)
Async XLA Ops:
  0.6 15.0 %collective-permute-start.7 = (bf16[48,640]{1,0:T(8,128)(2,1)}, bf16[48,640]{1,0:T(8,128)(2,1)S(1)}, u32[]{:S(2)}, u32[]{:S(2)}) collective-permute-start(bf16[48,640]{1,0:T(8,128)(2,1)} %texts.1), channel_id=1, source_target_pairs={{0,4},{1,5},{2,6},{3,7},{4,0},{5,1},{6,2},{7,3},{8,12},{9,13},{10,... | collective-permute-start | bytes 184328 | tf_op jit(solution)/shard_map/ppermute | solution.py:115
  4.7 4.5 %collective-permute-start = (bf16[48,640]{1,0:T(8,128)(2,1)}, bf16[48,640]{1,0:T(8,128)(2,1)S(1)}, u32[]{:S(2)}, u32[]{:S(2)}) collective-permute-start(bf16[48,640]{1,0:T(8,128)(2,1)} %texts.1), channel_id=1, source_target_pairs={{0,2},{1,3},{2,0},{3,1},{4,6},{5,7},{6,4},{7,5},{8,10},{9,11},{10,... | collective-permute-start | bytes 184328 | tf_op jit(solution)/shard_map/ppermute | solution.py:115
  6.3 11.0 %collective-permute-start.8 = (bf16[48,640]{1,0:T(8,128)(2,1)}, bf16[48,640]{1,0:T(8,128)(2,1)S(1)}, u32[]{:S(2)}, u32[]{:S(2)}) collective-permute-start(bf16[48,640]{1,0:T(8,128)(2,1)} %texts.1), channel_id=1, source_target_pairs={{0,6},{1,7},{2,4},{3,5},{4,2},{5,3},{6,0},{7,1},{8,14},{9,15},{10,... | collective-permute-start | bytes 184328 | tf_op jit(solution)/shard_map/ppermute | solution.py:115
  9.3 9.7 %collective-permute-start.4 = (bf16[48,1152]{1,0:T(8,128)(2,1)}, bf16[48,1152]{1,0:T(8,128)(2,1)S(1)}, u32[]{:S(2)}, u32[]{:S(2)}) collective-permute-start(bf16[48,1152]{1,0:T(8,128)(2,1)} %param.8), channel_id=1, source_target_pairs={{0,6},{1,7},{2,4},{3,5},{4,2},{5,3},{6,0},{7,1},{8,14},{9,15},{10,... | collective-permute-start | bytes 331784 | tf_op jit(solution)/shard_map/ppermute | solution.py:115
  13.1 8.9 %collective-permute-start.3 = (bf16[48,1152]{1,0:T(8,128)(2,1)}, bf16[48,1152]{1,0:T(8,128)(2,1)S(1)}, u32[]{:S(2)}, u32[]{:S(2)}) collective-permute-start(bf16[48,1152]{1,0:T(8,128)(2,1)} %param.8), channel_id=1, source_target_pairs={{0,4},{1,5},{2,6},{3,7},{4,0},{5,1},{6,2},{7,3},{8,12},{9,13},{10,... | collective-permute-start | bytes 331784 | tf_op jit(solution)/shard_map/ppermute | solution.py:115
  13.1 10.5 %collective-permute-start.1 = (bf16[48,1152]{1,0:T(8,128)(2,1)}, bf16[48,1152]{1,0:T(8,128)(2,1)S(1)}, u32[]{:S(2)}, u32[]{:S(2)}) collective-permute-start(bf16[48,1152]{1,0:T(8,128)(2,1)} %param.8), channel_id=1, source_target_pairs={{0,2},{1,3},{2,0},{3,1},{4,6},{5,7},{6,4},{7,5},{8,10},{9,11},{10,... | collective-permute-start | bytes 331784 | tf_op jit(solution)/shard_map/ppermute | solution.py:115
  15.6 23.6 %copy-start.1 = (bf16[1152,640]{1,0:T(8,128)(2,1)S(1)}, bf16[1152,640]{1,0:T(8,128)(2,1)}, u32[]{:S(2)}) copy-start(bf16[1152,640]{1,0:T(8,128)(2,1)} %weight.3) | copy-start | bytes 4423684
  15.6 10.5 %collective-permute-start.6 = (bf16[96,640]{1,0:T(8,128)(2,1)S(1)}, bf16[96,640]{1,0:T(8,128)(2,1)S(1)}, u32[]{:S(2)}, u32[]{:S(2)}) collective-permute-start(bf16[96,640]{1,0:T(8,128)(2,1)S(1)} %pad_maximum_fusion.2), channel_id=1, source_target_pairs={{0,1},{1,0},{2,3},{3,2},{4,5},{5,4},{6,7},{7,6},{8,9},{9,8},{10,11... | collective-permute-start | bytes 368648 | tf_op jit(solution)/shard_map/ppermute | solution.py:115
  17.3 9.4 %collective-permute-start.9 = (bf16[96,640]{1,0:T(8,128)(2,1)S(1)}, bf16[96,640]{1,0:T(8,128)(2,1)S(1)}, u32[]{:S(2)}, u32[]{:S(2)}) collective-permute-start(bf16[96,640]{1,0:T(8,128)(2,1)S(1)} %pad_maximum_fusion.3), channel_id=1, source_target_pairs={{0,16},{8,24},{16,0},{24,8},{1,17},{9,25},{17,1},{25,9},{2,18},{10... | collective-permute-start | bytes 368648 | tf_op jit(solution)/shard_map/ppermute | solution.py:115
  22.0 15.2 %collective-permute-start.5 = (bf16[96,1152]{1,0:T(8,128)(2,1)S(1)}, bf16[96,1152]{1,0:T(8,128)(2,1)S(1)}, u32[]{:S(2)}, u32[]{:S(2)}) collective-permute-start(bf16[96,1152]{1,0:T(8,128)(2,1)S(1)} %pad_maximum_fusion.1), channel_id=1, source_target_pairs={{0,16},{8,24},{16,0},{24,8},{1,17},{9,25},{17,1},{25,9},{2,18},{10... | collective-permute-start | bytes 663560 | tf_op jit(solution)/shard_map/ppermute | solution.py:115
  24.5 12.1 %collective-permute-start.2 = (bf16[96,1152]{1,0:T(8,128)(2,1)S(1)}, bf16[96,1152]{1,0:T(8,128)(2,1)S(1)}, u32[]{:S(2)}, u32[]{:S(2)}) collective-permute-start(bf16[96,1152]{1,0:T(8,128)(2,1)S(1)} %pad_maximum_fusion), channel_id=1, source_target_pairs={{0,1},{1,0},{2,3},{3,2},{4,5},{5,4},{6,7},{7,6},{8,9},{9,8},{10,11... | collective-permute-start | bytes 663560 | tf_op jit(solution)/shard_map/ppermute | solution.py:115
  26.1 7.9 %collective-permute-start.10 = (bf16[192,640]{1,0:T(8,128)(2,1)S(1)}, bf16[192,640]{1,0:T(8,128)(2,1)S(1)}, u32[]{:S(2)}, u32[]{:S(2)}) collective-permute-start(bf16[192,640]{1,0:T(8,128)(2,1)S(1)} %constant_dynamic-update-slice_fusion.6.refs_0_), channel_id=1, source_target_pairs={{0,16},{8,24},{16,0},{24,8},{1,17},{9,25},{17,1},{25,9},{2,18},{10... | collective-permute-start | bytes 737288 | tf_op jit(solution)/shard_map/ppermute | solution.py:115
  26.8 9.4 %collective-permute-start.11 = (bf16[192,640]{1,0:T(8,128)(2,1)S(1)}, bf16[192,640]{1,0:T(8,128)(2,1)S(1)}, u32[]{:S(2)}, u32[]{:S(2)}) collective-permute-start(bf16[192,640]{1,0:T(8,128)(2,1)S(1)} %constant_dynamic-update-slice_fusion.9.refs_1_), channel_id=1, source_target_pairs={{0,1},{1,0},{2,3},{3,2},{4,5},{5,4},{6,7},{7,6},{8,9},{9,8},{10,11... | collective-permute-start | bytes 737288 | tf_op jit(solution)/shard_map/ppermute | solution.py:115
  36.5 2.7 %collective-permute-start.12 = (bf16[768,640]{1,0:T(8,128)(2,1)S(1)}, bf16[768,640]{1,0:T(8,128)(2,1)S(1)}, u32[]{:S(2)}, u32[]{:S(2)}) collective-permute-start(bf16[768,640]{1,0:T(8,128)(2,1)S(1)} %shard_map.103.txt_own), channel_id=1, source_target_pairs={{0,8},{8,0},{16,24},{24,16},{1,9},{9,1},{17,25},{25,17},{2,10},{10... | collective-permute-start | bytes 2949128 | tf_op jit(solution)/shard_map/ppermute | solution.py:115
  36.7 12.6 %collective-permute-start.13 = (bf16[192,1152]{1,0:T(8,128)(2,1)S(1)}, bf16[192,1152]{1,0:T(8,128)(2,1)S(1)}, u32[]{:S(2)}, u32[]{:S(2)}) collective-permute-start(bf16[192,1152]{1,0:T(8,128)(2,1)S(1)} %constant_dynamic-update-slice_fusion.img_a.refs_0_), channel_id=1, source_target_pairs={{0,16},{8,24},{16,0},{24,8},{1,17},{9,25},{17,1},{25,9},{2,18},{10... | collective-permute-start | bytes 1327112 | tf_op jit(solution)/shard_map/ppermute | solution.py:115
  37.3 12.3 %collective-permute-start.14 = (bf16[192,1152]{1,0:T(8,128)(2,1)S(1)}, bf16[192,1152]{1,0:T(8,128)(2,1)S(1)}, u32[]{:S(2)}, u32[]{:S(2)}) collective-permute-start(bf16[192,1152]{1,0:T(8,128)(2,1)S(1)} %constant_dynamic-update-slice_fusion.3.img_b.refs_1_), channel_id=1, source_target_pairs={{0,1},{1,0},{2,3},{3,2},{4,5},{5,4},{6,7},{7,6},{8,9},{9,8},{10,11... | collective-permute-start | bytes 1327112 | tf_op jit(solution)/shard_map/ppermute | solution.py:115
  39.2 15.9 %collective-permute-start.16 = (bf16[192,1152]{1,0:T(8,128)(2,1)S(1)}, bf16[192,1152]{1,0:T(8,128)(2,1)S(1)}, u32[]{:S(2)}, u32[]{:S(2)}) collective-permute-start(bf16[192,1152]{1,0:T(8,128)(2,1)S(1)} %constant_dynamic-update-slice_fusion.img_a.refs_0_), channel_id=1, source_target_pairs={{0,8},{8,0},{16,24},{24,16},{1,9},{9,1},{17,25},{25,17},{2,10},{10... | collective-permute-start | bytes 1327112 | tf_op jit(solution)/shard_map/ppermute | solution.py:115
  49.6 6.0 %copy-start = (bf16[48,640]{1,0:T(8,128)(2,1)S(1)}, bf16[48,640]{1,0:T(8,128)(2,1)}, u32[]{:S(2)}) copy-start(bf16[48,640]{1,0:T(8,128)(2,1)} %texts.1) | copy-start | bytes 184324
  54.0 1.4 %collective-permute-start.15 = (f32[48,640]{1,0:T(8,128)S(1)}, f32[48,640]{1,0:T(8,128)S(1)}, u32[]{:S(2)}, u32[]{:S(2)}) collective-permute-start(f32[48,640]{1,0:T(8,128)S(1)} %get-tuple-element.16), channel_id=1, source_target_pairs={{0,8},{8,0},{16,24},{24,16},{1,9},{9,1},{17,25},{25,17},{2,10},{10... | collective-permute-start | bytes 368648 | tf_op jit(solution)/shard_map/ppermute | solution.py:115
  54.1 4.6 %collective-permute-start.21 = (bf16[384,640]{1,0:T(8,128)(2,1)S(1)}, bf16[384,640]{1,0:T(8,128)(2,1)S(1)}, u32[]{:S(2)}, u32[]{:S(2)}) collective-permute-start(bf16[384,640]{1,0:T(8,128)(2,1)S(1)} %get-tuple-element.18.refs_9_), channel_id=1, source_target_pairs={{0,8},{8,0},{16,24},{24,16},{1,9},{9,1},{17,25},{25,17},{2,10},{10... | collective-permute-start | bytes 1474568 | tf_op jit(solution)/shard_map/ppermute | solution.py:115
  54.6 4.1 %collective-permute-start.20 = (bf16[384,640]{1,0:T(8,128)(2,1)S(1)}, bf16[384,640]{1,0:T(8,128)(2,1)S(1)}, u32[]{:S(2)}, u32[]{:S(2)}) collective-permute-start(bf16[384,640]{1,0:T(8,128)(2,1)S(1)} %get-tuple-element.17.refs_8_), channel_id=1, source_target_pairs={{0,8},{8,0},{16,24},{24,16},{1,9},{9,1},{17,25},{25,17},{2,10},{10... | collective-permute-start | bytes 1474568 | tf_op jit(solution)/shard_map/ppermute | solution.py:115
  54.7 2.8 %collective-permute-start.17 = (bf16[192,1152]{1,0:T(8,128)(2,1)S(1)}, bf16[192,1152]{1,0:T(8,128)(2,1)S(1)}, u32[]{:S(2)}, u32[]{:S(2)}) collective-permute-start(bf16[192,1152]{1,0:T(8,128)(2,1)S(1)} %constant_dynamic-update-slice_fusion.3.img_b.refs_1_), channel_id=1, source_target_pairs={{0,8},{8,0},{16,24},{24,16},{1,9},{9,1},{17,25},{25,17},{2,10},{10... | collective-permute-start | bytes 1327112 | tf_op jit(solution)/shard_map/ppermute | solution.py:115
  55.1 3.0 %collective-permute-start.18 = (bf16[192,1152]{1,0:T(8,128)(2,1)S(1)}, bf16[192,1152]{1,0:T(8,128)(2,1)S(1)}, u32[]{:S(2)}, u32[]{:S(2)}) collective-permute-start(bf16[192,1152]{1,0:T(8,128)(2,1)S(1)} %collective-permute-done.13.img_a.refs_2_), channel_id=1, source_target_pairs={{0,8},{8,0},{16,24},{24,16},{1,9},{9,1},{17,25},{25,17},{2,10},{10... | collective-permute-start | bytes 1327112 | tf_op jit(solution)/shard_map/ppermute | solution.py:115
  55.4 3.3 %collective-permute-start.19 = (bf16[192,1152]{1,0:T(8,128)(2,1)S(1)}, bf16[192,1152]{1,0:T(8,128)(2,1)S(1)}, u32[]{:S(2)}, u32[]{:S(2)}) collective-permute-start(bf16[192,1152]{1,0:T(8,128)(2,1)S(1)} %collective-permute-done.14.img_b.refs_3_), channel_id=1, source_target_pairs={{0,8},{8,0},{16,24},{24,16},{1,9},{9,1},{17,25},{25,17},{2,10},{10... | collective-permute-start | bytes 1327112 | tf_op jit(solution)/shard_map/ppermute | solution.py:115

commit v2 on v0

v2 whole, which is shorter than its diff:
```python
import functools

import jax
import jax.numpy as jnp
import numpy as np
from jax import lax
from jax.experimental import pallas as pl
from jax.experimental.pallas import tpu as pltpu
from jax.sharding import PartitionSpec as P

eps = 1e-06
f32, bf16 = jnp.float32, jnp.bfloat16
NT = (((1,), (1,)), ((), ()))
TN = (((0,), (0,)), ((), ()))
VMEM = pl.BlockSpec(memory_space=pltpu.VMEM)
ANY = pl.BlockSpec(memory_space=pl.ANY)
SMEM = pl.BlockSpec(memory_space=pltpu.SMEM)
LIMIT = 32 * 1024 * 1024
GATHER_BYTES = 8 * 1024 * 1024


def dot(a, b, dims=(((1,), (0,)), ((), ()))):
    return lax.dot_general(a, b, dims, preferred_element_type=f32)


def call(body, out_shape, in_specs, flops, scratch=()):
    return pl.pallas_call(
        body,
        out_shape=out_shape,
        in_specs=in_specs,
        out_specs=jax.tree.map(lambda _: VMEM, out_shape),
        scratch_shapes=scratch,
        compiler_params=pltpu.CompilerParams(vmem_limit_bytes=LIMIT),
        cost_estimate=pl.CostEstimate(flops=flops, bytes_accessed=0, transcendentals=0),
    )


def source(place, side, entry):
    z, first, second = entry
    over = (place[2], place[3]) if side == 0 else (place[3], place[2])
    mask = first * over[0] + second * over[1]
    return place[0] ^ (2 * (mask // 2)), place[1] ^ z ^ lax.rem(mask, 2)


def unit_body(order, n_img, place, half, other, *outs):
    outs, whole, ids = outs[:-2], outs[-2], outs[-1]
    rows = half.shape[0]
    block = 2 * rows // len(order)
    total = 2 * rows
    lane = lax.broadcasted_iota(jnp.int32, ids.shape, 1)
    found = jnp.zeros(ids.shape, jnp.int32)
    for k, entry in enumerate(order):
        for side in (0, 1):
            img, txt = source(place, side, entry)
            first_id = (txt * n_img + (img ^ side)) * block
            at = side * total + k * block
            here = jnp.logical_and(lane >= at, lane < at + block)
            found = jnp.where(here, first_id - at + lane, found)
    ids[...] = found
    step = 16 * (rows // 48)
    while rows % step or outs[0].shape[0] % step:
        step -= 16
    for at in range(0, total, step):
        ref = half if at < rows else other
        full = ref[pl.ds(at % rows, step), :].astype(f32)
        inv = lax.rsqrt(jnp.sum(full * full, axis=1, keepdims=True) + eps)
        size = outs[0].shape[0]
        unit = (full * inv).astype(bf16)
        whole[pl.ds(at, step), :] = unit
        outs[at // size][pl.ds(at % size, step), :] = unit


def batch_body(first, order, n_txt, place, scale_ref, bias_ref, images, weight, txt_own, txt_sib, col_ids, *refs):
    if first:
        d_hidden_ref, own_ref, sib_ref, hidden_ref, unit_ref, grad_ref = refs
    else:
        own_in, sib_in, d_hidden_ref, own_ref, sib_ref, hidden_ref, unit_ref, grad_ref = refs
    scale, bias = scale_ref[0:1, 0:1], bias_ref[0:1, 0:1]
    block = own_ref.shape[0]
    hidden = dot(images[...], weight[...])
    inv = lax.rsqrt(jnp.sum(hidden * hidden, axis=1, keepdims=True) + eps)
    hidden_ref[...] = hidden
    unit_ref[...] = (hidden * inv).astype(bf16)
    ids = []
    for entry in order:
        img, txt = source(place, 0, entry)
        within = lax.broadcasted_iota(jnp.int32, (block, 1), 0)
        ids.append((img * n_txt + txt) * block + within)
    ids = jnp.concatenate(ids, axis=0)
    total = txt_own.shape[0]
    width = 256 if total % 256 == 0 else total
    for side, txt in enumerate((txt_own, txt_sib)):
        for at in range(0, total, width):
            columns = pl.ds(side * total + at, width)
            logits = scale * dot(unit_ref[...], txt[pl.ds(at, width), :], NT) + bias
            flip = jnp.where(ids == col_ids[:, columns], -1.0, 1.0)
            grad_ref[:, columns] = (flip * jax.nn.sigmoid(flip * logits)).astype(bf16)
    edge = 64
    both = jnp.concatenate([grad_ref[:, pl.ds(at, edge)] for at in (0, total)], axis=1)
    terms = dot(both, unit_ref[...], TN)
    for at, ref in ((0, own_ref), (edge, sib_ref)):
        ref[...] = terms[at : at + block, :]
    if not first:
        own_ref[...] += own_in[...]
        sib_ref[...] += sib_in[...]
    d_img = dot(grad_ref[:, pl.ds(0, total)], txt_own[...])
    d_img = scale * (d_img + dot(grad_ref[:, pl.ds(total, total)], txt_sib[...]))
    hidden = hidden_ref[...]
    inner = jnp.sum(hidden * d_img, axis=1, keepdims=True)
    d_hidden_ref[...] = (inv * (d_img - hidden * (inv * inv * inner))).astype(bf16)


def begin_body(log_scale, logit_bias, texts, images, _, texts_out, images_out, scale, bias):
    scale[...] = jnp.exp(jnp.full(scale.shape, log_scale[0], f32))
    bias[...] = jnp.full(bias.shape, logit_bias[0], f32)
    texts_out[...] = texts[...]
    images_out[...] = images[...]


def join_body(*refs):
    out, at = refs[-1], 0
    for ref in refs[:-1]:
        out[pl.ds(at, ref.shape[0]), :] = ref[...]
        at += ref.shape[0]


def head_early_body(count, weight, *refs):
    images, d_hidden, (out, grads) = refs[:count], refs[count:-2], refs[-2:]
    left = jnp.concatenate([ref[...] for ref in images], axis=0)
    right = jnp.concatenate([ref[...] for ref in d_hidden], axis=0)
    out[...] = dot(left, right, TN)
    mine = d_hidden[0][pl.ds(0, grads.shape[0]), :]
    grads[...] = dot(weight[...], mine, NT).T.astype(bf16)


def last_body(count, d_count, sizes, scale, texts, own, received, *refs):
    images, d_hidden = refs[:count], refs[count : count + d_count]
    before, out, text_out, held, text_held, sems = refs[count + d_count :]
    right = jnp.concatenate([ref[...] for ref in d_hidden], axis=0)
    copies = []
    first = 0
    for k, size in enumerate(sizes):
        at = pl.ds(first, size)
        first += size
        left = jnp.concatenate([ref[:, at] for ref in images], axis=0)
        held[at, :] = before[at, :] + dot(left, right, TN)
        copies.append(pltpu.make_async_copy(held.at[at, :], out.at[at, :], sems.at[k]))
        copies[-1].start()
    full = texts[...].astype(f32)
    inv = lax.rsqrt(jnp.sum(full * full, axis=1, keepdims=True) + eps)
    d_txt = scale[0:1, 0:1] * (own[...] + received[...])
    inner = jnp.sum(full * d_txt, axis=1, keepdims=True)
    text_held[...] = (inv * (d_txt - full * (inv * inv * inner))).astype(bf16)
    copies.append(pltpu.make_async_copy(text_held, text_out, sems.at[len(sizes)]))
    copies[-1].start()
    for copy in copies:
        copy.wait()


def gathered(n_img, n_txt, images, texts, head_weight, log_scale, logit_bias):
    rows, emb = images.shape
    features = texts.shape[1]
    img_at, txt_at = lax.axis_index("img"), lax.axis_index("txt")

    def move(array, axis, mask):
        size = n_img if axis == "img" else n_txt
        return lax.ppermute(array, axis, [(i, i ^ mask) for i in range(size)])

    core = functools.partial(move, axis="img", mask=1)

    def link(array, second):
        pairs = []
        for i in range(n_img):
            for t in range(n_txt):
                to = (i ^ 2) * n_txt + t if (i % 2 == 0) != second else i * n_txt + (t ^ 1)
                pairs.append((i * n_txt + t, to))
        return lax.ppermute(array, ("img", "txt"), pairs)

    def over_z(block):
        return [move(block, "txt", mask) for mask in (2, 4, 6)]

    def shape(count, like):
        return jax.ShapeDtypeStruct((count, like.shape[1]), bf16)

    def after(array, *others):
        return lax.optimization_barrier((array, *others))[0]

    def join(*parts, flops=0):
        count = sum(part.shape[0] for part in parts)
        return call(join_body, shape(count, parts[0]), [VMEM] * len(parts), flops)(*parts)

    far = range(2, n_txt, 2)
    both = ((0, 0), (1, 0), (0, 1), (1, 1))
    order = [(z, *over) for over in both for z in (0, *far)]
    early_order = [(0, *over) for over in both] + [(z, *over) for over in both[:2] for z in far]
    late_order = [(z, *over) for over in both[2:] for z in far]
    total = len(order) * rows
    split = len(early_order) * rows
    first = 2 - lax.rem(img_at, 2)
    place = jnp.stack([img_at, txt_at, first, 3 - first]).astype(jnp.int32)
    txt_z = over_z(texts)
    vector = jax.ShapeDtypeStruct((1, 128), f32)
    txt_own_block, img_own_block, scale, bias = call(
        begin_body,
        [shape(rows, texts), shape(rows, images), vector, vector],
        [SMEM, SMEM, VMEM, VMEM, ANY],
        0,
    )(log_scale, logit_bias, texts, images, txt_z[0])
    img_near = link(images, False)
    img_z = over_z(after(images, txt_z[0]))
    four = join(txt_own_block, *txt_z[:2], after(txt_z[2], img_near))
    got = link(four, False)
    two = join(img_own_block, img_near)
    img_two = link(two, True)
    half = join(four, after(got, img_two))
    got = link(half, True)
    third = total // 3
    *txt_parts, txt_own, col_ids = call(
        functools.partial(unit_body, order, n_img),
        [shape(third, texts)] * 3 + [shape(total, texts), jax.ShapeDtypeStruct((1, 2 * total), jnp.int32)],
        [SMEM] + [VMEM] * 2,
        0,
    )(place, half, got)
    txt_sib = join(*[core(part) for part in txt_parts])
    three = join(*img_z[:2], img_z[2], flops=0)
    six = join(three, link(three, False))
    img_last = [link(six, True)]
    early = [join(two, img_two, six)]
    early_sib = [core(part) for part in early]

    def batch(images, order, cost, before):
        held = images.shape[0]
        term = jax.ShapeDtypeStruct((rows, features), f32)
        return call(
            functools.partial(batch_body, not before, order, n_txt),
            [shape(held, texts), term, term],
            [SMEM] + [VMEM] * (7 + len(before)),
            cost,
            [
                pltpu.VMEM((held, features), f32),
                pltpu.VMEM((held, features), bf16),
                pltpu.VMEM((held, 2 * total), bf16),
            ],
        )(place, scale, bias, images, head_weight, txt_own, txt_sib, col_ids, *before)

    d_early, own, sib = batch(early[0], early_order, 3_000_000_000, [])
    d_early_sib = core(d_early)
    late_sib = [core(after(part, d_early)) for part in img_last]
    d_late, own, sib = batch(img_last[0], late_order, 6_000_000_000, [own, sib])
    d_late_sib = core(d_late)
    received = core(sib)

    left = early + early_sib
    right = [d_early, d_early_sib]
    head = jax.ShapeDtypeStruct((emb, features), f32)
    before, image_grads = call(
        functools.partial(head_early_body, len(left)),
        [head, shape(rows, images)],
        [VMEM] * (1 + len(left) + len(right)),
        0,
    )(head_weight, *left, *right)
    left = img_last + late_sib
    right = [d_late, d_late_sib]
    sizes = [256, 384, emb - 640] if emb % 128 == 0 and emb > 640 else [emb]
    head_grad, text_grads = pl.pallas_call(
        functools.partial(last_body, len(left), len(right), sizes),
        out_shape=[head, shape(rows, texts)],
        in_specs=[VMEM] * (len(left) + len(right) + 5),
        out_specs=[ANY, ANY],
        scratch_shapes=[
            pltpu.VMEM(head.shape, f32),
            pltpu.VMEM(texts.shape, bf16),
            pltpu.SemaphoreType.DMA((len(sizes) + 1,)),
        ],
        compiler_params=pltpu.CompilerParams(vmem_limit_bytes=LIMIT),
        cost_estimate=pl.CostEstimate(flops=0, bytes_accessed=0, transcendentals=0),
    )(scale, txt_own_block, own, received, *left, *right, before)
    return image_grads, text_grads, head_grad


def blocked(images, texts, head_weight, log_scale, logit_bias):
    scale = jnp.exp(log_scale[0])
    bias = logit_bias[0]
    hidden = jnp.dot(images, head_weight, preferred_element_type=f32)
    img_inv = lax.rsqrt(jnp.sum(hidden * hidden, axis=1, keepdims=True) + eps)
    img_unit = (hidden * img_inv).astype(bf16)
    txt_full = texts.astype(f32)
    txt_inv = lax.rsqrt(jnp.sum(txt_full * txt_full, axis=1, keepdims=True) + eps)
    txt_unit = (txt_full * txt_inv).astype(bf16)
    img_block = lax.all_gather(img_unit, "txt", axis=0, tiled=True)
    txt_block = lax.all_gather(txt_unit, "img", axis=0, tiled=True)
    total_rows = img_block.shape[0]
    total_cols = txt_block.shape[0]
    features = img_block.shape[1]
    row_first = lax.axis_index("img") * total_rows
    col_first = lax.axis_index("txt") * total_cols
    columns = col_first + jnp.arange(total_cols, dtype=jnp.int32)
    width = 512 if total_rows % 512 == 0 else total_rows
    count = total_rows // width
    blocks = img_block.reshape(count, width, features)

    def step(carry, inputs):
        block, index = inputs
        logits = scale * dot(block, txt_block, NT) + bias
        row_ids = row_first + index * width + jnp.arange(width, dtype=jnp.int32)
        label = jnp.where(row_ids[:, None] == columns[None, :], 1.0, -1.0).astype(f32)
        grad = (-label * jax.nn.sigmoid(-label * logits)).astype(bf16)
        d_rows = scale * dot(grad, txt_block)
        carry = carry + scale * dot(grad, block, TN)
        return (carry, d_rows)

    txt_terms, row_terms = lax.scan(
        step,
        jnp.zeros((total_cols, features), f32),
        (blocks, jnp.arange(count, dtype=jnp.int32)),
    )
    img_terms = row_terms.reshape(total_rows, features)
    d_img = lax.psum_scatter(
        img_terms.astype(bf16), "txt", scatter_dimension=0, tiled=True
    ).astype(f32)
    inner = jnp.sum(hidden * d_img, axis=1, keepdims=True)
    d_hidden = (img_inv * (d_img - hidden * img_inv * img_inv * inner)).astype(bf16)
    image_grads = dot(d_hidden, head_weight, NT).astype(bf16)
    head_grad = lax.psum(dot(images, d_hidden, TN), ("img", "txt"))
    d_txt = lax.psum_scatter(
        txt_terms.astype(bf16), "img", scatter_dimension=0, tiled=True
    ).astype(f32)
    inner_txt = jnp.sum(txt_full * d_txt, axis=1, keepdims=True)
    text_grads = (txt_inv * (d_txt - txt_full * txt_inv * txt_inv * inner_txt)).astype(bf16)
    return (image_grads, text_grads, head_grad)


def solution(mesh):
    n_img, n_txt = mesh.shape["img"], mesh.shape["txt"]

    def shards(images, texts, head_weight, log_scale, logit_bias):
        width = images.shape[1] + texts.shape[1]
        held = 2 * n_img * n_txt * images.shape[0] * width
        same = images.shape[0] == texts.shape[0]
        if (n_img, n_txt) == (4, 8) and same and held <= GATHER_BYTES:
            return gathered(n_img, n_txt, images, texts, head_weight, log_scale, logit_bias)
        return blocked(images, texts, head_weight, log_scale, logit_bias)

    return jax.shard_map(
        shards,
        mesh=mesh,
        in_specs=(P(("img", "txt"), None), P(("txt", "img"), None), P(), P(), P()),
        out_specs=(P(("img", "txt"), None), P(("txt", "img"), None), P()),
        check_vma=False,
    )
```

time: 290 us -> 55.9 us (0.19)
  waiting for transfers between devices: 216 us -> 16.5 us
  blocking collectives: 39 us -> 0 us
  starting transfers between devices: 0.12 us -> 19.4 us
  Pallas kernels: 0 us -> 16 us
  between operations: 15.3 us -> 2.04 us
  matrix products: 8.24 us -> 0 us
  other arithmetic: 5.41 us -> 0.08 us
  local copies, waits for them, and re-layouts: 4.75 us -> 1.73 us
    psum x1 -> x0, waiting for transfers between devices: 140 us -> none  [shards(): head_grad = lax.psum(head_term, ('img', 'txt'))]
    reduce_scatter x2 -> x0, waiting for transfers between devices: 76.4 us -> none  [the longest x1 59.1 us: shards(): lax.psum_scatter(img_terms.astype(jnp.bfloat16), 'txt', scatter_dimension...]
    all_gather x2 -> x0, blocking collectives: 39 us -> none  [the longest x1 31.9 us: shards(): img_block = lax.all_gather(img_unit, 'txt', axis=0, tiled=True)]
    ppermute x0 -> x20, starting transfers between devices: none -> 19.4 us  [the longest x14 10.6 us: move(): return lax.ppermute(array, axis, [(i, i ^ mask) for i in range(size)])]
    ppermute x0 -> x20, waiting for transfers between devices: none -> 16.5 us  [the longest x14 8.95 us: move(): return lax.ppermute(array, axis, [(i, i ^ mask) for i in range(size)])]
    pallas_call x0 -> x13, Pallas kernels: none -> 16 us  [the longest x2 8.97 us: batch(): call(functools.partial(batch_body, not before, order, n_txt), [shape(held...]
    dot_general x6 -> x0, matrix products: 8.24 us -> none  [the longest x1 3.08 us: shards(): lax.dot_general(images, d_hidden, (((0,), (0,)), ((), ())), preferred_ele...]
    unnamed x9 -> x6, local copies, waits for them, and re-layouts: 4.75 us -> 1.73 us
  transfers between devices with their start and end apart: 3 -> 20, of which waited for: 3 -> 10; matrix products, arithmetic and copies ran while one was open for 3% -> 0% of each run, Pallas kernels for 0% -> 24%
where the time goes in v2:
time: 55.9 us; the launch traced here: 55.7 us
  starting transfers between devices  19.4 us (35%)
  waiting for transfers between devices  16.5 us (30%)
  Pallas kernels  16 us (29%)
  between operations  2.04 us (4%)
  local copies, waits for them, and re-layouts  1.73 us (3%)
    ppermute x14, starting transfers between devices, move(): return lax.ppermute(array, axis, [(i, i ^ mask) for i in range(size)])  10.6 us
    pallas_call x2, Pallas kernels, batch(): call(functools.partial(batch_body, not before, order, n_txt), [shape(held...  8.97 us
    ppermute x14, waiting for transfers between devices, move(): return lax.ppermute(array, axis, [(i, i ^ mask) for i in range(size)])  8.95 us
    ppermute x6, starting transfers between devices, link(): return lax.ppermute(array, ('img', 'txt'), pairs)  8.85 us
    ppermute x6, waiting for transfers between devices, link(): return lax.ppermute(array, ('img', 'txt'), pairs)  7.5 us
    pallas_call x1, Pallas kernels, gathered(): call(functools.partial(head_early_body, len(left)), [head, shape(rows, im...  3.14 us
    pallas_call x1, Pallas kernels, gathered(): pl.pallas_call(functools.partial(last_body, len(left), len(right), sizes)...  2.71 us
    unnamed x6, local copies, waits for them, and re-layouts  1.73 us
  transfers between devices with their start and end apart: 20, of which 10 were waited for; matrix products, arithmetic and copies ran while one was open for 0% of the time, Pallas kernels for 24%

profile of v2, /device:TPU:0, one launch (start us, length us, event | category | flops | bytes accessed | tf_op | source)
XLA Modules:
  0.0 55.7 jit_solution(14762353235152199612)
XLA Ops:
  0.6 3.0 %collective-permute-start.1 = (bf16[48,1152]{1,0:T(8,128)(2,1)}, bf16[48,1152]{1,0:T(8,128)(2,1)S(1)}, u32[]{:S(2)}, u32[]{:S(2)}) collective-permute-start(bf16[48,1152]{1,0:T(8,128)(2,1)} %images.1), channel_id=1, source_target_pairs={{0,16},{1,17},{2,18},{3,19},{4,20},{5,21},{6,22},{7,23},{8,9},{9,8... | collective-permute-start | bytes 331784 | tf_op jit(solution)/shard_map/ppermute | solution.py:177
  3.6 1.6 %collective-permute-start = (bf16[48,640]{1,0:T(8,128)(2,1)}, bf16[48,640]{1,0:T(8,128)(2,1)S(1)}, u32[]{:S(2)}, u32[]{:S(2)}) collective-permute-start(bf16[48,640]{1,0:T(8,128)(2,1)} %texts.1), channel_id=1, source_target_pairs={{0,2},{1,3},{2,0},{3,1},{4,6},{5,7},{6,4},{7,5},{8,10},{9,11},{10,... | collective-permute-start | bytes 184328 | tf_op jit(solution)/shard_map/ppermute | solution.py:167
  5.2 2.5 %collective-permute-start.9 = (bf16[48,640]{1,0:T(8,128)(2,1)}, bf16[48,640]{1,0:T(8,128)(2,1)S(1)}, u32[]{:S(2)}, u32[]{:S(2)}) collective-permute-start(bf16[48,640]{1,0:T(8,128)(2,1)} %texts.1), channel_id=1, source_target_pairs={{0,6},{1,7},{2,4},{3,5},{4,2},{5,3},{6,0},{7,1},{8,14},{9,15},{10,... | collective-permute-start | bytes 184328 | tf_op jit(solution)/shard_map/ppermute | solution.py:167
  7.7 0.1 collective-permute-start.8
  9.1 0.0 collective-permute-done._.refs_1_
  9.1 0.0 copy-start.1
  9.1 0.9 %copy-done.1 = bf16[48,1152]{1,0:T(8,128)(2,1)S(1)} copy-done((bf16[48,1152]{1,0:T(8,128)(2,1)S(1)}, bf16[48,1152]{1,0:T(8,128)(2,1)}, u32[]{:S(2)}) %copy-start.1) | copy-done | bytes 110616
  10.0 0.8 %copy-done.2 = bf16[48,640]{1,0:T(8,128)(2,1)S(1)} copy-done((bf16[48,640]{1,0:T(8,128)(2,1)S(1)}, bf16[48,640]{1,0:T(8,128)(2,1)}, u32[]{:S(2)}) %copy-start.2) | copy-done | bytes 61464
  10.9 1.1 %collective-permute-done.9.refs_3_ = bf16[48,640]{1,0:T(8,128)(2,1)S(1)} collective-permute-done((bf16[48,640]{1,0:T(8,128)(2,1)}, bf16[48,640]{1,0:T(8,128)(2,1)S(1)}, u32[]{:S(2)}, u32[]{:S(2)}) %collective-permute-start.9) | collective-permute-done | bytes 61472 | tf_op jit(solution)/shard_map/ppermute | solution.py:167
  11.9 0.0 collective-permute-done.1.refs_1_
  12.0 1.9 %collective-permute-done.8.refs_2_ = bf16[48,640]{1,0:T(8,128)(2,1)S(1)} collective-permute-done((bf16[48,640]{1,0:T(8,128)(2,1)}, bf16[48,640]{1,0:T(8,128)(2,1)S(1)}, u32[]{:S(2)}, u32[]{:S(2)}) %collective-permute-start.8) | collective-permute-done | bytes 61472 | tf_op jit(solution)/shard_map/ppermute | solution.py:167
  13.8 1.2 %collective-permute-start.10 = (bf16[192,640]{1,0:T(8,128)(2,1)S(1)}, bf16[192,640]{1,0:T(8,128)(2,1)S(1)}, u32[]{:S(2)}, u32[]{:S(2)}) collective-permute-start(bf16[192,640]{1,0:T(8,128)(2,1)S(1)} %shard_map.81.refs_0_), channel_id=1, source_target_pairs={{0,16},{1,17},{2,18},{3,19},{4,20},{5,21},{6,22},{7,23},{8,9},{9,8... | collective-permute-start | bytes 737288 | tf_op jit(solution)/shard_map/ppermute | solution.py:177
  15.1 1.0 %collective-permute-start.2 = (bf16[96,1152]{1,0:T(8,128)(2,1)S(1)}, bf16[96,1152]{1,0:T(8,128)(2,1)S(1)}, u32[]{:S(2)}, u32[]{:S(2)}) collective-permute-start(bf16[96,1152]{1,0:T(8,128)(2,1)S(1)} %shard_map.77.refs_0_), channel_id=1, source_target_pairs={{0,1},{1,0},{2,3},{3,2},{4,5},{5,4},{6,7},{7,6},{8,24},{9,25},{10,... | collective-permute-start | bytes 663560 | tf_op jit(solution)/shard_map/ppermute | solution.py:177
  16.0 2.4 %collective-permute-start.5 = (bf16[48,1152]{1,0:T(8,128)(2,1)}, bf16[48,1152]{1,0:T(8,128)(2,1)S(1)}, u32[]{:S(2)}, u32[]{:S(2)}) collective-permute-start(bf16[48,1152]{1,0:T(8,128)(2,1)} %images.1), channel_id=1, source_target_pairs={{0,6},{1,7},{2,4},{3,5},{4,2},{5,3},{6,0},{7,1},{8,14},{9,15},{10,... | collective-permute-start | bytes 331784 | tf_op jit(solution)/shard_map/ppermute | solution.py:167
  18.4 0.0 collective-permute-start.4
  18.4 2.0 %collective-permute-start.3 = (bf16[48,1152]{1,0:T(8,128)(2,1)}, bf16[48,1152]{1,0:T(8,128)(2,1)S(1)}, u32[]{:S(2)}, u32[]{:S(2)}) collective-permute-start(bf16[48,1152]{1,0:T(8,128)(2,1)} %images.1), channel_id=1, source_target_pairs={{0,2},{1,3},{2,0},{3,1},{4,6},{5,7},{6,4},{7,5},{8,10},{9,11},{10,... | collective-permute-start | bytes 331784 | tf_op jit(solution)/shard_map/ppermute | solution.py:167
  20.4 0.7 %collective-permute-done.2.refs_1_ = bf16[96,1152]{1,0:T(8,128)(2,1)S(1)} collective-permute-done((bf16[96,1152]{1,0:T(8,128)(2,1)S(1)}, bf16[96,1152]{1,0:T(8,128)(2,1)S(1)}, u32[]{:S(2)}, u32[]{:S(2)}) %collective-permute-start.2) | collective-permute-done | bytes 221216 | tf_op jit(solution)/shard_map/ppermute | solution.py:177
  21.1 0.0 collective-permute-done.10.refs_1_
  21.1 1.8 %collective-permute-start.11 = (bf16[384,640]{1,0:T(8,128)(2,1)S(1)}, bf16[384,640]{1,0:T(8,128)(2,1)S(1)}, u32[]{:S(2)}, u32[]{:S(2)}) collective-permute-start(bf16[384,640]{1,0:T(8,128)(2,1)S(1)} %shard_map.82.half), channel_id=1, source_target_pairs={{0,1},{1,0},{2,3},{3,2},{4,5},{5,4},{6,7},{7,6},{8,24},{9,25},{10,... | collective-permute-start | bytes 1474568 | tf_op jit(solution)/shard_map/ppermute | solution.py:177
  22.9 1.1 %collective-permute-done.5.refs_2_ = bf16[48,1152]{1,0:T(8,128)(2,1)S(1)} collective-permute-done((bf16[48,1152]{1,0:T(8,128)(2,1)}, bf16[48,1152]{1,0:T(8,128)(2,1)S(1)}, u32[]{:S(2)}, u32[]{:S(2)}) %collective-permute-start.5) | collective-permute-done | bytes 110624 | tf_op jit(solution)/shard_map/ppermute | solution.py:167
  24.0 3.5 %collective-permute-done.4.refs_1_ = bf16[48,1152]{1,0:T(8,128)(2,1)S(1)} collective-permute-done((bf16[48,1152]{1,0:T(8,128)(2,1)}, bf16[48,1152]{1,0:T(8,128)(2,1)S(1)}, u32[]{:S(2)}, u32[]{:S(2)}) %collective-permute-start.4) | collective-permute-done | bytes 110624 | tf_op jit(solution)/shard_map/ppermute | solution.py:167
  27.6 0.7 %collective-permute-start.6 = (bf16[144,1152]{1,0:T(8,128)(2,1)S(1)}, bf16[144,1152]{1,0:T(8,128)(2,1)S(1)}, u32[]{:S(2)}, u32[]{:S(2)}) collective-permute-start(bf16[144,1152]{1,0:T(8,128)(2,1)S(1)} %shard_map.78.refs_0_), channel_id=1, source_target_pairs={{0,16},{1,17},{2,18},{3,19},{4,20},{5,21},{6,22},{7,23},{8,9},{9,8... | collective-permute-start | bytes 995336 | tf_op jit(solution)/shard_map/ppermute | solution.py:177
  28.3 6.4 %collective-permute-done.6.refs_1_ = bf16[144,1152]{1,0:T(8,128)(2,1)S(1)} collective-permute-done((bf16[144,1152]{1,0:T(8,128)(2,1)S(1)}, bf16[144,1152]{1,0:T(8,128)(2,1)S(1)}, u32[]{:S(2)}, u32[]{:S(2)}) %collective-permute-start.6) | collective-permute-done | bytes 331808 | tf_op jit(solution)/shard_map/ppermute | solution.py:177
  34.8 1.1 %collective-permute-start.16 = (bf16[288,1152]{1,0:T(8,128)(2,1)S(1)}, bf16[288,1152]{1,0:T(8,128)(2,1)S(1)}, u32[]{:S(2)}, u32[]{:S(2)}) collective-permute-start(bf16[288,1152]{1,0:T(8,128)(2,1)S(1)} %shard_map.79.refs_2_), channel_id=1, source_target_pairs={{0,1},{1,0},{2,3},{3,2},{4,5},{5,4},{6,7},{7,6},{8,24},{9,25},{10,... | collective-permute-start | bytes 1990664 | tf_op jit(solution)/shard_map/ppermute | solution.py:177
  35.9 0.1 pad_add_fusion.place
  36.0 0.0 collective-permute-done.11.other
  36.0 0.9 %shard_map.83 = (bf16[256,640]{1,0:T(8,128)(2,1)S(1)}, bf16[256,640]{1,0:T(8,128)(2,1)S(1)}, bf16[256,640]{1,0:T(8,128)(2,1)S(1)}, bf16[768,640]{1,0:T(8,128)(2,1)S(1)}, s32[1,1536]{1,0:T(1,128)S(1)}) custom-call(s32[4]{0:T(128)S(1)} %pad_add_fusion.place, bf16[384,640]{1,0:T(8,128)(2,1)S(1)} %shard_map.82.half, ...), custom_call_target="tpu_custom_call" | custom-call | tf_op jit(solution)/shard_map/pallas_call | solution.py:218
  36.9 0.1 collective-permute-start.12
  37.0 0.5 collective-permute-start.13
  37.5 0.1 collective-permute-start.14
  37.6 0.1 shard_map.80.images.refs_0_
  37.7 0.0 copy-start
  37.7 0.5 collective-permute-start.7
  38.2 0.4 collective-permute-done.12.refs_0_
  38.6 0.5 collective-permute-done.13.refs_1_
  39.1 0.5 collective-permute-done.14.refs_2_
  39.6 0.1 shard_map.84.txt_sib
  39.7 5.3 %shard_map.85 = (bf16[480,640]{1,0:T(8,128)(2,1)S(1)}, f32[48,640]{1,0:T(8,128)S(1)}, f32[48,640]{1,0:T(8,128)S(1)}) custom-call(s32[4]{0:T(128)S(1)} %pad_add_fusion.place, f32[1,128]{1,0:T(1,128)S(1)} %get-tuple-element.28.scale_ref.scale, f32[1,128]{1,0:T(1,128)S(1)} %get-tuple-element.29.bias_ref, bf16[480,1152]{1,0:T(8,128)(2,1)S(1)} %shard_map.80.images.refs_0_, ...), custom_call_target="tpu_custom_call" | custom-call | flops 3000000000 | tf_op jit(solution)/shard_map/pallas_call | solution.py:234
  45.0 0.2 collective-permute-start.15
  45.2 0.4 collective-permute-done.16.images.refs_0_
  45.5 0.0 collective-permute-start.18
  45.6 3.7 %shard_map.87 = (bf16[288,640]{1,0:T(8,128)(2,1)S(1)}, f32[48,640]{1,0:T(8,128)S(1)}, f32[48,640]{1,0:T(8,128)S(1)}) custom-call(s32[4]{0:T(128)S(1)} %pad_add_fusion.place, f32[1,128]{1,0:T(1,128)S(1)} %get-tuple-element.28.scale_ref.scale, f32[1,128]{1,0:T(1,128)S(1)} %get-tuple-element.29.bias_ref, ...), custom_call_target="tpu_custom_call" | custom-call | flops 6000000000 | tf_op jit(solution)/shard_map/pallas_call | solution.py:234
  49.2 0.6 %collective-permute-start.19 = (bf16[288,640]{1,0:T(8,128)(2,1)S(1)}, bf16[288,640]{1,0:T(8,128)(2,1)S(1)}, u32[]{:S(2)}, u32[]{:S(2)}) collective-permute-start(bf16[288,640]{1,0:T(8,128)(2,1)S(1)} %get-tuple-element.45.refs_2_), channel_id=1, source_target_pairs={{0,8},{8,0},{16,24},{24,16},{1,9},{9,1},{17,25},{25,17},{2,10},{10... | collective-permute-start | bytes 1105928 | tf_op jit(solution)/shard_map/ppermute | solution.py:167
  49.8 0.1 collective-permute-start.17
  49.9 0.0 collective-permute-done.7.refs_1_
  49.9 0.0 collective-permute-done.15.refs_3_
  49.9 3.1 %shard_map.86 = (f32[1152,640]{1,0:T(8,128)S(1)}, bf16[48,1152]{1,0:T(8,128)(2,1)}) custom-call(bf16[1152,640]{1,0:T(8,128)(2,1)S(1)} %copy-done, bf16[480,1152]{1,0:T(8,128)(2,1)S(1)} %shard_map.80.images.refs_0_, bf16[480,1152]{1,0:T(8,128)(2,1)S(1)} %collective-permute-done.7.refs_1_, bf16[480,640]{1,0:T(8,128)(2,1)S(1)} %get-tuple-element.38.refs_2_, ...), custom_call_target="tpu_custom_call" | custom-call | tf_op jit(solution)/shard_map/pallas_call | solution.py:256
  53.0 2.7 %shard_map.88 = (f32[1152,640]{1,0:T(8,128)}, bf16[48,640]{1,0:T(8,128)(2,1)}) custom-call(f32[1,128]{1,0:T(1,128)S(1)} %get-tuple-element.28.scale_ref.scale, bf16[48,640]{1,0:T(8,128)(2,1)S(1)} %get-tuple-element.30.refs_0_.texts, f32[48,640]{1,0:T(8,128)S(1)} %get-tuple-element.42.own, f32[48,640]{1,0:T(8,128)S(1)} %collective-permute-done.17.received, ...), custom_call_target="tpu_custom_call" | custom-call | tf_op jit(solution)/shard_map/pallas_call | solution.py:265
  (12 shorter events, 0.2 us)
Async XLA Ops:
  0.6 11.3 %collective-permute-start.1 = (bf16[48,1152]{1,0:T(8,128)(2,1)}, bf16[48,1152]{1,0:T(8,128)(2,1)S(1)}, u32[]{:S(2)}, u32[]{:S(2)}) collective-permute-start(bf16[48,1152]{1,0:T(8,128)(2,1)} %images.1), channel_id=1, source_target_pairs={{0,16},{1,17},{2,18},{3,19},{4,20},{5,21},{6,22},{7,23},{8,9},{9,8... | collective-permute-start | bytes 331784 | tf_op jit(solution)/shard_map/ppermute | solution.py:177
  3.6 5.5 %collective-permute-start = (bf16[48,640]{1,0:T(8,128)(2,1)}, bf16[48,640]{1,0:T(8,128)(2,1)S(1)}, u32[]{:S(2)}, u32[]{:S(2)}) collective-permute-start(bf16[48,640]{1,0:T(8,128)(2,1)} %texts.1), channel_id=1, source_target_pairs={{0,2},{1,3},{2,0},{3,1},{4,6},{5,7},{6,4},{7,5},{8,10},{9,11},{10,... | collective-permute-start | bytes 184328 | tf_op jit(solution)/shard_map/ppermute | solution.py:167
  5.2 6.7 %collective-permute-start.9 = (bf16[48,640]{1,0:T(8,128)(2,1)}, bf16[48,640]{1,0:T(8,128)(2,1)S(1)}, u32[]{:S(2)}, u32[]{:S(2)}) collective-permute-start(bf16[48,640]{1,0:T(8,128)(2,1)} %texts.1), channel_id=1, source_target_pairs={{0,6},{1,7},{2,4},{3,5},{4,2},{5,3},{6,0},{7,1},{8,14},{9,15},{10,... | collective-permute-start | bytes 184328 | tf_op jit(solution)/shard_map/ppermute | solution.py:167
  7.7 6.1 %collective-permute-start.8 = (bf16[48,640]{1,0:T(8,128)(2,1)}, bf16[48,640]{1,0:T(8,128)(2,1)S(1)}, u32[]{:S(2)}, u32[]{:S(2)}) collective-permute-start(bf16[48,640]{1,0:T(8,128)(2,1)} %texts.1), channel_id=1, source_target_pairs={{0,4},{1,5},{2,6},{3,7},{4,0},{5,1},{6,2},{7,3},{8,12},{9,13},{10,... | collective-permute-start | bytes 184328 | tf_op jit(solution)/shard_map/ppermute | solution.py:167
  9.1 0.9 %copy-start.1 = (bf16[48,1152]{1,0:T(8,128)(2,1)S(1)}, bf16[48,1152]{1,0:T(8,128)(2,1)}, u32[]{:S(2)}) copy-start(bf16[48,1152]{1,0:T(8,128)(2,1)} %images.1) | copy-start | bytes 331780
  10.0 0.8 %copy-start.2 = (bf16[48,640]{1,0:T(8,128)(2,1)S(1)}, bf16[48,640]{1,0:T(8,128)(2,1)}, u32[]{:S(2)}) copy-start(bf16[48,640]{1,0:T(8,128)(2,1)} %texts.1) | copy-start | bytes 184324
  13.8 7.3 %collective-permute-start.10 = (bf16[192,640]{1,0:T(8,128)(2,1)S(1)}, bf16[192,640]{1,0:T(8,128)(2,1)S(1)}, u32[]{:S(2)}, u32[]{:S(2)}) collective-permute-start(bf16[192,640]{1,0:T(8,128)(2,1)S(1)} %shard_map.81.refs_0_), channel_id=1, source_target_pairs={{0,16},{1,17},{2,18},{3,19},{4,20},{5,21},{6,22},{7,23},{8,9},{9,8... | collective-permute-start | bytes 737288 | tf_op jit(solution)/shard_map/ppermute | solution.py:177
  15.1 6.0 %collective-permute-start.2 = (bf16[96,1152]{1,0:T(8,128)(2,1)S(1)}, bf16[96,1152]{1,0:T(8,128)(2,1)S(1)}, u32[]{:S(2)}, u32[]{:S(2)}) collective-permute-start(bf16[96,1152]{1,0:T(8,128)(2,1)S(1)} %shard_map.77.refs_0_), channel_id=1, source_target_pairs={{0,1},{1,0},{2,3},{3,2},{4,5},{5,4},{6,7},{7,6},{8,24},{9,25},{10,... | collective-permute-start | bytes 663560 | tf_op jit(solution)/shard_map/ppermute | solution.py:177
  16.0 8.0 %collective-permute-start.5 = (bf16[48,1152]{1,0:T(8,128)(2,1)}, bf16[48,1152]{1,0:T(8,128)(2,1)S(1)}, u32[]{:S(2)}, u32[]{:S(2)}) collective-permute-start(bf16[48,1152]{1,0:T(8,128)(2,1)} %images.1), channel_id=1, source_target_pairs={{0,6},{1,7},{2,4},{3,5},{4,2},{5,3},{6,0},{7,1},{8,14},{9,15},{10,... | collective-permute-start | bytes 331784 | tf_op jit(solution)/shard_map/ppermute | solution.py:167
  18.4 9.2 %collective-permute-start.4 = (bf16[48,1152]{1,0:T(8,128)(2,1)}, bf16[48,1152]{1,0:T(8,128)(2,1)S(1)}, u32[]{:S(2)}, u32[]{:S(2)}) collective-permute-start(bf16[48,1152]{1,0:T(8,128)(2,1)} %images.1), channel_id=1, source_target_pairs={{0,4},{1,5},{2,6},{3,7},{4,0},{5,1},{6,2},{7,3},{8,12},{9,13},{10,... | collective-permute-start | bytes 331784 | tf_op jit(solution)/shard_map/ppermute | solution.py:167
  18.4 9.2 %collective-permute-start.3 = (bf16[48,1152]{1,0:T(8,128)(2,1)}, bf16[48,1152]{1,0:T(8,128)(2,1)S(1)}, u32[]{:S(2)}, u32[]{:S(2)}) collective-permute-start(bf16[48,1152]{1,0:T(8,128)(2,1)} %images.1), channel_id=1, source_target_pairs={{0,2},{1,3},{2,0},{3,1},{4,6},{5,7},{6,4},{7,5},{8,10},{9,11},{10,... | collective-permute-start | bytes 331784 | tf_op jit(solution)/shard_map/ppermute | solution.py:167
  21.1 14.9 %collective-permute-start.11 = (bf16[384,640]{1,0:T(8,128)(2,1)S(1)}, bf16[384,640]{1,0:T(8,128)(2,1)S(1)}, u32[]{:S(2)}, u32[]{:S(2)}) collective-permute-start(bf16[384,640]{1,0:T(8,128)(2,1)S(1)} %shard_map.82.half), channel_id=1, source_target_pairs={{0,1},{1,0},{2,3},{3,2},{4,5},{5,4},{6,7},{7,6},{8,24},{9,25},{10,... | collective-permute-start | bytes 1474568 | tf_op jit(solution)/shard_map/ppermute | solution.py:177
  27.6 7.2 %collective-permute-start.6 = (bf16[144,1152]{1,0:T(8,128)(2,1)S(1)}, bf16[144,1152]{1,0:T(8,128)(2,1)S(1)}, u32[]{:S(2)}, u32[]{:S(2)}) collective-permute-start(bf16[144,1152]{1,0:T(8,128)(2,1)S(1)} %shard_map.78.refs_0_), channel_id=1, source_target_pairs={{0,16},{1,17},{2,18},{3,19},{4,20},{5,21},{6,22},{7,23},{8,9},{9,8... | collective-permute-start | bytes 995336 | tf_op jit(solution)/shard_map/ppermute | solution.py:177
  34.8 10.7 %collective-permute-start.16 = (bf16[288,1152]{1,0:T(8,128)(2,1)S(1)}, bf16[288,1152]{1,0:T(8,128)(2,1)S(1)}, u32[]{:S(2)}, u32[]{:S(2)}) collective-permute-start(bf16[288,1152]{1,0:T(8,128)(2,1)S(1)} %shard_map.79.refs_2_), channel_id=1, source_target_pairs={{0,1},{1,0},{2,3},{3,2},{4,5},{5,4},{6,7},{7,6},{8,24},{9,25},{10,... | collective-permute-start | bytes 1990664 | tf_op jit(solution)/shard_map/ppermute | solution.py:177
  36.9 1.7 %collective-permute-start.12 = (bf16[256,640]{1,0:T(8,128)(2,1)S(1)}, bf16[256,640]{1,0:T(8,128)(2,1)S(1)}, u32[]{:S(2)}, u32[]{:S(2)}) collective-permute-start(bf16[256,640]{1,0:T(8,128)(2,1)S(1)} %get-tuple-element.34), channel_id=1, source_target_pairs={{0,8},{8,0},{16,24},{24,16},{1,9},{9,1},{17,25},{25,17},{2,10},{10... | collective-permute-start | bytes 983048 | tf_op jit(solution)/shard_map/ppermute | solution.py:167
  37.0 2.1 %collective-permute-start.13 = (bf16[256,640]{1,0:T(8,128)(2,1)S(1)}, bf16[256,640]{1,0:T(8,128)(2,1)S(1)}, u32[]{:S(2)}, u32[]{:S(2)}) collective-permute-start(bf16[256,640]{1,0:T(8,128)(2,1)S(1)} %get-tuple-element.35), channel_id=1, source_target_pairs={{0,8},{8,0},{16,24},{24,16},{1,9},{9,1},{17,25},{25,17},{2,10},{10... | collective-permute-start | bytes 983048 | tf_op jit(solution)/shard_map/ppermute | solution.py:167
  37.5 2.1 %collective-permute-start.14 = (bf16[256,640]{1,0:T(8,128)(2,1)S(1)}, bf16[256,640]{1,0:T(8,128)(2,1)S(1)}, u32[]{:S(2)}, u32[]{:S(2)}) collective-permute-start(bf16[256,640]{1,0:T(8,128)(2,1)S(1)} %get-tuple-element.36), channel_id=1, source_target_pairs={{0,8},{8,0},{16,24},{24,16},{1,9},{9,1},{17,25},{25,17},{2,10},{10... | collective-permute-start | bytes 983048 | tf_op jit(solution)/shard_map/ppermute | solution.py:167
  37.7 2.0 %copy-start = (bf16[1152,640]{1,0:T(8,128)(2,1)S(1)}, bf16[1152,640]{1,0:T(8,128)(2,1)}, u32[]{:S(2)}) copy-start(bf16[1152,640]{1,0:T(8,128)(2,1)} %weight.5) | copy-start | bytes 4423684
  37.7 12.2 %collective-permute-start.7 = (bf16[480,1152]{1,0:T(8,128)(2,1)S(1)}, bf16[480,1152]{1,0:T(8,128)(2,1)S(1)}, u32[]{:S(2)}, u32[]{:S(2)}) collective-permute-start(bf16[480,1152]{1,0:T(8,128)(2,1)S(1)} %shard_map.80.images.refs_0_), channel_id=1, source_target_pairs={{0,8},{8,0},{16,24},{24,16},{1,9},{9,1},{17,25},{25,17},{2,10},{10... | collective-permute-start | bytes 3317768 | tf_op jit(solution)/shard_map/ppermute | solution.py:167
  45.0 4.9 %collective-permute-start.15 = (bf16[480,640]{1,0:T(8,128)(2,1)S(1)}, bf16[480,640]{1,0:T(8,128)(2,1)S(1)}, u32[]{:S(2)}, u32[]{:S(2)}) collective-permute-start(bf16[480,640]{1,0:T(8,128)(2,1)S(1)} %get-tuple-element.38.refs_2_), channel_id=1, source_target_pairs={{0,8},{8,0},{16,24},{24,16},{1,9},{9,1},{17,25},{25,17},{2,10},{10... | collective-permute-start | bytes 1843208 | tf_op jit(solution)/shard_map/ppermute | solution.py:167
  45.5 7.5 %collective-permute-start.18 = (bf16[288,1152]{1,0:T(8,128)(2,1)S(1)}, bf16[288,1152]{1,0:T(8,128)(2,1)S(1)}, u32[]{:S(2)}, u32[]{:S(2)}) collective-permute-start(bf16[288,1152]{1,0:T(8,128)(2,1)S(1)} %collective-permute-done.16.images.refs_0_), channel_id=1, source_target_pairs={{0,8},{8,0},{16,24},{24,16},{1,9},{9,1},{17,25},{25,17},{2,10},{10... | collective-permute-start | bytes 1990664 | tf_op jit(solution)/shard_map/ppermute | solution.py:167
  49.2 3.8 %collective-permute-start.19 = (bf16[288,640]{1,0:T(8,128)(2,1)S(1)}, bf16[288,640]{1,0:T(8,128)(2,1)S(1)}, u32[]{:S(2)}, u32[]{:S(2)}) collective-permute-start(bf16[288,640]{1,0:T(8,128)(2,1)S(1)} %get-tuple-element.45.refs_2_), channel_id=1, source_target_pairs={{0,8},{8,0},{16,24},{24,16},{1,9},{9,1},{17,25},{25,17},{2,10},{10... | collective-permute-start | bytes 1105928 | tf_op jit(solution)/shard_map/ppermute | solution.py:167
  49.8 3.2 %collective-permute-start.17 = (f32[48,640]{1,0:T(8,128)S(1)}, f32[48,640]{1,0:T(8,128)S(1)}, u32[]{:S(2)}, u32[]{:S(2)}) collective-permute-start(f32[48,640]{1,0:T(8,128)S(1)} %get-tuple-element.43), channel_id=1, source_target_pairs={{0,8},{8,0},{16,24},{24,16},{1,9},{9,1},{17,25},{25,17},{2,10},{10... | collective-permute-start | bytes 368648 | tf_op jit(solution)/shard_map/ppermute | solution.py:167

commit v3 on v2

--- a/solution.py
+++ b/solution.py
@@ -42,11 +42,10 @@
     return place[0] ^ (2 * (mask // 2)), place[1] ^ z ^ lax.rem(mask, 2)
 
 
-def unit_body(order, n_img, place, half, other, *outs):
-    outs, whole, ids = outs[:-2], outs[-2], outs[-1]
-    rows = half.shape[0]
-    block = 2 * rows // len(order)
-    total = 2 * rows
+def unit_body(order, n_img, place, *refs):
+    parts, sent, whole, ids = refs[:4], refs[4:-2], refs[-2], refs[-1]
+    total, rows = whole.shape[0], parts[0].shape[0]
+    block = total // len(order)
     lane = lax.broadcasted_iota(jnp.int32, ids.shape, 1)
     found = jnp.zeros(ids.shape, jnp.int32)
     for k, entry in enumerate(order):
@@ -57,17 +56,14 @@
             here = jnp.logical_and(lane >= at, lane < at + block)
             found = jnp.where(here, first_id - at + lane, found)
     ids[...] = found
-    step = 16 * (rows // 48)
-    while rows % step or outs[0].shape[0] % step:
-        step -= 16
+    size = sent[0].shape[0]
+    step = 64
     for at in range(0, total, step):
-        ref = half if at < rows else other
-        full = ref[pl.ds(at % rows, step), :].astype(f32)
+        full = parts[at // rows][pl.ds(at % rows, step), :].astype(f32)
         inv = lax.rsqrt(jnp.sum(full * full, axis=1, keepdims=True) + eps)
-        size = outs[0].shape[0]
         unit = (full * inv).astype(bf16)
         whole[pl.ds(at, step), :] = unit
-        outs[at // size][pl.ds(at % size, step), :] = unit
+        sent[at // size][pl.ds(at % size, step), :] = unit
 
 
 def batch_body(first, order, n_txt, place, scale_ref, bias_ref, images, weight, txt_own, txt_sib, col_ids, *refs):
@@ -117,6 +113,12 @@
     images_out[...] = images[...]
 
 
+def hold_body(array, _, out, sem):
+    copy = pltpu.make_async_copy(array, out, sem)
+    copy.start()
+    copy.wait()
+
+
 def join_body(*refs):
     out, at = refs[-1], 0
     for ref in refs[:-1]:
@@ -124,18 +126,16 @@
         at += ref.shape[0]
 
 
-def head_early_body(count, weight, *refs):
-    images, d_hidden, (out, grads) = refs[:count], refs[count:-2], refs[-2:]
+def head_early_body(count, *refs):
+    images, d_hidden, out = refs[:count], refs[count:-1], refs[-1]
     left = jnp.concatenate([ref[...] for ref in images], axis=0)
     right = jnp.concatenate([ref[...] for ref in d_hidden], axis=0)
     out[...] = dot(left, right, TN)
-    mine = d_hidden[0][pl.ds(0, grads.shape[0]), :]
-    grads[...] = dot(weight[...], mine, NT).T.astype(bf16)
-
-
-def last_body(count, d_count, sizes, scale, texts, own, received, *refs):
+
+
+def last_body(count, d_count, sizes, scale, texts, own, received, weight, mine, *refs):
     images, d_hidden = refs[:count], refs[count : count + d_count]
-    before, out, text_out, held, text_held, sems = refs[count + d_count :]
+    before, out, text_out, img_out, held, text_held, img_held, sems = refs[count + d_count :]
     right = jnp.concatenate([ref[...] for ref in d_hidden], axis=0)
     copies = []
     first = 0
@@ -152,6 +152,10 @@
     inner = jnp.sum(full * d_txt, axis=1, keepdims=True)
     text_held[...] = (inv * (d_txt - full * (inv * inv * inner))).astype(bf16)
     copies.append(pltpu.make_async_copy(text_held, text_out, sems.at[len(sizes)]))
+    copies[-1].start()
+    block = mine[pl.ds(0, img_held.shape[0]), :]
+    img_held[...] = dot(weight[...], block, NT).T.astype(bf16)
+    copies.append(pltpu.make_async_copy(img_held, img_out, sems.at[len(sizes) + 1]))
     copies[-1].start()
     for copy in copies:
         copy.wait()
@@ -209,23 +213,27 @@
     img_near = link(images, False)
     img_z = over_z(after(images, txt_z[0]))
     four = join(txt_own_block, *txt_z[:2], after(txt_z[2], img_near))
-    got = link(four, False)
+    near = link(four, False)
+    far = link(four, True)
     two = join(img_own_block, img_near)
     img_two = link(two, True)
-    half = join(four, after(got, img_two))
-    got = link(half, True)
+    txt_parts = [four, near, far, link(after(near, *(img_two,)), True)]
     third = total // 3
-    *txt_parts, txt_own, col_ids = call(
+    *sent, txt_own, col_ids = call(
         functools.partial(unit_body, order, n_img),
         [shape(third, texts)] * 3 + [shape(total, texts), jax.ShapeDtypeStruct((1, 2 * total), jnp.int32)],
-        [SMEM] + [VMEM] * 2,
+        [SMEM] + [VMEM] * len(txt_parts),
         0,
-    )(place, half, got)
-    txt_sib = join(*[core(part) for part in txt_parts])
-    three = join(*img_z[:2], img_z[2], flops=0)
-    six = join(three, link(three, False))
-    img_last = [link(six, True)]
-    early = [join(two, img_two, six)]
+    )(place, *txt_parts)
+    txt_sib = join(*[core(part) for part in sent])
+    weight = call(hold_body, jax.ShapeDtypeStruct(head_weight.shape, bf16), [ANY, ANY], 0, [
+        pltpu.SemaphoreType.DMA
+    ])(head_weight, img_two)
+    three = join(*img_z[:2], after(img_z[2], weight), flops=0)
+    near = link(three, False)
+    far = link(three, True)
+    early = [join(two, img_two, three, near)]
+    img_last = [join(far, link(after(near, *()), True))]
     early_sib = [core(part) for part in early]
 
     def batch(images, order, cost, before):
@@ -241,9 +249,9 @@
                 pltpu.VMEM((held, features), bf16),
                 pltpu.VMEM((held, 2 * total), bf16),
             ],
-        )(place, scale, bias, images, head_weight, txt_own, txt_sib, col_ids, *before)
-
-    d_early, own, sib = batch(early[0], early_order, 3_000_000_000, [])
+        )(place, scale, bias, images, weight, txt_own, txt_sib, col_ids, *before)
+
+    d_early, own, sib = batch(early[0], early_order, 1_400_000_000, [])
     d_early_sib = core(d_early)
     late_sib = [core(after(part, d_early)) for part in img_last]
     d_late, own, sib = batch(img_last[0], late_order, 6_000_000_000, [own, sib])
@@ -253,28 +261,29 @@
     left = early + early_sib
     right = [d_early, d_early_sib]
     head = jax.ShapeDtypeStruct((emb, features), f32)
-    before, image_grads = call(
+    before = call(
         functools.partial(head_early_body, len(left)),
-        [head, shape(rows, images)],
-        [VMEM] * (1 + len(left) + len(right)),
+        head,
+        [VMEM] * (len(left) + len(right)),
         0,
-    )(head_weight, *left, *right)
+    )(*left, *right)
     left = img_last + late_sib
     right = [d_late, d_late_sib]
     sizes = [256, 384, emb - 640] if emb % 128 == 0 and emb > 640 else [emb]
-    head_grad, text_grads = pl.pallas_call(
+    head_grad, text_grads, image_grads = pl.pallas_call(
         functools.partial(last_body, len(left), len(right), sizes),
-        out_shape=[head, shape(rows, texts)],
-        in_specs=[VMEM] * (len(left) + len(right) + 5),
-        out_specs=[ANY, ANY],
+        out_shape=[head, shape(rows, texts), shape(rows, images)],
+        in_specs=[VMEM] * (len(left) + len(right) + 7),
+        out_specs=[ANY] * 3,
         scratch_shapes=[
             pltpu.VMEM(head.shape, f32),
             pltpu.VMEM(texts.shape, bf16),
-            pltpu.SemaphoreType.DMA((len(sizes) + 1,)),
+            pltpu.VMEM(images.shape, bf16),
+            pltpu.SemaphoreType.DMA((len(sizes) + 2,)),
         ],
         compiler_params=pltpu.CompilerParams(vmem_limit_bytes=LIMIT),
         cost_estimate=pl.CostEstimate(flops=0, bytes_accessed=0, transcendentals=0),
-    )(scale, txt_own_block, own, received, *left, *right, before)
+    )(scale, txt_own_block, own, received, weight, d_early, *left, *right, before)
     return image_grads, text_grads, head_grad
 
 

time: 55.9 us -> 53.2 us (0.952)
  waiting for transfers between devices: 16.5 us -> 11 us
  local copies, waits for them, and re-layouts: 1.73 us -> 3.09 us
  starting transfers between devices: 19.4 us -> 20.6 us
    ppermute x14, waiting for transfers between devices: 8.95 us -> 5.71 us  [move(): return lax.ppermute(array, axis, [(i, i ^ mask) for i in range(size)])]
    ppermute x6 -> x8, waiting for transfers between devices: 7.5 us -> 5.31 us  [link(): return lax.ppermute(array, ('img', 'txt'), pairs)]
    unnamed x6, local copies, waits for them, and re-layouts: 1.73 us -> 3.09 us
    ppermute x6 -> x8, starting transfers between devices: 8.85 us -> 9.69 us  [link(): return lax.ppermute(array, ('img', 'txt'), pairs)]
    pallas_call x1 -> x2, Pallas kernels: 3.14 us -> 2.38 us  [the longest x1 2.07 us: gathered(): call(functools.partial(head_early_body, len(left)), head, [VMEM] * (len(l...]
  transfers between devices with their start and end apart: 20 -> 22, of which waited for: 10 -> 7; matrix products, arithmetic and copies ran while one was open for 0% -> 0% of each run, Pallas kernels for 24% -> 24%
where the time goes in v3:
time: 53.2 us; the launch traced here: 52.7 us
  starting transfers between devices  20.6 us (39%)
  Pallas kernels  15.8 us (30%)
  waiting for transfers between devices  11 us (21%)
  local copies, waits for them, and re-layouts  3.09 us (6%)
  between operations  2.1 us (4%)
    ppermute x14, starting transfers between devices, move(): return lax.ppermute(array, axis, [(i, i ^ mask) for i in range(size)])  10.9 us
    ppermute x8, starting transfers between devices, link(): return lax.ppermute(array, ('img', 'txt'), pairs)  9.69 us
    pallas_call x2, Pallas kernels, batch(): call(functools.partial(batch_body, not before, order, n_txt), [shape(held...  8.94 us
    ppermute x14, waiting for transfers between devices, move(): return lax.ppermute(array, axis, [(i, i ^ mask) for i in range(size)])  5.71 us
    ppermute x8, waiting for transfers between devices, link(): return lax.ppermute(array, ('img', 'txt'), pairs)  5.31 us
    unnamed x6, local copies, waits for them, and re-layouts  3.09 us
    pallas_call x1, Pallas kernels, gathered(): pl.pallas_call(functools.partial(last_body, len(left), len(right), sizes)...  2.85 us
    pallas_call x1, Pallas kernels, gathered(): call(functools.partial(head_early_body, len(left)), head, [VMEM] * (len(l...  2.07 us
  transfers between devices with their start and end apart: 22, of which 7 were waited for; matrix products, arithmetic and copies ran while one was open for 0% of the time, Pallas kernels for 24%

profile of v3, /device:TPU:0, one launch (start us, length us, event | category | flops | bytes accessed | tf_op | source)
XLA Modules:
  0.0 52.7 jit_solution(12135258025372671824)
XLA Ops:
  0.6 3.0 %collective-permute-start.4 = (bf16[48,1152]{1,0:T(8,128)(2,1)}, bf16[48,1152]{1,0:T(8,128)(2,1)S(1)}, u32[]{:S(2)}, u32[]{:S(2)}) collective-permute-start(bf16[48,1152]{1,0:T(8,128)(2,1)} %images.1), channel_id=1, source_target_pairs={{0,16},{1,17},{2,18},{3,19},{4,20},{5,21},{6,22},{7,23},{8,9},{9,8... | collective-permute-start | bytes 331784 | tf_op jit(solution)/shard_map/ppermute | solution.py:181
  3.6 1.6 %collective-permute-start = (bf16[48,640]{1,0:T(8,128)(2,1)}, bf16[48,640]{1,0:T(8,128)(2,1)S(1)}, u32[]{:S(2)}, u32[]{:S(2)}) collective-permute-start(bf16[48,640]{1,0:T(8,128)(2,1)} %texts.1), channel_id=1, source_target_pairs={{0,2},{1,3},{2,0},{3,1},{4,6},{5,7},{6,4},{7,5},{8,10},{9,11},{10,... | collective-permute-start | bytes 184328 | tf_op jit(solution)/shard_map/ppermute | solution.py:171
  5.2 2.5 %collective-permute-start.10 = (bf16[48,640]{1,0:T(8,128)(2,1)}, bf16[48,640]{1,0:T(8,128)(2,1)S(1)}, u32[]{:S(2)}, u32[]{:S(2)}) collective-permute-start(bf16[48,640]{1,0:T(8,128)(2,1)} %texts.1), channel_id=1, source_target_pairs={{0,6},{1,7},{2,4},{3,5},{4,2},{5,3},{6,0},{7,1},{8,14},{9,15},{10,... | collective-permute-start | bytes 184328 | tf_op jit(solution)/shard_map/ppermute | solution.py:171
  7.7 0.1 collective-permute-start.9
  9.1 0.0 copy-start.1
  9.1 0.9 %copy-done.1 = bf16[48,1152]{1,0:T(8,128)(2,1)S(1)} copy-done((bf16[48,1152]{1,0:T(8,128)(2,1)S(1)}, bf16[48,1152]{1,0:T(8,128)(2,1)}, u32[]{:S(2)}) %copy-start.1) | copy-done | bytes 110616
  10.0 0.8 %copy-done.2 = bf16[48,640]{1,0:T(8,128)(2,1)S(1)} copy-done((bf16[48,640]{1,0:T(8,128)(2,1)S(1)}, bf16[48,640]{1,0:T(8,128)(2,1)}, u32[]{:S(2)}) %copy-start.2) | copy-done | bytes 61464
  10.9 1.1 %collective-permute-done.10.refs_3_ = bf16[48,640]{1,0:T(8,128)(2,1)S(1)} collective-permute-done((bf16[48,640]{1,0:T(8,128)(2,1)}, bf16[48,640]{1,0:T(8,128)(2,1)S(1)}, u32[]{:S(2)}, u32[]{:S(2)}) %collective-permute-start.10) | collective-permute-done | bytes 61472 | tf_op jit(solution)/shard_map/ppermute | solution.py:171
  11.9 0.0 collective-permute-done.4.refs_1_
  12.0 1.9 %collective-permute-done.9.refs_2_ = bf16[48,640]{1,0:T(8,128)(2,1)S(1)} collective-permute-done((bf16[48,640]{1,0:T(8,128)(2,1)}, bf16[48,640]{1,0:T(8,128)(2,1)S(1)}, u32[]{:S(2)}, u32[]{:S(2)}) %collective-permute-start.9) | collective-permute-done | bytes 61472 | tf_op jit(solution)/shard_map/ppermute | solution.py:171
  13.8 1.2 %collective-permute-start.11 = (bf16[192,640]{1,0:T(8,128)(2,1)S(1)}, bf16[192,640]{1,0:T(8,128)(2,1)S(1)}, u32[]{:S(2)}, u32[]{:S(2)}) collective-permute-start(bf16[192,640]{1,0:T(8,128)(2,1)S(1)} %shard_map.81.refs_0_), channel_id=1, source_target_pairs={{0,16},{1,17},{2,18},{3,19},{4,20},{5,21},{6,22},{7,23},{8,9},{9,8... | collective-permute-start | bytes 737288 | tf_op jit(solution)/shard_map/ppermute | solution.py:181
  15.1 1.0 %collective-permute-start.5 = (bf16[96,1152]{1,0:T(8,128)(2,1)S(1)}, bf16[96,1152]{1,0:T(8,128)(2,1)S(1)}, u32[]{:S(2)}, u32[]{:S(2)}) collective-permute-start(bf16[96,1152]{1,0:T(8,128)(2,1)S(1)} %shard_map.77.refs_0_), channel_id=1, source_target_pairs={{0,1},{1,0},{2,3},{3,2},{4,5},{5,4},{6,7},{7,6},{8,24},{9,25},{10,... | collective-permute-start | bytes 663560 | tf_op jit(solution)/shard_map/ppermute | solution.py:181
  16.0 2.4 %collective-permute-start.3 = (bf16[48,1152]{1,0:T(8,128)(2,1)}, bf16[48,1152]{1,0:T(8,128)(2,1)S(1)}, u32[]{:S(2)}, u32[]{:S(2)}) collective-permute-start(bf16[48,1152]{1,0:T(8,128)(2,1)} %images.1), channel_id=1, source_target_pairs={{0,6},{1,7},{2,4},{3,5},{4,2},{5,3},{6,0},{7,1},{8,14},{9,15},{10,... | collective-permute-start | bytes 331784 | tf_op jit(solution)/shard_map/ppermute | solution.py:171
  18.4 2.0 %collective-permute-start.1 = (bf16[48,1152]{1,0:T(8,128)(2,1)}, bf16[48,1152]{1,0:T(8,128)(2,1)S(1)}, u32[]{:S(2)}, u32[]{:S(2)}) collective-permute-start(bf16[48,1152]{1,0:T(8,128)(2,1)} %images.1), channel_id=1, source_target_pairs={{0,2},{1,3},{2,0},{3,1},{4,6},{5,7},{6,4},{7,5},{8,10},{9,11},{10,... | collective-permute-start | bytes 331784 | tf_op jit(solution)/shard_map/ppermute | solution.py:171
  20.4 0.7 %collective-permute-done.5._.refs_1_ = bf16[96,1152]{1,0:T(8,128)(2,1)S(1)} collective-permute-done((bf16[96,1152]{1,0:T(8,128)(2,1)S(1)}, bf16[96,1152]{1,0:T(8,128)(2,1)S(1)}, u32[]{:S(2)}, u32[]{:S(2)}) %collective-permute-start.5) | collective-permute-done | bytes 221216 | tf_op jit(solution)/shard_map/ppermute | solution.py:181
  21.1 0.9 %collective-permute-start.12 = (bf16[192,640]{1,0:T(8,128)(2,1)S(1)}, bf16[192,640]{1,0:T(8,128)(2,1)S(1)}, u32[]{:S(2)}, u32[]{:S(2)}) collective-permute-start(bf16[192,640]{1,0:T(8,128)(2,1)S(1)} %shard_map.81.refs_0_), channel_id=1, source_target_pairs={{0,1},{1,0},{2,3},{3,2},{4,5},{5,4},{6,7},{7,6},{8,24},{9,25},{10,... | collective-permute-start | bytes 737288 | tf_op jit(solution)/shard_map/ppermute | solution.py:181
  22.0 1.1 %collective-permute-start.13 = (bf16[192,640]{1,0:T(8,128)(2,1)S(1)}, bf16[192,640]{1,0:T(8,128)(2,1)}, u32[]{:S(2)}, u32[]{:S(2)}) collective-permute-start(bf16[192,640]{1,0:T(8,128)(2,1)S(1)} %collective-permute-done.11.refs_1_), channel_id=1, source_target_pairs={{0,1},{1,0},{2,3},{3,2},{4,5},{5,4},{6,7},{7,6},{8,24},{9,25},{10,... | collective-permute-start | bytes 737288 | tf_op jit(solution)/shard_map/ppermute | solution.py:181
  23.1 1.4 %copy-done = bf16[1152,640]{1,0:T(8,128)(2,1)S(1)} copy-done((bf16[1152,640]{1,0:T(8,128)(2,1)S(1)}, bf16[1152,640]{1,0:T(8,128)(2,1)}, u32[]{:S(2)}) %copy-start) | copy-done | bytes 1474584
  24.5 0.3 shard_map.78.weight
  24.8 0.0 collective-permute-done.3.refs_2_
  24.8 2.7 %collective-permute-done.2.refs_1_ = bf16[48,1152]{1,0:T(8,128)(2,1)S(1)} collective-permute-done((bf16[48,1152]{1,0:T(8,128)(2,1)}, bf16[48,1152]{1,0:T(8,128)(2,1)S(1)}, u32[]{:S(2)}, u32[]{:S(2)}) %collective-permute-start.2) | collective-permute-done | bytes 110624 | tf_op jit(solution)/shard_map/ppermute | solution.py:171
  27.6 0.7 %collective-permute-start.7 = (bf16[144,1152]{1,0:T(8,128)(2,1)S(1)}, bf16[144,1152]{1,0:T(8,128)(2,1)S(1)}, u32[]{:S(2)}, u32[]{:S(2)}) collective-permute-start(bf16[144,1152]{1,0:T(8,128)(2,1)S(1)} %shard_map.79.refs_2_), channel_id=1, source_target_pairs={{0,16},{1,17},{2,18},{3,19},{4,20},{5,21},{6,22},{7,23},{8,9},{9,8... | collective-permute-start | bytes 995336 | tf_op jit(solution)/shard_map/ppermute | solution.py:181
  28.3 0.1 pad_add_fusion.place
  28.4 1.8 %collective-permute-done.13.refs_3_ = bf16[192,640]{1,0:T(8,128)(2,1)} collective-permute-done((bf16[192,640]{1,0:T(8,128)(2,1)S(1)}, bf16[192,640]{1,0:T(8,128)(2,1)}, u32[]{:S(2)}, u32[]{:S(2)}) %collective-permute-start.13) | collective-permute-done | bytes 245792 | tf_op jit(solution)/shard_map/ppermute | solution.py:181
  30.2 1.3 %shard_map.82 = (bf16[256,640]{1,0:T(8,128)(2,1)S(1)}, bf16[256,640]{1,0:T(8,128)(2,1)S(1)}, bf16[256,640]{1,0:T(8,128)(2,1)S(1)}, bf16[768,640]{1,0:T(8,128)(2,1)S(1)}, s32[1,1536]{1,0:T(1,128)S(1)}) custom-call(s32[4]{0:T(128)S(1)} %pad_add_fusion.place, bf16[192,640]{1,0:T(8,128)(2,1)S(1)} %shard_map.81.refs_0_, ...), custom_call_target="tpu_custom_call" | custom-call | tf_op jit(solution)/shard_map/pallas_call | solution.py:222
  31.5 0.1 collective-permute-start.14
  31.6 0.5 collective-permute-start.15
  32.1 0.1 collective-permute-start.16
  32.2 0.7 %collective-permute-start.6 = (bf16[144,1152]{1,0:T(8,128)(2,1)S(1)}, bf16[144,1152]{1,0:T(8,128)(2,1)S(1)}, u32[]{:S(2)}, u32[]{:S(2)}) collective-permute-start(bf16[144,1152]{1,0:T(8,128)(2,1)S(1)} %shard_map.79.refs_2_), channel_id=1, source_target_pairs={{0,1},{1,0},{2,3},{3,2},{4,5},{5,4},{6,7},{7,6},{8,24},{9,25},{10,... | collective-permute-start | bytes 995336 | tf_op jit(solution)/shard_map/ppermute | solution.py:181
  32.9 1.9 %collective-permute-done.7.refs_3_ = bf16[144,1152]{1,0:T(8,128)(2,1)S(1)} collective-permute-done((bf16[144,1152]{1,0:T(8,128)(2,1)S(1)}, bf16[144,1152]{1,0:T(8,128)(2,1)S(1)}, u32[]{:S(2)}, u32[]{:S(2)}) %collective-permute-start.7) | collective-permute-done | bytes 331808 | tf_op jit(solution)/shard_map/ppermute | solution.py:181
  34.7 1.1 %collective-permute-start.8 = (bf16[144,1152]{1,0:T(8,128)(2,1)S(1)}, bf16[144,1152]{1,0:T(8,128)(2,1)S(1)}, u32[]{:S(2)}, u32[]{:S(2)}) collective-permute-start(bf16[144,1152]{1,0:T(8,128)(2,1)S(1)} %collective-permute-done.7.refs_3_), channel_id=1, source_target_pairs={{0,1},{1,0},{2,3},{3,2},{4,5},{5,4},{6,7},{7,6},{8,24},{9,25},{10,... | collective-permute-start | bytes 995336 | tf_op jit(solution)/shard_map/ppermute | solution.py:181
  35.8 0.1 shard_map.84.images.refs_0_
  35.9 0.0 collective-permute-done.14.refs_0_
  35.9 0.1 collective-permute-start.20
  36.0 0.0 collective-permute-done.15.refs_1_
  36.0 0.0 collective-permute-done.16.refs_2_
  36.0 0.1 shard_map.83.txt_sib
  36.1 5.3 %shard_map.85 = (bf16[480,640]{1,0:T(8,128)(2,1)S(1)}, f32[48,640]{1,0:T(8,128)S(1)}, f32[48,640]{1,0:T(8,128)S(1)}) custom-call(s32[4]{0:T(128)S(1)} %pad_add_fusion.place, f32[1,128]{1,0:T(1,128)S(1)} %get-tuple-element.26.scale_ref.scale, f32[1,128]{1,0:T(1,128)S(1)} %get-tuple-element.28.bias_ref, bf16[480,1152]{1,0:T(8,128)(2,1)S(1)} %shard_map.84.images.refs_0_, ...), custom_call_target="tpu_custom_call" | custom-call | flops 1400000000 | tf_op jit(solution)/shard_map/pallas_call | solution.py:242
  41.4 0.5 %collective-permute-start.21 = (bf16[480,640]{1,0:T(8,128)(2,1)S(1)}, bf16[480,640]{1,0:T(8,128)(2,1)S(1)}, u32[]{:S(2)}, u32[]{:S(2)}) collective-permute-start(bf16[480,640]{1,0:T(8,128)(2,1)S(1)} %get-tuple-element.43.refs_2_.mine), channel_id=1, source_target_pairs={{0,8},{8,0},{16,24},{24,16},{1,9},{9,1},{17,25},{25,17},{2,10},{10... | collective-permute-start | bytes 1843208 | tf_op jit(solution)/shard_map/ppermute | solution.py:171
  41.9 0.0 collective-permute-done.6.refs_0_
  41.9 0.9 %collective-permute-done.8.refs_1_ = bf16[144,1152]{1,0:T(8,128)(2,1)S(1)} collective-permute-done((bf16[144,1152]{1,0:T(8,128)(2,1)S(1)}, bf16[144,1152]{1,0:T(8,128)(2,1)S(1)}, u32[]{:S(2)}, u32[]{:S(2)}) %collective-permute-start.8) | collective-permute-done | bytes 331808 | tf_op jit(solution)/shard_map/ppermute | solution.py:181
  42.9 0.6 %collective-permute-start.18 = (bf16[288,1152]{1,0:T(8,128)(2,1)S(1)}, bf16[288,1152]{1,0:T(8,128)(2,1)S(1)}, u32[]{:S(2)}, u32[]{:S(2)}) collective-permute-start(bf16[288,1152]{1,0:T(8,128)(2,1)S(1)} %shard_map.80.images.refs_0_), channel_id=1, source_target_pairs={{0,8},{8,0},{16,24},{24,16},{1,9},{9,1},{17,25},{25,17},{2,10},{10... | collective-permute-start | bytes 1990664 | tf_op jit(solution)/shard_map/ppermute | solution.py:171
  43.5 3.7 %shard_map.86 = (bf16[288,640]{1,0:T(8,128)(2,1)S(1)}, f32[48,640]{1,0:T(8,128)S(1)}, f32[48,640]{1,0:T(8,128)S(1)}) custom-call(s32[4]{0:T(128)S(1)} %pad_add_fusion.place, f32[1,128]{1,0:T(1,128)S(1)} %get-tuple-element.26.scale_ref.scale, f32[1,128]{1,0:T(1,128)S(1)} %get-tuple-element.28.bias_ref, bf16[288,1152]{1,0:T(8,128)(2,1)S(1)} %shard_map.80.images.refs_0_, ...), custom_call_target="tpu_custom_call" | custom-call | flops 6000000000 | tf_op jit(solution)/shard_map/pallas_call | solution.py:242
  47.2 0.1 collective-permute-start.19
  47.2 0.5 collective-permute-start.17
  47.7 0.0 collective-permute-done.20.refs_1_
  47.7 2.1 %shard_map.87.refs_4_ = f32[1152,640]{1,0:T(8,128)S(1)} custom-call(bf16[480,1152]{1,0:T(8,128)(2,1)S(1)} %shard_map.84.images.refs_0_, bf16[480,1152]{1,0:T(8,128)(2,1)S(1)} %collective-permute-done.20.refs_1_, bf16[480,640]{1,0:T(8,128)(2,1)S(1)} %get-tuple-element.43.refs_2_.mine, bf16[480,640]{1,0:T(8,128)(2,1)S(1)} %collective-permute-done.21.refs_3_), custom_call_target="tpu_custom_call" | custom-call | tf_op jit(solution)/shard_map/pallas_call | solution.py:264
  49.8 2.9 %shard_map.88 = (f32[1152,640]{1,0:T(8,128)}, bf16[48,640]{1,0:T(8,128)(2,1)}, bf16[48,1152]{1,0:T(8,128)(2,1)}) custom-call(f32[1,128]{1,0:T(1,128)S(1)} %get-tuple-element.26.scale_ref.scale, bf16[48,640]{1,0:T(8,128)(2,1)S(1)} %get-tuple-element.27.refs_0_.texts, f32[48,640]{1,0:T(8,128)S(1)} %get-tuple-element.41.own, ...), custom_call_target="tpu_custom_call" | custom-call | tf_op jit(solution)/shard_map/pallas_call | solution.py:273
  (16 shorter events, 0.2 us)
Async XLA Ops:
  0.6 11.3 %collective-permute-start.4 = (bf16[48,1152]{1,0:T(8,128)(2,1)}, bf16[48,1152]{1,0:T(8,128)(2,1)S(1)}, u32[]{:S(2)}, u32[]{:S(2)}) collective-permute-start(bf16[48,1152]{1,0:T(8,128)(2,1)} %images.1), channel_id=1, source_target_pairs={{0,16},{1,17},{2,18},{3,19},{4,20},{5,21},{6,22},{7,23},{8,9},{9,8... | collective-permute-start | bytes 331784 | tf_op jit(solution)/shard_map/ppermute | solution.py:181
  3.6 5.5 %collective-permute-start = (bf16[48,640]{1,0:T(8,128)(2,1)}, bf16[48,640]{1,0:T(8,128)(2,1)S(1)}, u32[]{:S(2)}, u32[]{:S(2)}) collective-permute-start(bf16[48,640]{1,0:T(8,128)(2,1)} %texts.1), channel_id=1, source_target_pairs={{0,2},{1,3},{2,0},{3,1},{4,6},{5,7},{6,4},{7,5},{8,10},{9,11},{10,... | collective-permute-start | bytes 184328 | tf_op jit(solution)/shard_map/ppermute | solution.py:171
  5.2 6.7 %collective-permute-start.10 = (bf16[48,640]{1,0:T(8,128)(2,1)}, bf16[48,640]{1,0:T(8,128)(2,1)S(1)}, u32[]{:S(2)}, u32[]{:S(2)}) collective-permute-start(bf16[48,640]{1,0:T(8,128)(2,1)} %texts.1), channel_id=1, source_target_pairs={{0,6},{1,7},{2,4},{3,5},{4,2},{5,3},{6,0},{7,1},{8,14},{9,15},{10,... | collective-permute-start | bytes 184328 | tf_op jit(solution)/shard_map/ppermute | solution.py:171
  7.7 6.1 %collective-permute-start.9 = (bf16[48,640]{1,0:T(8,128)(2,1)}, bf16[48,640]{1,0:T(8,128)(2,1)S(1)}, u32[]{:S(2)}, u32[]{:S(2)}) collective-permute-start(bf16[48,640]{1,0:T(8,128)(2,1)} %texts.1), channel_id=1, source_target_pairs={{0,4},{1,5},{2,6},{3,7},{4,0},{5,1},{6,2},{7,3},{8,12},{9,13},{10,... | collective-permute-start | bytes 184328 | tf_op jit(solution)/shard_map/ppermute | solution.py:171
  9.1 0.9 %copy-start.1 = (bf16[48,1152]{1,0:T(8,128)(2,1)S(1)}, bf16[48,1152]{1,0:T(8,128)(2,1)}, u32[]{:S(2)}) copy-start(bf16[48,1152]{1,0:T(8,128)(2,1)} %images.1) | copy-start | bytes 331780
  10.0 0.8 %copy-start.2 = (bf16[48,640]{1,0:T(8,128)(2,1)S(1)}, bf16[48,640]{1,0:T(8,128)(2,1)}, u32[]{:S(2)}) copy-start(bf16[48,640]{1,0:T(8,128)(2,1)} %texts.1) | copy-start | bytes 184324
  13.8 8.1 %collective-permute-start.11 = (bf16[192,640]{1,0:T(8,128)(2,1)S(1)}, bf16[192,640]{1,0:T(8,128)(2,1)S(1)}, u32[]{:S(2)}, u32[]{:S(2)}) collective-permute-start(bf16[192,640]{1,0:T(8,128)(2,1)S(1)} %shard_map.81.refs_0_), channel_id=1, source_target_pairs={{0,16},{1,17},{2,18},{3,19},{4,20},{5,21},{6,22},{7,23},{8,9},{9,8... | collective-permute-start | bytes 737288 | tf_op jit(solution)/shard_map/ppermute | solution.py:181
  15.1 6.0 %collective-permute-start.5 = (bf16[96,1152]{1,0:T(8,128)(2,1)S(1)}, bf16[96,1152]{1,0:T(8,128)(2,1)S(1)}, u32[]{:S(2)}, u32[]{:S(2)}) collective-permute-start(bf16[96,1152]{1,0:T(8,128)(2,1)S(1)} %shard_map.77.refs_0_), channel_id=1, source_target_pairs={{0,1},{1,0},{2,3},{3,2},{4,5},{5,4},{6,7},{7,6},{8,24},{9,25},{10,... | collective-permute-start | bytes 663560 | tf_op jit(solution)/shard_map/ppermute | solution.py:181
  16.0 8.8 %collective-permute-start.3 = (bf16[48,1152]{1,0:T(8,128)(2,1)}, bf16[48,1152]{1,0:T(8,128)(2,1)S(1)}, u32[]{:S(2)}, u32[]{:S(2)}) collective-permute-start(bf16[48,1152]{1,0:T(8,128)(2,1)} %images.1), channel_id=1, source_target_pairs={{0,6},{1,7},{2,4},{3,5},{4,2},{5,3},{6,0},{7,1},{8,14},{9,15},{10,... | collective-permute-start | bytes 331784 | tf_op jit(solution)/shard_map/ppermute | solution.py:171
  18.4 9.2 %collective-permute-start.2 = (bf16[48,1152]{1,0:T(8,128)(2,1)}, bf16[48,1152]{1,0:T(8,128)(2,1)S(1)}, u32[]{:S(2)}, u32[]{:S(2)}) collective-permute-start(bf16[48,1152]{1,0:T(8,128)(2,1)} %images.1), channel_id=1, source_target_pairs={{0,4},{1,5},{2,6},{3,7},{4,0},{5,1},{6,2},{7,3},{8,12},{9,13},{10,... | collective-permute-start | bytes 331784 | tf_op jit(solution)/shard_map/ppermute | solution.py:171
  18.4 9.2 %collective-permute-start.1 = (bf16[48,1152]{1,0:T(8,128)(2,1)}, bf16[48,1152]{1,0:T(8,128)(2,1)S(1)}, u32[]{:S(2)}, u32[]{:S(2)}) collective-permute-start(bf16[48,1152]{1,0:T(8,128)(2,1)} %images.1), channel_id=1, source_target_pairs={{0,2},{1,3},{2,0},{3,1},{4,6},{5,7},{6,4},{7,5},{8,10},{9,11},{10,... | collective-permute-start | bytes 331784 | tf_op jit(solution)/shard_map/ppermute | solution.py:171
  21.1 7.3 %collective-permute-start.12 = (bf16[192,640]{1,0:T(8,128)(2,1)S(1)}, bf16[192,640]{1,0:T(8,128)(2,1)S(1)}, u32[]{:S(2)}, u32[]{:S(2)}) collective-permute-start(bf16[192,640]{1,0:T(8,128)(2,1)S(1)} %shard_map.81.refs_0_), channel_id=1, source_target_pairs={{0,1},{1,0},{2,3},{3,2},{4,5},{5,4},{6,7},{7,6},{8,24},{9,25},{10,... | collective-permute-start | bytes 737288 | tf_op jit(solution)/shard_map/ppermute | solution.py:181
  22.0 8.3 %collective-permute-start.13 = (bf16[192,640]{1,0:T(8,128)(2,1)S(1)}, bf16[192,640]{1,0:T(8,128)(2,1)}, u32[]{:S(2)}, u32[]{:S(2)}) collective-permute-start(bf16[192,640]{1,0:T(8,128)(2,1)S(1)} %collective-permute-done.11.refs_1_), channel_id=1, source_target_pairs={{0,1},{1,0},{2,3},{3,2},{4,5},{5,4},{6,7},{7,6},{8,24},{9,25},{10,... | collective-permute-start | bytes 737288 | tf_op jit(solution)/shard_map/ppermute | solution.py:181
  23.1 1.4 %copy-start = (bf16[1152,640]{1,0:T(8,128)(2,1)S(1)}, bf16[1152,640]{1,0:T(8,128)(2,1)}, u32[]{:S(2)}) copy-start(bf16[1152,640]{1,0:T(8,128)(2,1)} %array.1) | copy-start | bytes 4423684
  27.6 7.2 %collective-permute-start.7 = (bf16[144,1152]{1,0:T(8,128)(2,1)S(1)}, bf16[144,1152]{1,0:T(8,128)(2,1)S(1)}, u32[]{:S(2)}, u32[]{:S(2)}) collective-permute-start(bf16[144,1152]{1,0:T(8,128)(2,1)S(1)} %shard_map.79.refs_2_), channel_id=1, source_target_pairs={{0,16},{1,17},{2,18},{3,19},{4,20},{5,21},{6,22},{7,23},{8,9},{9,8... | collective-permute-start | bytes 995336 | tf_op jit(solution)/shard_map/ppermute | solution.py:181
  31.5 4.4 %collective-permute-start.14 = (bf16[256,640]{1,0:T(8,128)(2,1)S(1)}, bf16[256,640]{1,0:T(8,128)(2,1)S(1)}, u32[]{:S(2)}, u32[]{:S(2)}) collective-permute-start(bf16[256,640]{1,0:T(8,128)(2,1)S(1)} %get-tuple-element.35), channel_id=1, source_target_pairs={{0,8},{8,0},{16,24},{24,16},{1,9},{9,1},{17,25},{25,17},{2,10},{10... | collective-permute-start | bytes 983048 | tf_op jit(solution)/shard_map/ppermute | solution.py:171
  31.6 4.4 %collective-permute-start.15 = (bf16[256,640]{1,0:T(8,128)(2,1)S(1)}, bf16[256,640]{1,0:T(8,128)(2,1)S(1)}, u32[]{:S(2)}, u32[]{:S(2)}) collective-permute-start(bf16[256,640]{1,0:T(8,128)(2,1)S(1)} %get-tuple-element.36), channel_id=1, source_target_pairs={{0,8},{8,0},{16,24},{24,16},{1,9},{9,1},{17,25},{25,17},{2,10},{10... | collective-permute-start | bytes 983048 | tf_op jit(solution)/shard_map/ppermute | solution.py:171
  32.1 3.9 %collective-permute-start.16 = (bf16[256,640]{1,0:T(8,128)(2,1)S(1)}, bf16[256,640]{1,0:T(8,128)(2,1)S(1)}, u32[]{:S(2)}, u32[]{:S(2)}) collective-permute-start(bf16[256,640]{1,0:T(8,128)(2,1)S(1)} %get-tuple-element.37), channel_id=1, source_target_pairs={{0,8},{8,0},{16,24},{24,16},{1,9},{9,1},{17,25},{25,17},{2,10},{10... | collective-permute-start | bytes 983048 | tf_op jit(solution)/shard_map/ppermute | solution.py:171
  32.2 9.7 %collective-permute-start.6 = (bf16[144,1152]{1,0:T(8,128)(2,1)S(1)}, bf16[144,1152]{1,0:T(8,128)(2,1)S(1)}, u32[]{:S(2)}, u32[]{:S(2)}) collective-permute-start(bf16[144,1152]{1,0:T(8,128)(2,1)S(1)} %shard_map.79.refs_2_), channel_id=1, source_target_pairs={{0,1},{1,0},{2,3},{3,2},{4,5},{5,4},{6,7},{7,6},{8,24},{9,25},{10,... | collective-permute-start | bytes 995336 | tf_op jit(solution)/shard_map/ppermute | solution.py:181
  34.7 8.1 %collective-permute-start.8 = (bf16[144,1152]{1,0:T(8,128)(2,1)S(1)}, bf16[144,1152]{1,0:T(8,128)(2,1)S(1)}, u32[]{:S(2)}, u32[]{:S(2)}) collective-permute-start(bf16[144,1152]{1,0:T(8,128)(2,1)S(1)} %collective-permute-done.7.refs_3_), channel_id=1, source_target_pairs={{0,1},{1,0},{2,3},{3,2},{4,5},{5,4},{6,7},{7,6},{8,24},{9,25},{10,... | collective-permute-start | bytes 995336 | tf_op jit(solution)/shard_map/ppermute | solution.py:181
  35.9 11.8 %collective-permute-start.20 = (bf16[480,1152]{1,0:T(8,128)(2,1)S(1)}, bf16[480,1152]{1,0:T(8,128)(2,1)S(1)}, u32[]{:S(2)}, u32[]{:S(2)}) collective-permute-start(bf16[480,1152]{1,0:T(8,128)(2,1)S(1)} %shard_map.84.images.refs_0_), channel_id=1, source_target_pairs={{0,8},{8,0},{16,24},{24,16},{1,9},{9,1},{17,25},{25,17},{2,10},{10... | collective-permute-start | bytes 3317768 | tf_op jit(solution)/shard_map/ppermute | solution.py:171
  41.4 6.3 %collective-permute-start.21 = (bf16[480,640]{1,0:T(8,128)(2,1)S(1)}, bf16[480,640]{1,0:T(8,128)(2,1)S(1)}, u32[]{:S(2)}, u32[]{:S(2)}) collective-permute-start(bf16[480,640]{1,0:T(8,128)(2,1)S(1)} %get-tuple-element.43.refs_2_.mine), channel_id=1, source_target_pairs={{0,8},{8,0},{16,24},{24,16},{1,9},{9,1},{17,25},{25,17},{2,10},{10... | collective-permute-start | bytes 1843208 | tf_op jit(solution)/shard_map/ppermute | solution.py:171
  42.9 6.9 %collective-permute-start.18 = (bf16[288,1152]{1,0:T(8,128)(2,1)S(1)}, bf16[288,1152]{1,0:T(8,128)(2,1)S(1)}, u32[]{:S(2)}, u32[]{:S(2)}) collective-permute-start(bf16[288,1152]{1,0:T(8,128)(2,1)S(1)} %shard_map.80.images.refs_0_), channel_id=1, source_target_pairs={{0,8},{8,0},{16,24},{24,16},{1,9},{9,1},{17,25},{25,17},{2,10},{10... | collective-permute-start | bytes 1990664 | tf_op jit(solution)/shard_map/ppermute | solution.py:171
  47.2 2.7 %collective-permute-start.19 = (bf16[288,640]{1,0:T(8,128)(2,1)S(1)}, bf16[288,640]{1,0:T(8,128)(2,1)S(1)}, u32[]{:S(2)}, u32[]{:S(2)}) collective-permute-start(bf16[288,640]{1,0:T(8,128)(2,1)S(1)} %get-tuple-element.45.refs_2_), channel_id=1, source_target_pairs={{0,8},{8,0},{16,24},{24,16},{1,9},{9,1},{17,25},{25,17},{2,10},{10... | collective-permute-start | bytes 1105928 | tf_op jit(solution)/shard_map/ppermute | solution.py:171
  47.2 2.6 %collective-permute-start.17 = (f32[48,640]{1,0:T(8,128)S(1)}, f32[48,640]{1,0:T(8,128)S(1)}, u32[]{:S(2)}, u32[]{:S(2)}) collective-permute-start(f32[48,640]{1,0:T(8,128)S(1)} %get-tuple-element.42), channel_id=1, source_target_pairs={{0,8},{8,0},{16,24},{24,16},{1,9},{9,1},{17,25},{25,17},{2,10},{10... | collective-permute-start | bytes 368648 | tf_op jit(solution)/shard_map/ppermute | solution.py:171

commit v4 on v3

--- a/solution.py
+++ b/solution.py
@@ -42,7 +42,7 @@
     return place[0] ^ (2 * (mask // 2)), place[1] ^ z ^ lax.rem(mask, 2)
 
 
-def unit_body(order, n_img, place, *refs):
+def unit_body(order, n_img, place, _, *refs):
     parts, sent, whole, ids = refs[:4], refs[4:-2], refs[-2], refs[-1]
     total, rows = whole.shape[0], parts[0].shape[0]
     block = total // len(order)
@@ -66,17 +66,32 @@
         sent[at // size][pl.ds(at % size, step), :] = unit
 
 
-def batch_body(first, order, n_txt, place, scale_ref, bias_ref, images, weight, txt_own, txt_sib, col_ids, *refs):
+def hidden_body(images, weight, hidden_out, unit_out, inv_out):
+    hidden = dot(images[...], weight[...])
+    inv = lax.rsqrt(jnp.sum(hidden * hidden, axis=1, keepdims=True) + eps)
+    hidden_out[...] = hidden
+    unit_out[...] = (hidden * inv).astype(bf16)
+    inv_out[...] = inv
+
+
+def batch_body(
+    first, order, n_txt, place, scale_ref, bias_ref, images, weight, txt_own, txt_sib, col_ids, *refs
+):
     if first:
-        d_hidden_ref, own_ref, sib_ref, hidden_ref, unit_ref, grad_ref = refs
+        hidden_in, unit_in, inv_in, d_hidden_ref, own_ref, sib_ref, hidden_ref, unit_ref, grad_ref = refs
     else:
         own_in, sib_in, d_hidden_ref, own_ref, sib_ref, hidden_ref, unit_ref, grad_ref = refs
     scale, bias = scale_ref[0:1, 0:1], bias_ref[0:1, 0:1]
     block = own_ref.shape[0]
     hidden = dot(images[...], weight[...])
     inv = lax.rsqrt(jnp.sum(hidden * hidden, axis=1, keepdims=True) + eps)
-    hidden_ref[...] = hidden
-    unit_ref[...] = (hidden * inv).astype(bf16)
+    at = hidden_ref.shape[0] - images.shape[0]
+    hidden_ref[pl.ds(at, images.shape[0]), :] = hidden
+    unit_ref[pl.ds(at, images.shape[0]), :] = (hidden * inv).astype(bf16)
+    if first:
+        hidden_ref[pl.ds(0, at), :] = hidden_in[...]
+        unit_ref[pl.ds(0, at), :] = unit_in[...]
+        inv = jnp.concatenate([inv_in[...], inv], axis=0)
     ids = []
     for entry in order:
         img, txt = source(place, 0, entry)
@@ -126,11 +141,12 @@
         at += ref.shape[0]
 
 
-def head_early_body(count, *refs):
-    images, d_hidden, out = refs[:count], refs[count:-1], refs[-1]
+def head_body(count, d_count, *refs):
+    images, d_hidden, rest = refs[:count], refs[count : count + d_count], refs[count + d_count :]
     left = jnp.concatenate([ref[...] for ref in images], axis=0)
     right = jnp.concatenate([ref[...] for ref in d_hidden], axis=0)
-    out[...] = dot(left, right, TN)
+    terms = dot(left, right, TN)
+    rest[-1][...] = terms + rest[0][...] if len(rest) == 2 else terms
 
 
 def last_body(count, d_count, sizes, scale, texts, own, received, weight, mine, *refs):
@@ -218,29 +234,40 @@
     two = join(img_own_block, img_near)
     img_two = link(two, True)
     txt_parts = [four, near, far, link(after(near, *(img_two,)), True)]
+    weight = call(hold_body, jax.ShapeDtypeStruct(head_weight.shape, bf16), [ANY, ANY], 0, [
+        pltpu.SemaphoreType.DMA
+    ])(head_weight, img_two)
+    three = join(*img_z[:2], after(img_z[2], weight), flops=1_000_000_000)
+    near = link(three, False)
+    far = link(three, True)
+    ready = join(two, img_two, three)
+    ready_hidden = call(
+        hidden_body,
+        [
+            jax.ShapeDtypeStruct((ready.shape[0], features), f32),
+            shape(ready.shape[0], texts),
+            jax.ShapeDtypeStruct((ready.shape[0], 1), f32),
+        ],
+        [VMEM] * 2,
+        0,
+    )(ready, weight)
     third = total // 3
     *sent, txt_own, col_ids = call(
         functools.partial(unit_body, order, n_img),
         [shape(third, texts)] * 3 + [shape(total, texts), jax.ShapeDtypeStruct((1, 2 * total), jnp.int32)],
-        [SMEM] + [VMEM] * len(txt_parts),
+        [SMEM, ANY] + [VMEM] * len(txt_parts),
         0,
-    )(place, *txt_parts)
+    )(place, ready_hidden[2], *txt_parts)
     txt_sib = join(*[core(part) for part in sent])
-    weight = call(hold_body, jax.ShapeDtypeStruct(head_weight.shape, bf16), [ANY, ANY], 0, [
-        pltpu.SemaphoreType.DMA
-    ])(head_weight, img_two)
-    three = join(*img_z[:2], after(img_z[2], weight), flops=0)
-    near = link(three, False)
-    far = link(three, True)
-    early = [join(two, img_two, three, near)]
-    img_last = [join(far, link(after(near, *()), True))]
-    early_sib = [core(part) for part in early]
+    early = [ready, near]
+    last = link(near, True)
 
     def batch(images, order, cost, before):
-        held = images.shape[0]
+        held = len(order) * rows
+        first = held > images.shape[0]
         term = jax.ShapeDtypeStruct((rows, features), f32)
         return call(
-            functools.partial(batch_body, not before, order, n_txt),
+            functools.partial(batch_body, first, order, n_txt),
             [shape(held, texts), term, term],
             [SMEM] + [VMEM] * (7 + len(before)),
             cost,
@@ -251,22 +278,24 @@
             ],
         )(place, scale, bias, images, weight, txt_own, txt_sib, col_ids, *before)
 
-    d_early, own, sib = batch(early[0], early_order, 1_400_000_000, [])
+    d_early, own, sib = batch(near, early_order, 1_400_000_000, ready_hidden)
     d_early_sib = core(d_early)
-    late_sib = [core(after(part, d_early)) for part in img_last]
+    early_sib = [core(ready), core(near)]
+    head = jax.ShapeDtypeStruct((emb, features), f32)
+
+    def head_terms(images, d_hidden, *before):
+        refs = [*images, *d_hidden, *before]
+        body = functools.partial(head_body, len(images), len(d_hidden))
+        return call(body, head, [VMEM] * len(refs), 0)(*refs)
+
+    before = head_terms(early, [d_early])
+    img_last = [join(after(far, before, early_sib[1]), last)]
+    late_sib = [core(part) for part in img_last]
     d_late, own, sib = batch(img_last[0], late_order, 6_000_000_000, [own, sib])
     d_late_sib = core(d_late)
     received = core(sib)
 
-    left = early + early_sib
-    right = [d_early, d_early_sib]
-    head = jax.ShapeDtypeStruct((emb, features), f32)
-    before = call(
-        functools.partial(head_early_body, len(left)),
-        head,
-        [VMEM] * (len(left) + len(right)),
-        0,
-    )(*left, *right)
+    before = head_terms(early_sib, [d_early_sib], before)
     left = img_last + late_sib
     right = [d_late, d_late_sib]
     sizes = [256, 384, emb - 640] if emb % 128 == 0 and emb > 640 else [emb]

time: 53.2 us -> 51.9 us (0.976)
  waiting for transfers between devices: 11 us -> 9.69 us
    ppermute x8, waiting for transfers between devices: 5.31 us -> 3.8 us  [link(): return lax.ppermute(array, ('img', 'txt'), pairs)]
    pallas_call x3 -> x5, Pallas kernels: 11 us -> 11.3 us  [the longest x2 8.07 us: batch(): call(functools.partial(batch_body, first, order, n_txt), [shape(held, tex...]
    ppermute x14 -> x15, waiting for transfers between devices: 5.71 us -> 5.89 us  [move(): return lax.ppermute(array, axis, [(i, i ^ mask) for i in range(size)])]
    ppermute x14 -> x15, starting transfers between devices: 10.9 us -> 10.8 us  [move(): return lax.ppermute(array, axis, [(i, i ^ mask) for i in range(size)])]
  transfers between devices with their start and end apart: 22 -> 23, of which waited for: 7 -> 7; matrix products, arithmetic and copies ran while one was open for 0% -> 0% of each run, Pallas kernels for 24% -> 25%
where the time goes in v4:
time: 51.9 us; the launch traced here: 51.4 us
  starting transfers between devices  20.8 us (40%)
  Pallas kernels  15.6 us (30%)
  waiting for transfers between devices  9.69 us (19%)
  local copies, waits for them, and re-layouts  3.09 us (6%)
  between operations  2.1 us (4%)
    ppermute x15, starting transfers between devices, move(): return lax.ppermute(array, axis, [(i, i ^ mask) for i in range(size)])  10.8 us
    ppermute x8, starting transfers between devices, link(): return lax.ppermute(array, ('img', 'txt'), pairs)  9.98 us
    pallas_call x2, Pallas kernels, batch(): call(functools.partial(batch_body, first, order, n_txt), [shape(held, tex...  8.07 us
    ppermute x15, waiting for transfers between devices, move(): return lax.ppermute(array, axis, [(i, i ^ mask) for i in range(size)])  5.89 us
    ppermute x8, waiting for transfers between devices, link(): return lax.ppermute(array, ('img', 'txt'), pairs)  3.8 us
    unnamed x6, local copies, waits for them, and re-layouts  3.09 us
    pallas_call x1, Pallas kernels, gathered(): pl.pallas_call(functools.partial(last_body, len(left), len(right), sizes)...  2.87 us
    pallas_call x2, Pallas kernels, head_terms(): return call(body, head, [VMEM] * len(refs), 0)(*refs)  2.29 us
  transfers between devices with their start and end apart: 23, of which 7 were waited for; matrix products, arithmetic and copies ran while one was open for 0% of the time, Pallas kernels for 25%

profile of v4, /device:TPU:0, one launch (start us, length us, event | category | flops | bytes accessed | tf_op | source)
XLA Modules:
  0.0 51.4 jit_solution(17774334379516842427)
XLA Ops:
  0.6 3.0 %collective-permute-start.4 = (bf16[48,1152]{1,0:T(8,128)(2,1)}, bf16[48,1152]{1,0:T(8,128)(2,1)S(1)}, u32[]{:S(2)}, u32[]{:S(2)}) collective-permute-start(bf16[48,1152]{1,0:T(8,128)(2,1)} %images.1), channel_id=1, source_target_pairs={{0,16},{1,17},{2,18},{3,19},{4,20},{5,21},{6,22},{7,23},{8,9},{9,8... | collective-permute-start | bytes 331784 | tf_op jit(solution)/shard_map/ppermute | solution.py:197
  3.6 1.6 %collective-permute-start = (bf16[48,640]{1,0:T(8,128)(2,1)}, bf16[48,640]{1,0:T(8,128)(2,1)S(1)}, u32[]{:S(2)}, u32[]{:S(2)}) collective-permute-start(bf16[48,640]{1,0:T(8,128)(2,1)} %texts.1), channel_id=1, source_target_pairs={{0,2},{1,3},{2,0},{3,1},{4,6},{5,7},{6,4},{7,5},{8,10},{9,11},{10,... | collective-permute-start | bytes 184328 | tf_op jit(solution)/shard_map/ppermute | solution.py:187
  5.2 2.5 %collective-permute-start.9 = (bf16[48,640]{1,0:T(8,128)(2,1)}, bf16[48,640]{1,0:T(8,128)(2,1)S(1)}, u32[]{:S(2)}, u32[]{:S(2)}) collective-permute-start(bf16[48,640]{1,0:T(8,128)(2,1)} %texts.1), channel_id=1, source_target_pairs={{0,6},{1,7},{2,4},{3,5},{4,2},{5,3},{6,0},{7,1},{8,14},{9,15},{10,... | collective-permute-start | bytes 184328 | tf_op jit(solution)/shard_map/ppermute | solution.py:187
  7.7 0.1 collective-permute-start.8
  9.1 0.0 copy-start.1
  9.1 0.9 %copy-done.1 = bf16[48,1152]{1,0:T(8,128)(2,1)S(1)} copy-done((bf16[48,1152]{1,0:T(8,128)(2,1)S(1)}, bf16[48,1152]{1,0:T(8,128)(2,1)}, u32[]{:S(2)}) %copy-start.1) | copy-done | bytes 110616
  10.0 0.8 %copy-done.2 = bf16[48,640]{1,0:T(8,128)(2,1)S(1)} copy-done((bf16[48,640]{1,0:T(8,128)(2,1)S(1)}, bf16[48,640]{1,0:T(8,128)(2,1)}, u32[]{:S(2)}) %copy-start.2) | copy-done | bytes 61464
  10.9 1.1 %collective-permute-done.9.refs_3_ = bf16[48,640]{1,0:T(8,128)(2,1)S(1)} collective-permute-done((bf16[48,640]{1,0:T(8,128)(2,1)}, bf16[48,640]{1,0:T(8,128)(2,1)S(1)}, u32[]{:S(2)}, u32[]{:S(2)}) %collective-permute-start.9) | collective-permute-done | bytes 61472 | tf_op jit(solution)/shard_map/ppermute | solution.py:187
  11.9 0.0 collective-permute-done.4.refs_1_
  12.0 1.9 %collective-permute-done.8.refs_2_ = bf16[48,640]{1,0:T(8,128)(2,1)S(1)} collective-permute-done((bf16[48,640]{1,0:T(8,128)(2,1)}, bf16[48,640]{1,0:T(8,128)(2,1)S(1)}, u32[]{:S(2)}, u32[]{:S(2)}) %collective-permute-start.8) | collective-permute-done | bytes 61472 | tf_op jit(solution)/shard_map/ppermute | solution.py:187
  13.8 1.2 %collective-permute-start.10 = (bf16[192,640]{1,0:T(8,128)(2,1)S(1)}, bf16[192,640]{1,0:T(8,128)(2,1)S(1)}, u32[]{:S(2)}, u32[]{:S(2)}) collective-permute-start(bf16[192,640]{1,0:T(8,128)(2,1)S(1)} %shard_map.82.refs_0_), channel_id=1, source_target_pairs={{0,16},{1,17},{2,18},{3,19},{4,20},{5,21},{6,22},{7,23},{8,9},{9,8... | collective-permute-start | bytes 737288 | tf_op jit(solution)/shard_map/ppermute | solution.py:197
  15.1 1.0 %collective-permute-start.5 = (bf16[96,1152]{1,0:T(8,128)(2,1)S(1)}, bf16[96,1152]{1,0:T(8,128)(2,1)S(1)}, u32[]{:S(2)}, u32[]{:S(2)}) collective-permute-start(bf16[96,1152]{1,0:T(8,128)(2,1)S(1)} %shard_map.77.refs_0_), channel_id=1, source_target_pairs={{0,1},{1,0},{2,3},{3,2},{4,5},{5,4},{6,7},{7,6},{8,24},{9,25},{10,... | collective-permute-start | bytes 663560 | tf_op jit(solution)/shard_map/ppermute | solution.py:197
  16.0 2.4 %collective-permute-start.3 = (bf16[48,1152]{1,0:T(8,128)(2,1)}, bf16[48,1152]{1,0:T(8,128)(2,1)S(1)}, u32[]{:S(2)}, u32[]{:S(2)}) collective-permute-start(bf16[48,1152]{1,0:T(8,128)(2,1)} %images.1), channel_id=1, source_target_pairs={{0,6},{1,7},{2,4},{3,5},{4,2},{5,3},{6,0},{7,1},{8,14},{9,15},{10,... | collective-permute-start | bytes 331784 | tf_op jit(solution)/shard_map/ppermute | solution.py:187
  18.4 0.0 collective-permute-start.2
  18.4 2.0 %collective-permute-start.1 = (bf16[48,1152]{1,0:T(8,128)(2,1)}, bf16[48,1152]{1,0:T(8,128)(2,1)S(1)}, u32[]{:S(2)}, u32[]{:S(2)}) collective-permute-start(bf16[48,1152]{1,0:T(8,128)(2,1)} %images.1), channel_id=1, source_target_pairs={{0,2},{1,3},{2,0},{3,1},{4,6},{5,7},{6,4},{7,5},{8,10},{9,11},{10,... | collective-permute-start | bytes 331784 | tf_op jit(solution)/shard_map/ppermute | solution.py:187
  20.4 0.7 %collective-permute-done.5._.refs_1_ = bf16[96,1152]{1,0:T(8,128)(2,1)S(1)} collective-permute-done((bf16[96,1152]{1,0:T(8,128)(2,1)S(1)}, bf16[96,1152]{1,0:T(8,128)(2,1)S(1)}, u32[]{:S(2)}, u32[]{:S(2)}) %collective-permute-start.5) | collective-permute-done | bytes 221216 | tf_op jit(solution)/shard_map/ppermute | solution.py:197
  21.1 0.9 %collective-permute-start.11 = (bf16[192,640]{1,0:T(8,128)(2,1)S(1)}, bf16[192,640]{1,0:T(8,128)(2,1)S(1)}, u32[]{:S(2)}, u32[]{:S(2)}) collective-permute-start(bf16[192,640]{1,0:T(8,128)(2,1)S(1)} %shard_map.82.refs_0_), channel_id=1, source_target_pairs={{0,1},{1,0},{2,3},{3,2},{4,5},{5,4},{6,7},{7,6},{8,24},{9,25},{10,... | collective-permute-start | bytes 737288 | tf_op jit(solution)/shard_map/ppermute | solution.py:197
  22.0 0.0 collective-permute-done.10.refs_1_
  22.0 1.1 %collective-permute-start.12 = (bf16[192,640]{1,0:T(8,128)(2,1)S(1)}, bf16[192,640]{1,0:T(8,128)(2,1)S(1)}, u32[]{:S(2)}, u32[]{:S(2)}) collective-permute-start(bf16[192,640]{1,0:T(8,128)(2,1)S(1)} %collective-permute-done.10.refs_1_), channel_id=1, source_target_pairs={{0,1},{1,0},{2,3},{3,2},{4,5},{5,4},{6,7},{7,6},{8,24},{9,25},{10,... | collective-permute-start | bytes 737288 | tf_op jit(solution)/shard_map/ppermute | solution.py:197
  23.1 1.4 %copy-done = bf16[1152,640]{1,0:T(8,128)(2,1)S(1)} copy-done((bf16[1152,640]{1,0:T(8,128)(2,1)S(1)}, bf16[1152,640]{1,0:T(8,128)(2,1)}, u32[]{:S(2)}) %copy-start) | copy-done | bytes 1474584
  24.5 0.3 shard_map.78.weight
  24.8 2.7 %collective-permute-done.2.refs_1_ = bf16[48,1152]{1,0:T(8,128)(2,1)S(1)} collective-permute-done((bf16[48,1152]{1,0:T(8,128)(2,1)}, bf16[48,1152]{1,0:T(8,128)(2,1)S(1)}, u32[]{:S(2)}, u32[]{:S(2)}) %collective-permute-start.2) | collective-permute-done | bytes 110624 | tf_op jit(solution)/shard_map/ppermute | solution.py:187
  27.5 0.0 collective-permute-done.1.refs_0_
  27.6 0.7 %collective-permute-start.7 = (bf16[144,1152]{1,0:T(8,128)(2,1)S(1)}, bf16[144,1152]{1,0:T(8,128)(2,1)S(1)}, u32[]{:S(2)}, u32[]{:S(2)}) collective-permute-start(bf16[144,1152]{1,0:T(8,128)(2,1)S(1)} %shard_map.79.refs_2_), channel_id=1, source_target_pairs={{0,16},{1,17},{2,18},{3,19},{4,20},{5,21},{6,22},{7,23},{8,9},{9,8... | collective-permute-start | bytes 995336 | tf_op jit(solution)/shard_map/ppermute | solution.py:197
  28.3 0.1 pad_add_fusion.place
  28.4 0.1 shard_map.80.images.refs_0_
  28.4 0.9 %shard_map.81 = (f32[336,640]{1,0:T(8,128)S(1)}, bf16[336,640]{1,0:T(8,128)(2,1)S(1)}, f32[336,1]{1,0:T(8,128)S(1)}) custom-call(bf16[336,1152]{1,0:T(8,128)(2,1)S(1)} %shard_map.80.images.refs_0_, bf16[1152,640]{1,0:T(8,128)(2,1)S(1)} %shard_map.78.weight), custom_call_target="tpu_custom_call" | custom-call | tf_op jit(solution)/shard_map/pallas_call | solution.py:244
  29.4 0.7 %collective-permute-done.12.refs_3_ = bf16[192,640]{1,0:T(8,128)(2,1)S(1)} collective-permute-done((bf16[192,640]{1,0:T(8,128)(2,1)S(1)}, bf16[192,640]{1,0:T(8,128)(2,1)S(1)}, u32[]{:S(2)}, u32[]{:S(2)}) %collective-permute-start.12) | collective-permute-done | bytes 245792 | tf_op jit(solution)/shard_map/ppermute | solution.py:197
  30.1 0.9 %shard_map.83 = (bf16[256,640]{1,0:T(8,128)(2,1)S(1)}, bf16[256,640]{1,0:T(8,128)(2,1)S(1)}, bf16[256,640]{1,0:T(8,128)(2,1)S(1)}, bf16[768,640]{1,0:T(8,128)(2,1)S(1)}, s32[1,1536]{1,0:T(1,128)S(1)}) custom-call(s32[4]{0:T(128)S(1)} %pad_add_fusion.place, f32[336,1]{1,0:T(8,128)S(1)} %get-tuple-element.35._.refs_2_, ...), custom_call_target="tpu_custom_call" | custom-call | tf_op jit(solution)/shard_map/pallas_call | solution.py:255
  31.0 0.1 collective-permute-start.13
  31.1 0.5 collective-permute-start.14
  31.6 0.1 collective-permute-start.15
  31.7 0.7 %collective-permute-start.6 = (bf16[144,1152]{1,0:T(8,128)(2,1)S(1)}, bf16[144,1152]{1,0:T(8,128)(2,1)S(1)}, u32[]{:S(2)}, u32[]{:S(2)}) collective-permute-start(bf16[144,1152]{1,0:T(8,128)(2,1)S(1)} %shard_map.79.refs_2_), channel_id=1, source_target_pairs={{0,1},{1,0},{2,3},{3,2},{4,5},{5,4},{6,7},{7,6},{8,24},{9,25},{10,... | collective-permute-start | bytes 995336 | tf_op jit(solution)/shard_map/ppermute | solution.py:197
  32.3 2.4 %collective-permute-done.7.images.refs_1_ = bf16[144,1152]{1,0:T(8,128)(2,1)S(1)} collective-permute-done((bf16[144,1152]{1,0:T(8,128)(2,1)S(1)}, bf16[144,1152]{1,0:T(8,128)(2,1)S(1)}, u32[]{:S(2)}, u32[]{:S(2)}) %collective-permute-start.7) | collective-permute-done | bytes 331808 | tf_op jit(solution)/shard_map/ppermute | solution.py:197
  34.7 0.0 collective-permute-start.16
  34.8 1.4 %collective-permute-start.17 = (bf16[144,1152]{1,0:T(8,128)(2,1)S(1)}, bf16[144,1152]{1,0:T(8,128)(2,1)S(1)}, u32[]{:S(2)}, u32[]{:S(2)}) collective-permute-start(bf16[144,1152]{1,0:T(8,128)(2,1)S(1)} %collective-permute-done.7.images.refs_1_), channel_id=1, source_target_pairs={{0,1},{1,0},{2,3},{3,2},{4,5},{5,4},{6,7},{7,6},{8,24},{9,25},{10,... | collective-permute-start | bytes 995336 | tf_op jit(solution)/shard_map/ppermute | solution.py:197
  36.2 0.1 shard_map.84.txt_sib
  36.2 4.4 %shard_map.85 = (bf16[480,640]{1,0:T(8,128)(2,1)S(1)}, f32[48,640]{1,0:T(8,128)S(1)}, f32[48,640]{1,0:T(8,128)S(1)}) custom-call(s32[4]{0:T(128)S(1)} %pad_add_fusion.place, f32[1,128]{1,0:T(1,128)S(1)} %get-tuple-element.29.scale_ref.scale, f32[1,128]{1,0:T(1,128)S(1)} %get-tuple-element.31.bias_ref, ...), custom_call_target="tpu_custom_call" | custom-call | flops 1400000000 | tf_op jit(solution)/shard_map/pallas_call | solution.py:269
  40.7 0.6 %collective-permute-start.22 = (bf16[480,640]{1,0:T(8,128)(2,1)S(1)}, bf16[480,640]{1,0:T(8,128)(2,1)S(1)}, u32[]{:S(2)}, u32[]{:S(2)}) collective-permute-start(bf16[480,640]{1,0:T(8,128)(2,1)S(1)} %get-tuple-element.45.refs_2_.mine), channel_id=1, source_target_pairs={{0,8},{8,0},{16,24},{24,16},{1,9},{9,1},{17,25},{25,17},{2,10},{10... | collective-permute-start | bytes 1843208 | tf_op jit(solution)/shard_map/ppermute | solution.py:187
  41.3 1.1 %shard_map.86.refs_3_ = f32[1152,640]{1,0:T(8,128)S(1)} custom-call(bf16[336,1152]{1,0:T(8,128)(2,1)S(1)} %shard_map.80.images.refs_0_, bf16[144,1152]{1,0:T(8,128)(2,1)S(1)} %collective-permute-done.7.images.refs_1_, bf16[480,640]{1,0:T(8,128)(2,1)S(1)} %get-tuple-element.45.refs_2_.mine), custom_call_target="tpu_custom_call" | custom-call | tf_op jit(solution)/shard_map/pallas_call | solution.py:289
  42.4 0.1 shard_map.87.images.refs_0_
  42.5 0.5 collective-permute-start.19
  43.0 3.6 %shard_map.88 = (bf16[288,640]{1,0:T(8,128)(2,1)S(1)}, f32[48,640]{1,0:T(8,128)S(1)}, f32[48,640]{1,0:T(8,128)S(1)}) custom-call(s32[4]{0:T(128)S(1)} %pad_add_fusion.place, f32[1,128]{1,0:T(1,128)S(1)} %get-tuple-element.29.scale_ref.scale, f32[1,128]{1,0:T(1,128)S(1)} %get-tuple-element.31.bias_ref, bf16[288,1152]{1,0:T(8,128)(2,1)S(1)} %shard_map.87.images.refs_0_, ...), custom_call_target="tpu_custom_call" | custom-call | flops 6000000000 | tf_op jit(solution)/shard_map/pallas_call | solution.py:269
  46.6 0.2 collective-permute-start.20
  46.8 0.4 collective-permute-start.18
  47.2 1.2 %shard_map.89.refs_4_ = f32[1152,640]{1,0:T(8,128)S(1)} custom-call(bf16[336,1152]{1,0:T(8,128)(2,1)S(1)} %collective-permute-done.21.refs_0_, bf16[144,1152]{1,0:T(8,128)(2,1)S(1)} %collective-permute-done.16.refs_1_, bf16[480,640]{1,0:T(8,128)(2,1)S(1)} %collective-permute-done.22.refs_2_, f32[1152,640]{1,0:T(8,128)S(1)} %shard_map.86.refs_3_), custom_call_target="tpu_custom_call" | custom-call | tf_op jit(solution)/shard_map/pallas_call | solution.py:289
  48.3 0.2 collective-permute-done.18.received
  48.5 2.9 %shard_map.90 = (f32[1152,640]{1,0:T(8,128)}, bf16[48,640]{1,0:T(8,128)(2,1)}, bf16[48,1152]{1,0:T(8,128)(2,1)}) custom-call(f32[1,128]{1,0:T(1,128)S(1)} %get-tuple-element.29.scale_ref.scale, bf16[48,640]{1,0:T(8,128)(2,1)S(1)} %get-tuple-element.30.refs_0_.texts, f32[48,640]{1,0:T(8,128)S(1)} %get-tuple-element.49.own, ...), custom_call_target="tpu_custom_call" | custom-call | tf_op jit(solution)/shard_map/pallas_call | solution.py:302
  (20 shorter events, 0.1 us)
Async XLA Ops:
  0.6 11.3 %collective-permute-start.4 = (bf16[48,1152]{1,0:T(8,128)(2,1)}, bf16[48,1152]{1,0:T(8,128)(2,1)S(1)}, u32[]{:S(2)}, u32[]{:S(2)}) collective-permute-start(bf16[48,1152]{1,0:T(8,128)(2,1)} %images.1), channel_id=1, source_target_pairs={{0,16},{1,17},{2,18},{3,19},{4,20},{5,21},{6,22},{7,23},{8,9},{9,8... | collective-permute-start | bytes 331784 | tf_op jit(solution)/shard_map/ppermute | solution.py:197
  3.6 5.5 %collective-permute-start = (bf16[48,640]{1,0:T(8,128)(2,1)}, bf16[48,640]{1,0:T(8,128)(2,1)S(1)}, u32[]{:S(2)}, u32[]{:S(2)}) collective-permute-start(bf16[48,640]{1,0:T(8,128)(2,1)} %texts.1), channel_id=1, source_target_pairs={{0,2},{1,3},{2,0},{3,1},{4,6},{5,7},{6,4},{7,5},{8,10},{9,11},{10,... | collective-permute-start | bytes 184328 | tf_op jit(solution)/shard_map/ppermute | solution.py:187
  5.2 6.7 %collective-permute-start.9 = (bf16[48,640]{1,0:T(8,128)(2,1)}, bf16[48,640]{1,0:T(8,128)(2,1)S(1)}, u32[]{:S(2)}, u32[]{:S(2)}) collective-permute-start(bf16[48,640]{1,0:T(8,128)(2,1)} %texts.1), channel_id=1, source_target_pairs={{0,6},{1,7},{2,4},{3,5},{4,2},{5,3},{6,0},{7,1},{8,14},{9,15},{10,... | collective-permute-start | bytes 184328 | tf_op jit(solution)/shard_map/ppermute | solution.py:187
  7.7 6.1 %collective-permute-start.8 = (bf16[48,640]{1,0:T(8,128)(2,1)}, bf16[48,640]{1,0:T(8,128)(2,1)S(1)}, u32[]{:S(2)}, u32[]{:S(2)}) collective-permute-start(bf16[48,640]{1,0:T(8,128)(2,1)} %texts.1), channel_id=1, source_target_pairs={{0,4},{1,5},{2,6},{3,7},{4,0},{5,1},{6,2},{7,3},{8,12},{9,13},{10,... | collective-permute-start | bytes 184328 | tf_op jit(solution)/shard_map/ppermute | solution.py:187
  9.1 0.9 %copy-start.1 = (bf16[48,1152]{1,0:T(8,128)(2,1)S(1)}, bf16[48,1152]{1,0:T(8,128)(2,1)}, u32[]{:S(2)}) copy-start(bf16[48,1152]{1,0:T(8,128)(2,1)} %images.1) | copy-start | bytes 331780
  10.0 0.8 %copy-start.2 = (bf16[48,640]{1,0:T(8,128)(2,1)S(1)}, bf16[48,640]{1,0:T(8,128)(2,1)}, u32[]{:S(2)}) copy-start(bf16[48,640]{1,0:T(8,128)(2,1)} %texts.1) | copy-start | bytes 184324
  13.8 8.1 %collective-permute-start.10 = (bf16[192,640]{1,0:T(8,128)(2,1)S(1)}, bf16[192,640]{1,0:T(8,128)(2,1)S(1)}, u32[]{:S(2)}, u32[]{:S(2)}) collective-permute-start(bf16[192,640]{1,0:T(8,128)(2,1)S(1)} %shard_map.82.refs_0_), channel_id=1, source_target_pairs={{0,16},{1,17},{2,18},{3,19},{4,20},{5,21},{6,22},{7,23},{8,9},{9,8... | collective-permute-start | bytes 737288 | tf_op jit(solution)/shard_map/ppermute | solution.py:197
  15.1 6.0 %collective-permute-start.5 = (bf16[96,1152]{1,0:T(8,128)(2,1)S(1)}, bf16[96,1152]{1,0:T(8,128)(2,1)S(1)}, u32[]{:S(2)}, u32[]{:S(2)}) collective-permute-start(bf16[96,1152]{1,0:T(8,128)(2,1)S(1)} %shard_map.77.refs_0_), channel_id=1, source_target_pairs={{0,1},{1,0},{2,3},{3,2},{4,5},{5,4},{6,7},{7,6},{8,24},{9,25},{10,... | collective-permute-start | bytes 663560 | tf_op jit(solution)/shard_map/ppermute | solution.py:197
  16.0 8.8 %collective-permute-start.3 = (bf16[48,1152]{1,0:T(8,128)(2,1)}, bf16[48,1152]{1,0:T(8,128)(2,1)S(1)}, u32[]{:S(2)}, u32[]{:S(2)}) collective-permute-start(bf16[48,1152]{1,0:T(8,128)(2,1)} %images.1), channel_id=1, source_target_pairs={{0,6},{1,7},{2,4},{3,5},{4,2},{5,3},{6,0},{7,1},{8,14},{9,15},{10,... | collective-permute-start | bytes 331784 | tf_op jit(solution)/shard_map/ppermute | solution.py:187
  18.4 9.2 %collective-permute-start.2 = (bf16[48,1152]{1,0:T(8,128)(2,1)}, bf16[48,1152]{1,0:T(8,128)(2,1)S(1)}, u32[]{:S(2)}, u32[]{:S(2)}) collective-permute-start(bf16[48,1152]{1,0:T(8,128)(2,1)} %images.1), channel_id=1, source_target_pairs={{0,4},{1,5},{2,6},{3,7},{4,0},{5,1},{6,2},{7,3},{8,12},{9,13},{10,... | collective-permute-start | bytes 331784 | tf_op jit(solution)/shard_map/ppermute | solution.py:187
  18.4 9.2 %collective-permute-start.1 = (bf16[48,1152]{1,0:T(8,128)(2,1)}, bf16[48,1152]{1,0:T(8,128)(2,1)S(1)}, u32[]{:S(2)}, u32[]{:S(2)}) collective-permute-start(bf16[48,1152]{1,0:T(8,128)(2,1)} %images.1), channel_id=1, source_target_pairs={{0,2},{1,3},{2,0},{3,1},{4,6},{5,7},{6,4},{7,5},{8,10},{9,11},{10,... | collective-permute-start | bytes 331784 | tf_op jit(solution)/shard_map/ppermute | solution.py:187
  21.1 8.3 %collective-permute-start.11 = (bf16[192,640]{1,0:T(8,128)(2,1)S(1)}, bf16[192,640]{1,0:T(8,128)(2,1)S(1)}, u32[]{:S(2)}, u32[]{:S(2)}) collective-permute-start(bf16[192,640]{1,0:T(8,128)(2,1)S(1)} %shard_map.82.refs_0_), channel_id=1, source_target_pairs={{0,1},{1,0},{2,3},{3,2},{4,5},{5,4},{6,7},{7,6},{8,24},{9,25},{10,... | collective-permute-start | bytes 737288 | tf_op jit(solution)/shard_map/ppermute | solution.py:197
  22.0 8.2 %collective-permute-start.12 = (bf16[192,640]{1,0:T(8,128)(2,1)S(1)}, bf16[192,640]{1,0:T(8,128)(2,1)S(1)}, u32[]{:S(2)}, u32[]{:S(2)}) collective-permute-start(bf16[192,640]{1,0:T(8,128)(2,1)S(1)} %collective-permute-done.10.refs_1_), channel_id=1, source_target_pairs={{0,1},{1,0},{2,3},{3,2},{4,5},{5,4},{6,7},{7,6},{8,24},{9,25},{10,... | collective-permute-start | bytes 737288 | tf_op jit(solution)/shard_map/ppermute | solution.py:197
  23.1 1.4 %copy-start = (bf16[1152,640]{1,0:T(8,128)(2,1)S(1)}, bf16[1152,640]{1,0:T(8,128)(2,1)}, u32[]{:S(2)}) copy-start(bf16[1152,640]{1,0:T(8,128)(2,1)} %array.1) | copy-start | bytes 4423684
  27.6 7.2 %collective-permute-start.7 = (bf16[144,1152]{1,0:T(8,128)(2,1)S(1)}, bf16[144,1152]{1,0:T(8,128)(2,1)S(1)}, u32[]{:S(2)}, u32[]{:S(2)}) collective-permute-start(bf16[144,1152]{1,0:T(8,128)(2,1)S(1)} %shard_map.79.refs_2_), channel_id=1, source_target_pairs={{0,16},{1,17},{2,18},{3,19},{4,20},{5,21},{6,22},{7,23},{8,9},{9,8... | collective-permute-start | bytes 995336 | tf_op jit(solution)/shard_map/ppermute | solution.py:197
  31.0 3.8 %collective-permute-start.13 = (bf16[256,640]{1,0:T(8,128)(2,1)S(1)}, bf16[256,640]{1,0:T(8,128)(2,1)S(1)}, u32[]{:S(2)}, u32[]{:S(2)}) collective-permute-start(bf16[256,640]{1,0:T(8,128)(2,1)S(1)} %get-tuple-element.39), channel_id=1, source_target_pairs={{0,8},{8,0},{16,24},{24,16},{1,9},{9,1},{17,25},{25,17},{2,10},{10... | collective-permute-start | bytes 983048 | tf_op jit(solution)/shard_map/ppermute | solution.py:187
  31.1 5.1 %collective-permute-start.14 = (bf16[256,640]{1,0:T(8,128)(2,1)S(1)}, bf16[256,640]{1,0:T(8,128)(2,1)S(1)}, u32[]{:S(2)}, u32[]{:S(2)}) collective-permute-start(bf16[256,640]{1,0:T(8,128)(2,1)S(1)} %get-tuple-element.40), channel_id=1, source_target_pairs={{0,8},{8,0},{16,24},{24,16},{1,9},{9,1},{17,25},{25,17},{2,10},{10... | collective-permute-start | bytes 983048 | tf_op jit(solution)/shard_map/ppermute | solution.py:187
  31.6 4.6 %collective-permute-start.15 = (bf16[256,640]{1,0:T(8,128)(2,1)S(1)}, bf16[256,640]{1,0:T(8,128)(2,1)S(1)}, u32[]{:S(2)}, u32[]{:S(2)}) collective-permute-start(bf16[256,640]{1,0:T(8,128)(2,1)S(1)} %get-tuple-element.41), channel_id=1, source_target_pairs={{0,8},{8,0},{16,24},{24,16},{1,9},{9,1},{17,25},{25,17},{2,10},{10... | collective-permute-start | bytes 983048 | tf_op jit(solution)/shard_map/ppermute | solution.py:187
  31.7 10.7 %collective-permute-start.6 = (bf16[144,1152]{1,0:T(8,128)(2,1)S(1)}, bf16[144,1152]{1,0:T(8,128)(2,1)S(1)}, u32[]{:S(2)}, u32[]{:S(2)}) collective-permute-start(bf16[144,1152]{1,0:T(8,128)(2,1)S(1)} %shard_map.79.refs_2_), channel_id=1, source_target_pairs={{0,1},{1,0},{2,3},{3,2},{4,5},{5,4},{6,7},{7,6},{8,24},{9,25},{10,... | collective-permute-start | bytes 995336 | tf_op jit(solution)/shard_map/ppermute | solution.py:197
  34.7 7.7 %collective-permute-start.16 = (bf16[144,1152]{1,0:T(8,128)(2,1)S(1)}, bf16[144,1152]{1,0:T(8,128)(2,1)S(1)}, u32[]{:S(2)}, u32[]{:S(2)}) collective-permute-start(bf16[144,1152]{1,0:T(8,128)(2,1)S(1)} %collective-permute-done.7.images.refs_1_), channel_id=1, source_target_pairs={{0,8},{8,0},{16,24},{24,16},{1,9},{9,1},{17,25},{25,17},{2,10},{10... | collective-permute-start | bytes 995336 | tf_op jit(solution)/shard_map/ppermute | solution.py:187
  34.8 7.6 %collective-permute-start.17 = (bf16[144,1152]{1,0:T(8,128)(2,1)S(1)}, bf16[144,1152]{1,0:T(8,128)(2,1)S(1)}, u32[]{:S(2)}, u32[]{:S(2)}) collective-permute-start(bf16[144,1152]{1,0:T(8,128)(2,1)S(1)} %collective-permute-done.7.images.refs_1_), channel_id=1, source_target_pairs={{0,1},{1,0},{2,3},{3,2},{4,5},{5,4},{6,7},{7,6},{8,24},{9,25},{10,... | collective-permute-start | bytes 995336 | tf_op jit(solution)/shard_map/ppermute | solution.py:197
  36.2 11.0 %collective-permute-start.21 = (bf16[336,1152]{1,0:T(8,128)(2,1)S(1)}, bf16[336,1152]{1,0:T(8,128)(2,1)S(1)}, u32[]{:S(2)}, u32[]{:S(2)}) collective-permute-start(bf16[336,1152]{1,0:T(8,128)(2,1)S(1)} %shard_map.80.images.refs_0_), channel_id=1, source_target_pairs={{0,8},{8,0},{16,24},{24,16},{1,9},{9,1},{17,25},{25,17},{2,10},{10... | collective-permute-start | bytes 2322440 | tf_op jit(solution)/shard_map/ppermute | solution.py:187
  40.7 6.5 %collective-permute-start.22 = (bf16[480,640]{1,0:T(8,128)(2,1)S(1)}, bf16[480,640]{1,0:T(8,128)(2,1)S(1)}, u32[]{:S(2)}, u32[]{:S(2)}) collective-permute-start(bf16[480,640]{1,0:T(8,128)(2,1)S(1)} %get-tuple-element.45.refs_2_.mine), channel_id=1, source_target_pairs={{0,8},{8,0},{16,24},{24,16},{1,9},{9,1},{17,25},{25,17},{2,10},{10... | collective-permute-start | bytes 1843208 | tf_op jit(solution)/shard_map/ppermute | solution.py:187
  42.5 6.0 %collective-permute-start.19 = (bf16[288,1152]{1,0:T(8,128)(2,1)S(1)}, bf16[288,1152]{1,0:T(8,128)(2,1)S(1)}, u32[]{:S(2)}, u32[]{:S(2)}) collective-permute-start(bf16[288,1152]{1,0:T(8,128)(2,1)S(1)} %shard_map.87.images.refs_0_), channel_id=1, source_target_pairs={{0,8},{8,0},{16,24},{24,16},{1,9},{9,1},{17,25},{25,17},{2,10},{10... | collective-permute-start | bytes 1990664 | tf_op jit(solution)/shard_map/ppermute | solution.py:187
  46.6 1.9 %collective-permute-start.20 = (bf16[288,640]{1,0:T(8,128)(2,1)S(1)}, bf16[288,640]{1,0:T(8,128)(2,1)S(1)}, u32[]{:S(2)}, u32[]{:S(2)}) collective-permute-start(bf16[288,640]{1,0:T(8,128)(2,1)S(1)} %get-tuple-element.51.refs_2_), channel_id=1, source_target_pairs={{0,8},{8,0},{16,24},{24,16},{1,9},{9,1},{17,25},{25,17},{2,10},{10... | collective-permute-start | bytes 1105928 | tf_op jit(solution)/shard_map/ppermute | solution.py:187
  46.8 1.7 %collective-permute-start.18 = (f32[48,640]{1,0:T(8,128)S(1)}, f32[48,640]{1,0:T(8,128)S(1)}, u32[]{:S(2)}, u32[]{:S(2)}) collective-permute-start(f32[48,640]{1,0:T(8,128)S(1)} %get-tuple-element.50), channel_id=1, source_target_pairs={{0,8},{8,0},{16,24},{24,16},{1,9},{9,1},{17,25},{25,17},{2,10},{10... | collective-permute-start | bytes 368648 | tf_op jit(solution)/shard_map/ppermute | solution.py:187

commit v5 on v4

--- a/solution.py
+++ b/solution.py
@@ -251,10 +251,10 @@
         [VMEM] * 2,
         0,
     )(ready, weight)
-    third = total // 3
+    third = total // 2
     *sent, txt_own, col_ids = call(
         functools.partial(unit_body, order, n_img),
-        [shape(third, texts)] * 3 + [shape(total, texts), jax.ShapeDtypeStruct((1, 2 * total), jnp.int32)],
+        [shape(third, texts)] * 2 + [shape(total, texts), jax.ShapeDtypeStruct((1, 2 * total), jnp.int32)],
         [SMEM, ANY] + [VMEM] * len(txt_parts),
         0,
     )(place, ready_hidden[2], *txt_parts)
@@ -280,7 +280,7 @@
 
     d_early, own, sib = batch(near, early_order, 1_400_000_000, ready_hidden)
     d_early_sib = core(d_early)
-    early_sib = [core(ready), core(near)]
+    early_sib = [core(after(ready, d_early)), core(near)]
     head = jax.ShapeDtypeStruct((emb, features), f32)
 
     def head_terms(images, d_hidden, *before):

time: 51.9 us -> 51.9 us (level)
    ppermute x15 -> x14, starting transfers between devices: 10.8 us -> 10.4 us  [move(): return lax.ppermute(array, axis, [(i, i ^ mask) for i in range(size)])]
    ppermute x15 -> x14, waiting for transfers between devices: 5.89 us -> 5.94 us  [move(): return lax.ppermute(array, axis, [(i, i ^ mask) for i in range(size)])]
  transfers between devices with their start and end apart: 23 -> 22, of which waited for: 7 -> 7; matrix products, arithmetic and copies ran while one was open for 0% -> 0% of each run, Pallas kernels for 25% -> 25%
where the time goes in v5:
time: 51.9 us; the launch traced here: 51.6 us
  starting transfers between devices  20.8 us (40%)
  Pallas kernels  15.7 us (30%)
  waiting for transfers between devices  9.81 us (19%)
  local copies, waits for them, and re-layouts  3.09 us (6%)
  between operations  2.1 us (4%)
    ppermute x8, starting transfers between devices, link(): return lax.ppermute(array, ('img', 'txt'), pairs)  10.4 us
    ppermute x14, starting transfers between devices, move(): return lax.ppermute(array, axis, [(i, i ^ mask) for i in range(size)])  10.4 us
    pallas_call x2, Pallas kernels, batch(): call(functools.partial(batch_body, first, order, n_txt), [shape(held, tex...  8.12 us
    ppermute x14, waiting for transfers between devices, move(): return lax.ppermute(array, axis, [(i, i ^ mask) for i in range(size)])  5.94 us
    ppermute x8, waiting for transfers between devices, link(): return lax.ppermute(array, ('img', 'txt'), pairs)  3.88 us
    unnamed x6, local copies, waits for them, and re-layouts  3.09 us
    pallas_call x1, Pallas kernels, gathered(): pl.pallas_call(functools.partial(last_body, len(left), len(right), sizes)...  2.87 us
    pallas_call x2, Pallas kernels, head_terms(): return call(body, head, [VMEM] * len(refs), 0)(*refs)  2.3 us
  transfers between devices with their start and end apart: 22, of which 7 were waited for; matrix products, arithmetic and copies ran while one was open for 0% of the time, Pallas kernels for 25%

profile of v5, /device:TPU:0, one launch (start us, length us, event | category | flops | bytes accessed | tf_op | source)
XLA Modules:
  0.0 51.6 jit_solution(1920266602894126720)
XLA Ops:
  0.6 3.0 %collective-permute-start.4 = (bf16[48,1152]{1,0:T(8,128)(2,1)}, bf16[48,1152]{1,0:T(8,128)(2,1)S(1)}, u32[]{:S(2)}, u32[]{:S(2)}) collective-permute-start(bf16[48,1152]{1,0:T(8,128)(2,1)} %images.1), channel_id=1, source_target_pairs={{0,16},{1,17},{2,18},{3,19},{4,20},{5,21},{6,22},{7,23},{8,9},{9,8... | collective-permute-start | bytes 331784 | tf_op jit(solution)/shard_map/ppermute | solution.py:197
  3.6 1.6 %collective-permute-start = (bf16[48,640]{1,0:T(8,128)(2,1)}, bf16[48,640]{1,0:T(8,128)(2,1)S(1)}, u32[]{:S(2)}, u32[]{:S(2)}) collective-permute-start(bf16[48,640]{1,0:T(8,128)(2,1)} %texts.1), channel_id=1, source_target_pairs={{0,2},{1,3},{2,0},{3,1},{4,6},{5,7},{6,4},{7,5},{8,10},{9,11},{10,... | collective-permute-start | bytes 184328 | tf_op jit(solution)/shard_map/ppermute | solution.py:187
  5.2 2.5 %collective-permute-start.9 = (bf16[48,640]{1,0:T(8,128)(2,1)}, bf16[48,640]{1,0:T(8,128)(2,1)S(1)}, u32[]{:S(2)}, u32[]{:S(2)}) collective-permute-start(bf16[48,640]{1,0:T(8,128)(2,1)} %texts.1), channel_id=1, source_target_pairs={{0,6},{1,7},{2,4},{3,5},{4,2},{5,3},{6,0},{7,1},{8,14},{9,15},{10,... | collective-permute-start | bytes 184328 | tf_op jit(solution)/shard_map/ppermute | solution.py:187
  7.7 0.1 collective-permute-start.8
  9.1 0.0 copy-start.1
  9.1 0.9 %copy-done.1 = bf16[48,1152]{1,0:T(8,128)(2,1)S(1)} copy-done((bf16[48,1152]{1,0:T(8,128)(2,1)S(1)}, bf16[48,1152]{1,0:T(8,128)(2,1)}, u32[]{:S(2)}) %copy-start.1) | copy-done | bytes 110616
  10.0 0.8 %copy-done.2 = bf16[48,640]{1,0:T(8,128)(2,1)S(1)} copy-done((bf16[48,640]{1,0:T(8,128)(2,1)S(1)}, bf16[48,640]{1,0:T(8,128)(2,1)}, u32[]{:S(2)}) %copy-start.2) | copy-done | bytes 61464
  10.9 1.1 %collective-permute-done.9.refs_3_ = bf16[48,640]{1,0:T(8,128)(2,1)S(1)} collective-permute-done((bf16[48,640]{1,0:T(8,128)(2,1)}, bf16[48,640]{1,0:T(8,128)(2,1)S(1)}, u32[]{:S(2)}, u32[]{:S(2)}) %collective-permute-start.9) | collective-permute-done | bytes 61472 | tf_op jit(solution)/shard_map/ppermute | solution.py:187
  11.9 0.0 collective-permute-done.4.refs_1_
  12.0 1.9 %collective-permute-done.8.refs_2_ = bf16[48,640]{1,0:T(8,128)(2,1)S(1)} collective-permute-done((bf16[48,640]{1,0:T(8,128)(2,1)}, bf16[48,640]{1,0:T(8,128)(2,1)S(1)}, u32[]{:S(2)}, u32[]{:S(2)}) %collective-permute-start.8) | collective-permute-done | bytes 61472 | tf_op jit(solution)/shard_map/ppermute | solution.py:187
  13.8 1.2 %collective-permute-start.10 = (bf16[192,640]{1,0:T(8,128)(2,1)S(1)}, bf16[192,640]{1,0:T(8,128)(2,1)S(1)}, u32[]{:S(2)}, u32[]{:S(2)}) collective-permute-start(bf16[192,640]{1,0:T(8,128)(2,1)S(1)} %shard_map.82.refs_0_), channel_id=1, source_target_pairs={{0,16},{1,17},{2,18},{3,19},{4,20},{5,21},{6,22},{7,23},{8,9},{9,8... | collective-permute-start | bytes 737288 | tf_op jit(solution)/shard_map/ppermute | solution.py:197
  15.1 1.0 %collective-permute-start.5 = (bf16[96,1152]{1,0:T(8,128)(2,1)S(1)}, bf16[96,1152]{1,0:T(8,128)(2,1)S(1)}, u32[]{:S(2)}, u32[]{:S(2)}) collective-permute-start(bf16[96,1152]{1,0:T(8,128)(2,1)S(1)} %shard_map.77.refs_0_), channel_id=1, source_target_pairs={{0,1},{1,0},{2,3},{3,2},{4,5},{5,4},{6,7},{7,6},{8,24},{9,25},{10,... | collective-permute-start | bytes 663560 | tf_op jit(solution)/shard_map/ppermute | solution.py:197
  16.0 2.4 %collective-permute-start.3 = (bf16[48,1152]{1,0:T(8,128)(2,1)}, bf16[48,1152]{1,0:T(8,128)(2,1)S(1)}, u32[]{:S(2)}, u32[]{:S(2)}) collective-permute-start(bf16[48,1152]{1,0:T(8,128)(2,1)} %images.1), channel_id=1, source_target_pairs={{0,6},{1,7},{2,4},{3,5},{4,2},{5,3},{6,0},{7,1},{8,14},{9,15},{10,... | collective-permute-start | bytes 331784 | tf_op jit(solution)/shard_map/ppermute | solution.py:187
  18.4 2.0 %collective-permute-start.1 = (bf16[48,1152]{1,0:T(8,128)(2,1)}, bf16[48,1152]{1,0:T(8,128)(2,1)S(1)}, u32[]{:S(2)}, u32[]{:S(2)}) collective-permute-start(bf16[48,1152]{1,0:T(8,128)(2,1)} %images.1), channel_id=1, source_target_pairs={{0,2},{1,3},{2,0},{3,1},{4,6},{5,7},{6,4},{7,5},{8,10},{9,11},{10,... | collective-permute-start | bytes 331784 | tf_op jit(solution)/shard_map/ppermute | solution.py:187
  20.4 0.7 %collective-permute-done.5._.refs_1_ = bf16[96,1152]{1,0:T(8,128)(2,1)S(1)} collective-permute-done((bf16[96,1152]{1,0:T(8,128)(2,1)S(1)}, bf16[96,1152]{1,0:T(8,128)(2,1)S(1)}, u32[]{:S(2)}, u32[]{:S(2)}) %collective-permute-start.5) | collective-permute-done | bytes 221216 | tf_op jit(solution)/shard_map/ppermute | solution.py:197
  21.1 0.9 %collective-permute-start.11 = (bf16[192,640]{1,0:T(8,128)(2,1)S(1)}, bf16[192,640]{1,0:T(8,128)(2,1)S(1)}, u32[]{:S(2)}, u32[]{:S(2)}) collective-permute-start(bf16[192,640]{1,0:T(8,128)(2,1)S(1)} %shard_map.82.refs_0_), channel_id=1, source_target_pairs={{0,1},{1,0},{2,3},{3,2},{4,5},{5,4},{6,7},{7,6},{8,24},{9,25},{10,... | collective-permute-start | bytes 737288 | tf_op jit(solution)/shard_map/ppermute | solution.py:197
  22.0 0.0 collective-permute-done.10.refs_1_
  22.0 1.1 %collective-permute-start.12 = (bf16[192,640]{1,0:T(8,128)(2,1)S(1)}, bf16[192,640]{1,0:T(8,128)(2,1)S(1)}, u32[]{:S(2)}, u32[]{:S(2)}) collective-permute-start(bf16[192,640]{1,0:T(8,128)(2,1)S(1)} %collective-permute-done.10.refs_1_), channel_id=1, source_target_pairs={{0,1},{1,0},{2,3},{3,2},{4,5},{5,4},{6,7},{7,6},{8,24},{9,25},{10,... | collective-permute-start | bytes 737288 | tf_op jit(solution)/shard_map/ppermute | solution.py:197
  23.1 1.4 %copy-done = bf16[1152,640]{1,0:T(8,128)(2,1)S(1)} copy-done((bf16[1152,640]{1,0:T(8,128)(2,1)S(1)}, bf16[1152,640]{1,0:T(8,128)(2,1)}, u32[]{:S(2)}) %copy-start) | copy-done | bytes 1474584
  24.5 0.3 shard_map.78.weight
  24.8 2.7 %collective-permute-done.2.refs_1_ = bf16[48,1152]{1,0:T(8,128)(2,1)S(1)} collective-permute-done((bf16[48,1152]{1,0:T(8,128)(2,1)}, bf16[48,1152]{1,0:T(8,128)(2,1)S(1)}, u32[]{:S(2)}, u32[]{:S(2)}) %collective-permute-start.2) | collective-permute-done | bytes 110624 | tf_op jit(solution)/shard_map/ppermute | solution.py:187
  27.6 0.7 %collective-permute-start.7 = (bf16[144,1152]{1,0:T(8,128)(2,1)S(1)}, bf16[144,1152]{1,0:T(8,128)(2,1)S(1)}, u32[]{:S(2)}, u32[]{:S(2)}) collective-permute-start(bf16[144,1152]{1,0:T(8,128)(2,1)S(1)} %shard_map.79.refs_2_), channel_id=1, source_target_pairs={{0,16},{1,17},{2,18},{3,19},{4,20},{5,21},{6,22},{7,23},{8,9},{9,8... | collective-permute-start | bytes 995336 | tf_op jit(solution)/shard_map/ppermute | solution.py:197
  28.3 0.1 pad_add_fusion.place
  28.4 0.1 shard_map.80.images.refs_0_
  28.4 0.9 %shard_map.81 = (f32[336,640]{1,0:T(8,128)S(1)}, bf16[336,640]{1,0:T(8,128)(2,1)S(1)}, f32[336,1]{1,0:T(8,128)S(1)}) custom-call(bf16[336,1152]{1,0:T(8,128)(2,1)S(1)} %shard_map.80.images.refs_0_, bf16[1152,640]{1,0:T(8,128)(2,1)S(1)} %shard_map.78.weight), custom_call_target="tpu_custom_call" | custom-call | tf_op jit(solution)/shard_map/pallas_call | solution.py:244
  29.4 0.7 %collective-permute-done.12.refs_3_ = bf16[192,640]{1,0:T(8,128)(2,1)S(1)} collective-permute-done((bf16[192,640]{1,0:T(8,128)(2,1)S(1)}, bf16[192,640]{1,0:T(8,128)(2,1)S(1)}, u32[]{:S(2)}, u32[]{:S(2)}) %collective-permute-start.12) | collective-permute-done | bytes 245792 | tf_op jit(solution)/shard_map/ppermute | solution.py:197
  30.1 0.9 %shard_map.83 = (bf16[384,640]{1,0:T(8,128)(2,1)S(1)}, bf16[384,640]{1,0:T(8,128)(2,1)S(1)}, bf16[768,640]{1,0:T(8,128)(2,1)S(1)}, s32[1,1536]{1,0:T(1,128)S(1)}) custom-call(s32[4]{0:T(128)S(1)} %pad_add_fusion.place, f32[336,1]{1,0:T(8,128)S(1)} %get-tuple-element.35._.refs_2_, bf16[192,640]{1,0:T(8,128)(2,1)S(1)} %shard_map.82.refs_0_, ...), custom_call_target="tpu_custom_call" | custom-call | tf_op jit(solution)/shard_map/pallas_call | solution.py:255
  31.0 0.1 collective-permute-start.13
  31.1 0.5 collective-permute-start.14
  31.6 0.7 %collective-permute-start.6 = (bf16[144,1152]{1,0:T(8,128)(2,1)S(1)}, bf16[144,1152]{1,0:T(8,128)(2,1)S(1)}, u32[]{:S(2)}, u32[]{:S(2)}) collective-permute-start(bf16[144,1152]{1,0:T(8,128)(2,1)S(1)} %shard_map.79.refs_2_), channel_id=1, source_target_pairs={{0,1},{1,0},{2,3},{3,2},{4,5},{5,4},{6,7},{7,6},{8,24},{9,25},{10,... | collective-permute-start | bytes 995336 | tf_op jit(solution)/shard_map/ppermute | solution.py:197
  32.3 2.5 %collective-permute-done.7.images.refs_1_ = bf16[144,1152]{1,0:T(8,128)(2,1)S(1)} collective-permute-done((bf16[144,1152]{1,0:T(8,128)(2,1)S(1)}, bf16[144,1152]{1,0:T(8,128)(2,1)S(1)}, u32[]{:S(2)}, u32[]{:S(2)}) %collective-permute-start.7) | collective-permute-done | bytes 331808 | tf_op jit(solution)/shard_map/ppermute | solution.py:197
  34.7 0.0 collective-permute-start.15
  34.8 1.8 %collective-permute-start.16 = (bf16[144,1152]{1,0:T(8,128)(2,1)S(1)}, bf16[144,1152]{1,0:T(8,128)(2,1)S(1)}, u32[]{:S(2)}, u32[]{:S(2)}) collective-permute-start(bf16[144,1152]{1,0:T(8,128)(2,1)S(1)} %collective-permute-done.7.images.refs_1_), channel_id=1, source_target_pairs={{0,1},{1,0},{2,3},{3,2},{4,5},{5,4},{6,7},{7,6},{8,24},{9,25},{10,... | collective-permute-start | bytes 995336 | tf_op jit(solution)/shard_map/ppermute | solution.py:197
  36.6 0.0 collective-permute-done.13.refs_0_
  36.6 0.0 collective-permute-done.14.refs_1_
  36.6 0.1 shard_map.84.txt_sib
  36.7 4.5 %shard_map.85 = (bf16[480,640]{1,0:T(8,128)(2,1)S(1)}, f32[48,640]{1,0:T(8,128)S(1)}, f32[48,640]{1,0:T(8,128)S(1)}) custom-call(s32[4]{0:T(128)S(1)} %pad_add_fusion.place, f32[1,128]{1,0:T(1,128)S(1)} %get-tuple-element.29.scale_ref.scale, f32[1,128]{1,0:T(1,128)S(1)} %get-tuple-element.31.bias_ref, ...), custom_call_target="tpu_custom_call" | custom-call | flops 1400000000 | tf_op jit(solution)/shard_map/pallas_call | solution.py:269
  41.1 0.1 collective-permute-start.21
  41.2 0.5 collective-permute-start.20
  41.7 1.1 %shard_map.86.refs_3_ = f32[1152,640]{1,0:T(8,128)S(1)} custom-call(bf16[336,1152]{1,0:T(8,128)(2,1)S(1)} %shard_map.80.images.refs_0_, bf16[144,1152]{1,0:T(8,128)(2,1)S(1)} %collective-permute-done.7.images.refs_1_, bf16[480,640]{1,0:T(8,128)(2,1)S(1)} %get-tuple-element.44.refs_2_.mine), custom_call_target="tpu_custom_call" | custom-call | tf_op jit(solution)/shard_map/pallas_call | solution.py:289
  42.9 0.1 shard_map.87.images.refs_0_
  43.0 0.1 collective-permute-start.18
  43.1 3.7 %shard_map.88 = (bf16[288,640]{1,0:T(8,128)(2,1)S(1)}, f32[48,640]{1,0:T(8,128)S(1)}, f32[48,640]{1,0:T(8,128)S(1)}) custom-call(s32[4]{0:T(128)S(1)} %pad_add_fusion.place, f32[1,128]{1,0:T(1,128)S(1)} %get-tuple-element.29.scale_ref.scale, f32[1,128]{1,0:T(1,128)S(1)} %get-tuple-element.31.bias_ref, bf16[288,1152]{1,0:T(8,128)(2,1)S(1)} %shard_map.87.images.refs_0_, ...), custom_call_target="tpu_custom_call" | custom-call | flops 6000000000 | tf_op jit(solution)/shard_map/pallas_call | solution.py:269
  46.8 0.5 collective-permute-start.19
  47.2 0.1 collective-permute-start.17
  47.3 1.2 %shard_map.89.refs_4_ = f32[1152,640]{1,0:T(8,128)S(1)} custom-call(bf16[336,1152]{1,0:T(8,128)(2,1)S(1)} %collective-permute-done.20.refs_0_, bf16[144,1152]{1,0:T(8,128)(2,1)S(1)} %collective-permute-done.15.refs_1_, bf16[480,640]{1,0:T(8,128)(2,1)S(1)} %collective-permute-done.21.refs_2_, f32[1152,640]{1,0:T(8,128)S(1)} %shard_map.86.refs_3_), custom_call_target="tpu_custom_call" | custom-call | tf_op jit(solution)/shard_map/pallas_call | solution.py:289
  48.5 0.2 collective-permute-done.17.received
  48.7 2.9 %shard_map.90 = (f32[1152,640]{1,0:T(8,128)}, bf16[48,640]{1,0:T(8,128)(2,1)}, bf16[48,1152]{1,0:T(8,128)(2,1)}) custom-call(f32[1,128]{1,0:T(1,128)S(1)} %get-tuple-element.29.scale_ref.scale, bf16[48,640]{1,0:T(8,128)(2,1)S(1)} %get-tuple-element.30.refs_0_.texts, f32[48,640]{1,0:T(8,128)S(1)} %get-tuple-element.48.own, ...), custom_call_target="tpu_custom_call" | custom-call | tf_op jit(solution)/shard_map/pallas_call | solution.py:302
  (18 shorter events, 0.1 us)
Async XLA Ops:
  0.6 11.3 %collective-permute-start.4 = (bf16[48,1152]{1,0:T(8,128)(2,1)}, bf16[48,1152]{1,0:T(8,128)(2,1)S(1)}, u32[]{:S(2)}, u32[]{:S(2)}) collective-permute-start(bf16[48,1152]{1,0:T(8,128)(2,1)} %images.1), channel_id=1, source_target_pairs={{0,16},{1,17},{2,18},{3,19},{4,20},{5,21},{6,22},{7,23},{8,9},{9,8... | collective-permute-start | bytes 331784 | tf_op jit(solution)/shard_map/ppermute | solution.py:197
  3.6 5.5 %collective-permute-start = (bf16[48,640]{1,0:T(8,128)(2,1)}, bf16[48,640]{1,0:T(8,128)(2,1)S(1)}, u32[]{:S(2)}, u32[]{:S(2)}) collective-permute-start(bf16[48,640]{1,0:T(8,128)(2,1)} %texts.1), channel_id=1, source_target_pairs={{0,2},{1,3},{2,0},{3,1},{4,6},{5,7},{6,4},{7,5},{8,10},{9,11},{10,... | collective-permute-start | bytes 184328 | tf_op jit(solution)/shard_map/ppermute | solution.py:187
  5.2 6.7 %collective-permute-start.9 = (bf16[48,640]{1,0:T(8,128)(2,1)}, bf16[48,640]{1,0:T(8,128)(2,1)S(1)}, u32[]{:S(2)}, u32[]{:S(2)}) collective-permute-start(bf16[48,640]{1,0:T(8,128)(2,1)} %texts.1), channel_id=1, source_target_pairs={{0,6},{1,7},{2,4},{3,5},{4,2},{5,3},{6,0},{7,1},{8,14},{9,15},{10,... | collective-permute-start | bytes 184328 | tf_op jit(solution)/shard_map/ppermute | solution.py:187
  7.7 6.1 %collective-permute-start.8 = (bf16[48,640]{1,0:T(8,128)(2,1)}, bf16[48,640]{1,0:T(8,128)(2,1)S(1)}, u32[]{:S(2)}, u32[]{:S(2)}) collective-permute-start(bf16[48,640]{1,0:T(8,128)(2,1)} %texts.1), channel_id=1, source_target_pairs={{0,4},{1,5},{2,6},{3,7},{4,0},{5,1},{6,2},{7,3},{8,12},{9,13},{10,... | collective-permute-start | bytes 184328 | tf_op jit(solution)/shard_map/ppermute | solution.py:187
  9.1 0.9 %copy-start.1 = (bf16[48,1152]{1,0:T(8,128)(2,1)S(1)}, bf16[48,1152]{1,0:T(8,128)(2,1)}, u32[]{:S(2)}) copy-start(bf16[48,1152]{1,0:T(8,128)(2,1)} %images.1) | copy-start | bytes 331780
  10.0 0.8 %copy-start.2 = (bf16[48,640]{1,0:T(8,128)(2,1)S(1)}, bf16[48,640]{1,0:T(8,128)(2,1)}, u32[]{:S(2)}) copy-start(bf16[48,640]{1,0:T(8,128)(2,1)} %texts.1) | copy-start | bytes 184324
  13.8 8.1 %collective-permute-start.10 = (bf16[192,640]{1,0:T(8,128)(2,1)S(1)}, bf16[192,640]{1,0:T(8,128)(2,1)S(1)}, u32[]{:S(2)}, u32[]{:S(2)}) collective-permute-start(bf16[192,640]{1,0:T(8,128)(2,1)S(1)} %shard_map.82.refs_0_), channel_id=1, source_target_pairs={{0,16},{1,17},{2,18},{3,19},{4,20},{5,21},{6,22},{7,23},{8,9},{9,8... | collective-permute-start | bytes 737288 | tf_op jit(solution)/shard_map/ppermute | solution.py:197
  15.1 6.0 %collective-permute-start.5 = (bf16[96,1152]{1,0:T(8,128)(2,1)S(1)}, bf16[96,1152]{1,0:T(8,128)(2,1)S(1)}, u32[]{:S(2)}, u32[]{:S(2)}) collective-permute-start(bf16[96,1152]{1,0:T(8,128)(2,1)S(1)} %shard_map.77.refs_0_), channel_id=1, source_target_pairs={{0,1},{1,0},{2,3},{3,2},{4,5},{5,4},{6,7},{7,6},{8,24},{9,25},{10,... | collective-permute-start | bytes 663560 | tf_op jit(solution)/shard_map/ppermute | solution.py:197
  16.0 8.8 %collective-permute-start.3 = (bf16[48,1152]{1,0:T(8,128)(2,1)}, bf16[48,1152]{1,0:T(8,128)(2,1)S(1)}, u32[]{:S(2)}, u32[]{:S(2)}) collective-permute-start(bf16[48,1152]{1,0:T(8,128)(2,1)} %images.1), channel_id=1, source_target_pairs={{0,6},{1,7},{2,4},{3,5},{4,2},{5,3},{6,0},{7,1},{8,14},{9,15},{10,... | collective-permute-start | bytes 331784 | tf_op jit(solution)/shard_map/ppermute | solution.py:187
  18.4 9.2 %collective-permute-start.2 = (bf16[48,1152]{1,0:T(8,128)(2,1)}, bf16[48,1152]{1,0:T(8,128)(2,1)S(1)}, u32[]{:S(2)}, u32[]{:S(2)}) collective-permute-start(bf16[48,1152]{1,0:T(8,128)(2,1)} %images.1), channel_id=1, source_target_pairs={{0,4},{1,5},{2,6},{3,7},{4,0},{5,1},{6,2},{7,3},{8,12},{9,13},{10,... | collective-permute-start | bytes 331784 | tf_op jit(solution)/shard_map/ppermute | solution.py:187
  18.4 9.2 %collective-permute-start.1 = (bf16[48,1152]{1,0:T(8,128)(2,1)}, bf16[48,1152]{1,0:T(8,128)(2,1)S(1)}, u32[]{:S(2)}, u32[]{:S(2)}) collective-permute-start(bf16[48,1152]{1,0:T(8,128)(2,1)} %images.1), channel_id=1, source_target_pairs={{0,2},{1,3},{2,0},{3,1},{4,6},{5,7},{6,4},{7,5},{8,10},{9,11},{10,... | collective-permute-start | bytes 331784 | tf_op jit(solution)/shard_map/ppermute | solution.py:187
  21.1 8.3 %collective-permute-start.11 = (bf16[192,640]{1,0:T(8,128)(2,1)S(1)}, bf16[192,640]{1,0:T(8,128)(2,1)S(1)}, u32[]{:S(2)}, u32[]{:S(2)}) collective-permute-start(bf16[192,640]{1,0:T(8,128)(2,1)S(1)} %shard_map.82.refs_0_), channel_id=1, source_target_pairs={{0,1},{1,0},{2,3},{3,2},{4,5},{5,4},{6,7},{7,6},{8,24},{9,25},{10,... | collective-permute-start | bytes 737288 | tf_op jit(solution)/shard_map/ppermute | solution.py:197
  22.0 8.2 %collective-permute-start.12 = (bf16[192,640]{1,0:T(8,128)(2,1)S(1)}, bf16[192,640]{1,0:T(8,128)(2,1)S(1)}, u32[]{:S(2)}, u32[]{:S(2)}) collective-permute-start(bf16[192,640]{1,0:T(8,128)(2,1)S(1)} %collective-permute-done.10.refs_1_), channel_id=1, source_target_pairs={{0,1},{1,0},{2,3},{3,2},{4,5},{5,4},{6,7},{7,6},{8,24},{9,25},{10,... | collective-permute-start | bytes 737288 | tf_op jit(solution)/shard_map/ppermute | solution.py:197
  23.1 1.4 %copy-start = (bf16[1152,640]{1,0:T(8,128)(2,1)S(1)}, bf16[1152,640]{1,0:T(8,128)(2,1)}, u32[]{:S(2)}) copy-start(bf16[1152,640]{1,0:T(8,128)(2,1)} %array.1) | copy-start | bytes 4423684
  27.6 7.2 %collective-permute-start.7 = (bf16[144,1152]{1,0:T(8,128)(2,1)S(1)}, bf16[144,1152]{1,0:T(8,128)(2,1)S(1)}, u32[]{:S(2)}, u32[]{:S(2)}) collective-permute-start(bf16[144,1152]{1,0:T(8,128)(2,1)S(1)} %shard_map.79.refs_2_), channel_id=1, source_target_pairs={{0,16},{1,17},{2,18},{3,19},{4,20},{5,21},{6,22},{7,23},{8,9},{9,8... | collective-permute-start | bytes 995336 | tf_op jit(solution)/shard_map/ppermute | solution.py:197
  31.0 5.6 %collective-permute-start.13 = (bf16[384,640]{1,0:T(8,128)(2,1)S(1)}, bf16[384,640]{1,0:T(8,128)(2,1)S(1)}, u32[]{:S(2)}, u32[]{:S(2)}) collective-permute-start(bf16[384,640]{1,0:T(8,128)(2,1)S(1)} %get-tuple-element.39), channel_id=1, source_target_pairs={{0,8},{8,0},{16,24},{24,16},{1,9},{9,1},{17,25},{25,17},{2,10},{10... | collective-permute-start | bytes 1474568 | tf_op jit(solution)/shard_map/ppermute | solution.py:187
  31.1 5.5 %collective-permute-start.14 = (bf16[384,640]{1,0:T(8,128)(2,1)S(1)}, bf16[384,640]{1,0:T(8,128)(2,1)S(1)}, u32[]{:S(2)}, u32[]{:S(2)}) collective-permute-start(bf16[384,640]{1,0:T(8,128)(2,1)S(1)} %get-tuple-element.40), channel_id=1, source_target_pairs={{0,8},{8,0},{16,24},{24,16},{1,9},{9,1},{17,25},{25,17},{2,10},{10... | collective-permute-start | bytes 1474568 | tf_op jit(solution)/shard_map/ppermute | solution.py:187
  31.6 11.3 %collective-permute-start.6 = (bf16[144,1152]{1,0:T(8,128)(2,1)S(1)}, bf16[144,1152]{1,0:T(8,128)(2,1)S(1)}, u32[]{:S(2)}, u32[]{:S(2)}) collective-permute-start(bf16[144,1152]{1,0:T(8,128)(2,1)S(1)} %shard_map.79.refs_2_), channel_id=1, source_target_pairs={{0,1},{1,0},{2,3},{3,2},{4,5},{5,4},{6,7},{7,6},{8,24},{9,25},{10,... | collective-permute-start | bytes 995336 | tf_op jit(solution)/shard_map/ppermute | solution.py:197
  34.7 8.1 %collective-permute-start.15 = (bf16[144,1152]{1,0:T(8,128)(2,1)S(1)}, bf16[144,1152]{1,0:T(8,128)(2,1)S(1)}, u32[]{:S(2)}, u32[]{:S(2)}) collective-permute-start(bf16[144,1152]{1,0:T(8,128)(2,1)S(1)} %collective-permute-done.7.images.refs_1_), channel_id=1, source_target_pairs={{0,8},{8,0},{16,24},{24,16},{1,9},{9,1},{17,25},{25,17},{2,10},{10... | collective-permute-start | bytes 995336 | tf_op jit(solution)/shard_map/ppermute | solution.py:187
  34.8 8.1 %collective-permute-start.16 = (bf16[144,1152]{1,0:T(8,128)(2,1)S(1)}, bf16[144,1152]{1,0:T(8,128)(2,1)S(1)}, u32[]{:S(2)}, u32[]{:S(2)}) collective-permute-start(bf16[144,1152]{1,0:T(8,128)(2,1)S(1)} %collective-permute-done.7.images.refs_1_), channel_id=1, source_target_pairs={{0,1},{1,0},{2,3},{3,2},{4,5},{5,4},{6,7},{7,6},{8,24},{9,25},{10,... | collective-permute-start | bytes 995336 | tf_op jit(solution)/shard_map/ppermute | solution.py:197
  41.1 6.2 %collective-permute-start.21 = (bf16[480,640]{1,0:T(8,128)(2,1)S(1)}, bf16[480,640]{1,0:T(8,128)(2,1)S(1)}, u32[]{:S(2)}, u32[]{:S(2)}) collective-permute-start(bf16[480,640]{1,0:T(8,128)(2,1)S(1)} %get-tuple-element.44.refs_2_.mine), channel_id=1, source_target_pairs={{0,8},{8,0},{16,24},{24,16},{1,9},{9,1},{17,25},{25,17},{2,10},{10... | collective-permute-start | bytes 1843208 | tf_op jit(solution)/shard_map/ppermute | solution.py:187
  41.2 6.1 %collective-permute-start.20 = (bf16[336,1152]{1,0:T(8,128)(2,1)S(1)}, bf16[336,1152]{1,0:T(8,128)(2,1)S(1)}, u32[]{:S(2)}, u32[]{:S(2)}) collective-permute-start(bf16[336,1152]{1,0:T(8,128)(2,1)S(1)} %shard_map.80.images.refs_0_), channel_id=1, source_target_pairs={{0,8},{8,0},{16,24},{24,16},{1,9},{9,1},{17,25},{25,17},{2,10},{10... | collective-permute-start | bytes 2322440 | tf_op jit(solution)/shard_map/ppermute | solution.py:187
  43.0 5.8 %collective-permute-start.18 = (bf16[288,1152]{1,0:T(8,128)(2,1)S(1)}, bf16[288,1152]{1,0:T(8,128)(2,1)S(1)}, u32[]{:S(2)}, u32[]{:S(2)}) collective-permute-start(bf16[288,1152]{1,0:T(8,128)(2,1)S(1)} %shard_map.87.images.refs_0_), channel_id=1, source_target_pairs={{0,8},{8,0},{16,24},{24,16},{1,9},{9,1},{17,25},{25,17},{2,10},{10... | collective-permute-start | bytes 1990664 | tf_op jit(solution)/shard_map/ppermute | solution.py:187
  46.8 2.0 %collective-permute-start.19 = (bf16[288,640]{1,0:T(8,128)(2,1)S(1)}, bf16[288,640]{1,0:T(8,128)(2,1)S(1)}, u32[]{:S(2)}, u32[]{:S(2)}) collective-permute-start(bf16[288,640]{1,0:T(8,128)(2,1)S(1)} %get-tuple-element.50.refs_2_), channel_id=1, source_target_pairs={{0,8},{8,0},{16,24},{24,16},{1,9},{9,1},{17,25},{25,17},{2,10},{10... | collective-permute-start | bytes 1105928 | tf_op jit(solution)/shard_map/ppermute | solution.py:187
  47.2 1.5 %collective-permute-start.17 = (f32[48,640]{1,0:T(8,128)S(1)}, f32[48,640]{1,0:T(8,128)S(1)}, u32[]{:S(2)}, u32[]{:S(2)}) collective-permute-start(f32[48,640]{1,0:T(8,128)S(1)} %get-tuple-element.49), channel_id=1, source_target_pairs={{0,8},{8,0},{16,24},{24,16},{1,9},{9,1},{17,25},{25,17},{2,10},{10... | collective-permute-start | bytes 368648 | tf_op jit(solution)/shard_map/ppermute | solution.py:187
